TPU v7x, 128 devices: a whole 4x4x4 slice. The times are simulated.
128 devices in a mesh: row: 16 (over y_lo, z, core), col: 8 (over x, y_hi).
Axes of the slice: x: 4, y: 4 (y_hi: 2, y_lo: 2; y = y_hi * 2 + y_lo), z: 4, core: 2. Of those that a mesh axis runs over, the one named last changes fastest.
Arguments:
- block_input: bfloat16 [1, 256, 256, 512], P(None, 'row', 'col'), may hold values from -6 to 6
- w_expand: bfloat16 [512, 2048], replicated, may hold values from -0.25 to 0.25
- w_depthwise: bfloat16 [9, 2048], replicated, may hold values from -2 to 2
- w_project: bfloat16 [2048, 512], replicated, may hold values from -0.125 to 0.125
- w_qkv: bfloat16 [512, 1536], replicated, may hold values from -0.25 to 0.25
- w_out: bfloat16 [512, 512], replicated, may hold values from -0.25 to 0.25
- grad_out: bfloat16 [1, 256, 256, 512], P(None, 'row', 'col'), may hold values from -6 to 6
Outputs:
- block_output: bfloat16 [1, 256, 256, 512], P(None, 'row', 'col')
- grad_input: bfloat16 [1, 256, 256, 512], P(None, 'row', 'col')
- grad_expand: float32 [512, 2048], P(None, ('row', 'col'))
- grad_depthwise: float32 [9, 2048], P(None, ('row', 'col'))
- grad_project: float32 [512, 2048], P(None, ('row', 'col'))
- grad_qkv: float32 [512, 1536], P(None, ('row', 'col'))
- grad_outproj: float32 [512, 512], P(None, ('row', 'col'))
All inputs are finite; a program needn't handle non-finite values.
Results may differ from a plain program's by a relative error of at most 0.015.
Values may be sent and summed in bfloat16 or wider, within the bound.
No kernel may reach another device: no remote copies, remote signals or barrier semaphores. Data moves between devices by JAX's collectives and lax.ppermute only.
A program may use at most 128 MiB of HBM per device.

v0:
```python
import jax
import jax.numpy as jnp
from jax import lax
from jax.sharding import PartitionSpec as P

HEADS = 16
HDIM = 32
GRID = 8


EPS = 1e-05


def with_halo(x, sides, width):
    for axis, dim in sides:
        devices, length = (lax.axis_size(axis), x.shape[dim])
        up = [(i, (i + 1) % devices) for i in range(devices - 1)]
        down = [(j, i) for i, j in up]
        last = lax.slice_in_dim(x, length - width, length, axis=dim)
        initial = lax.slice_in_dim(x, 0, width, axis=dim)
        before = lax.ppermute(last, axis, up)
        after = lax.ppermute(initial, axis, down)
        x = jnp.concatenate([before, x, after], axis=dim)
    return x


def layer_normalize(value_tensor):
    center = value_tensor - jnp.mean(value_tensor, -1, keepdims=True)
    expand_ratio = lax.rsqrt(jnp.mean(center * center, -1, keepdims=True) + EPS)
    return (center * expand_ratio, expand_ratio)


def norm_back(value_tensor, gradient_tree):
    centered_scaled, expand_ratio = layer_normalize(value_tensor)
    return (
        gradient_tree
        - jnp.mean(gradient_tree, -1, keepdims=True)
        - centered_scaled * jnp.mean(gradient_tree * centered_scaled, -1, keepdims=True)
    ) * expand_ratio


def slope(value_tensor):
    return jax.vjp(jax.nn.gelu, value_tensor)[1](jnp.ones_like(value_tensor))[0]


def attend(qkv, grad_att):
    count = qkv.shape[0]
    members = qkv.shape[1]
    width = grad_att.shape[-1]
    scale = HDIM ** (-0.5)
    query = qkv[..., :width].reshape(count, members, HEADS, HDIM)
    keys = qkv[..., width : 2 * width].reshape(count, members, HEADS, HDIM)
    value_tensor = qkv[..., 2 * width :].reshape(count, members, HEADS, HDIM)
    grad_o = grad_att.reshape(count, members, HEADS, HDIM)
    scores = jnp.einsum("gqhd,gkhd->ghqk", query, keys, preferred_element_type=jnp.float32) * scale
    probs = jax.nn.softmax(scores, axis=-1)
    probs_b = probs.astype(jnp.bfloat16)
    attended = jnp.einsum(
        "ghqk,gkhd->gqhd", probs_b, value_tensor, preferred_element_type=jnp.float32
    ).astype(jnp.bfloat16)
    grad_probs = jnp.einsum(
        "gqhd,gkhd->ghqk", grad_o, value_tensor, preferred_element_type=jnp.float32
    )
    grad_scores = (
        probs * (grad_probs - jnp.sum(probs * grad_probs, -1, keepdims=True)) * scale
    ).astype(jnp.bfloat16)
    grad_query = jnp.einsum(
        "ghqk,gkhd->gqhd", grad_scores, keys, preferred_element_type=jnp.float32
    )
    grad_key = jnp.einsum("ghqk,gqhd->gkhd", grad_scores, query, preferred_element_type=jnp.float32)
    grad_value = jnp.einsum("ghqk,gqhd->gkhd", probs_b, grad_o, preferred_element_type=jnp.float32)
    joined = jnp.concatenate(
        [
            grad_query.reshape(count, members, width),
            grad_key.reshape(count, members, width),
            grad_value.reshape(count, members, width),
        ],
        -1,
    )
    return (attended.reshape(count, members, width), joined.astype(jnp.bfloat16))


def layout_plan(rows_here, cols_here):
    row_count = lax.axis_size("row")
    col_count = lax.axis_size("col")
    cell_rows = rows_here * row_count // GRID
    grid_cell_columns = cols_here * col_count // GRID
    key_rows = min(rows_here, cell_rows)
    key_cols = min(cols_here, grid_cell_columns)
    return (
        row_count,
        col_count,
        key_rows,
        key_cols,
        rows_here // key_rows,
        cols_here // key_cols,
        cell_rows // key_rows,
        grid_cell_columns // key_cols,
    )


def to_keys(value_tensor, plan):
    row_count, col_count, key_rows, key_cols, rep_rows, repeated_columns, class_rows, class_cols = (
        plan
    )
    chans = value_tensor.shape[-1]
    keyed = value_tensor.reshape(rep_rows, key_rows, repeated_columns, key_cols, chans).transpose(
        1, 3, 0, 2, 4
    )
    per_owner = key_rows * key_cols // (row_count * col_count)
    return keyed.reshape(row_count, col_count, per_owner, rep_rows * repeated_columns, chans)


def from_keys(value_tensor, plan):
    row_count, col_count, key_rows, key_cols, rep_rows, repeated_columns, class_rows, class_cols = (
        plan
    )
    chans = value_tensor.shape[-1]
    shaped = value_tensor.reshape(key_rows, key_cols, rep_rows, repeated_columns, chans).transpose(
        2, 0, 3, 1, 4
    )
    return shaped.reshape(rep_rows * key_rows, repeated_columns * key_cols, chans)


def into_groups(value_tensor, plan):
    row_count, col_count, key_rows, key_cols, rep_rows, repeated_columns, class_rows, class_cols = (
        plan
    )
    per_owner = value_tensor.shape[2]
    chans = value_tensor.shape[-1]
    shaped = value_tensor.reshape(
        row_count // class_rows,
        class_rows,
        col_count // class_cols,
        class_cols,
        per_owner,
        rep_rows,
        repeated_columns,
        chans,
    )
    shaped = shaped.transpose(1, 3, 4, 0, 5, 2, 6, 7)
    return shaped.reshape(class_rows * class_cols * per_owner, -1, chans)


def out_of_groups(value_tensor, plan):
    row_count, col_count, key_rows, key_cols, rep_rows, repeated_columns, class_rows, class_cols = (
        plan
    )
    chans = value_tensor.shape[-1]
    per_owner = value_tensor.shape[0] // (class_rows * class_cols)
    shaped = value_tensor.reshape(
        class_rows,
        class_cols,
        per_owner,
        row_count // class_rows,
        rep_rows,
        col_count // class_cols,
        repeated_columns,
        chans,
    )
    shaped = shaped.transpose(3, 0, 5, 1, 2, 4, 6, 7)
    return shaped.reshape(row_count, col_count, per_owner, rep_rows * repeated_columns, chans)


def outbound(first, second):
    flat_first = first.reshape((-1,) + first.shape[2:])
    flat_second = second.reshape((-1,) + second.shape[2:])
    moved_first, moved_second = (
        lax.all_to_all(flat_first, ("row", "col"), split_axis=0, concat_axis=0, tiled=True),
        lax.all_to_all(flat_second, ("row", "col"), split_axis=0, concat_axis=0, tiled=True),
    )
    moved_first = moved_first.reshape(first.shape)
    moved_second = moved_second.reshape(second.shape)
    return (moved_first, moved_second)


def inbound(first, second):
    flat_first = first.reshape((-1,) + first.shape[2:])
    flat_second = second.reshape((-1,) + second.shape[2:])
    moved_first, moved_second = (
        lax.all_to_all(flat_first, ("row", "col"), split_axis=0, concat_axis=0, tiled=True),
        lax.all_to_all(flat_second, ("row", "col"), split_axis=0, concat_axis=0, tiled=True),
    )
    moved_first = moved_first.reshape(first.shape)
    moved_second = moved_second.reshape(second.shape)
    return (moved_first, moved_second)


def one_image(block_input, w_expand, w_depthwise, w_project, w_qkv, w_out, grad_out):
    rows_here, cols_here, width = block_input.shape
    tokens = rows_here * cols_here
    plan = layout_plan(rows_here, cols_here)
    inputs = block_input.astype(jnp.float32)
    normed_in = layer_normalize(inputs)[0].astype(jnp.bfloat16)
    normed_in_flat = normed_in.reshape(tokens, width)
    widened_hidden = jnp.dot(normed_in_flat, w_expand, preferred_element_type=jnp.float32).reshape(
        rows_here, cols_here, -1
    )
    activated = jax.nn.gelu(widened_hidden).astype(jnp.bfloat16)
    padded = with_halo(activated, (("row", 0), ("col", 1)), 1)
    kernel = w_depthwise.astype(jnp.float32)
    conv = jnp.zeros(widened_hidden.shape, jnp.float32)
    for tap in range(9):
        shift_r, shift_c = divmod(tap, 3)
        conv = (
            conv
            + padded[shift_r : shift_r + rows_here, shift_c : shift_c + cols_here].astype(
                jnp.float32
            )
            * kernel[tap]
        )
    mid = jax.nn.gelu(conv).astype(jnp.bfloat16)
    mid_flat = mid.reshape(tokens, -1)
    resid = (
        inputs
        + jnp.dot(mid_flat, w_project, preferred_element_type=jnp.float32).reshape(
            rows_here, cols_here, width
        )
    ).astype(jnp.bfloat16)
    resid_f = resid.astype(jnp.float32)
    normed_mid = layer_normalize(resid_f)[0].astype(jnp.bfloat16)
    normed_mid_flat = normed_mid.reshape(tokens, width)
    leaving = (
        jnp.dot(normed_mid_flat, w_qkv, preferred_element_type=jnp.float32)
        .astype(jnp.bfloat16)
        .reshape(rows_here, cols_here, -1)
    )
    arrived_main, arrived_grad = outbound(to_keys(leaving, plan), to_keys(grad_out, plan))
    group_main = into_groups(arrived_main, plan)
    group_grad = into_groups(arrived_grad, plan)
    count, members = (group_grad.shape[0], group_grad.shape[1])
    group_grad_flat = group_grad.reshape(count * members, width)
    group_grad_att = (
        jnp.dot(group_grad_flat, w_out.T, preferred_element_type=jnp.float32)
        .astype(jnp.bfloat16)
        .reshape(count, members, width)
    )
    attended, grad_qkvact = attend(group_main, group_grad_att)
    attended_flat = attended.reshape(count * members, width)
    added = (
        jnp.dot(attended_flat, w_out, preferred_element_type=jnp.float32)
        .astype(jnp.bfloat16)
        .reshape(count, members, width)
    )
    grad_outproj = jnp.dot(attended_flat.T, group_grad_flat, preferred_element_type=jnp.float32)
    home_added, home_main = inbound(out_of_groups(added, plan), out_of_groups(grad_qkvact, plan))
    added_here = from_keys(home_added, plan)
    main_here = from_keys(home_main, plan)
    grad_qkvact_here = main_here.reshape(tokens, -1)
    grad_qkv = jnp.dot(normed_mid_flat.T, grad_qkvact_here, preferred_element_type=jnp.float32)
    grad_normed = (
        jnp.dot(grad_qkvact_here, w_qkv.T, preferred_element_type=jnp.float32)
        .astype(jnp.bfloat16)
        .reshape(rows_here, cols_here, width)
    )
    block_output = (resid_f + added_here.astype(jnp.float32)).astype(jnp.bfloat16)
    grad_resid = (
        grad_out.astype(jnp.float32) + norm_back(resid_f, grad_normed.astype(jnp.float32))
    ).astype(jnp.bfloat16)
    grad_resid_flat = grad_resid.reshape(tokens, width)
    grad_project = jnp.dot(grad_resid_flat.T, mid_flat, preferred_element_type=jnp.float32)
    grad_mid_f = jnp.dot(grad_resid_flat, w_project.T, preferred_element_type=jnp.float32).reshape(
        rows_here, cols_here, -1
    )
    grad_mid = (grad_mid_f * slope(conv)).astype(jnp.bfloat16)
    grad_pad = with_halo(grad_mid, (("row", 0), ("col", 1)), 1)
    grad_act = jnp.zeros(widened_hidden.shape, jnp.float32)
    tap_grads = []
    grad_mid_32 = grad_mid.astype(jnp.float32)
    for tap in range(9):
        shift_r, shift_c = divmod(tap, 3)
        grad_act = (
            grad_act
            + grad_pad[
                2 - shift_r : 2 - shift_r + rows_here, 2 - shift_c : 2 - shift_c + cols_here
            ].astype(jnp.float32)
            * kernel[tap]
        )
        tap_grads.append(
            jnp.sum(
                padded[shift_r : shift_r + rows_here, shift_c : shift_c + cols_here].astype(
                    jnp.float32
                )
                * grad_mid_32,
                axis=(0, 1),
            )
        )
    grad_depthwise = jnp.stack(tap_grads)
    grad_pre = (grad_act * slope(widened_hidden)).astype(jnp.bfloat16).reshape(tokens, -1)
    grad_expand = jnp.dot(normed_in_flat.T, grad_pre, preferred_element_type=jnp.float32)
    grad_norm_in = jnp.dot(grad_pre, w_expand.T, preferred_element_type=jnp.float32).reshape(
        rows_here, cols_here, width
    )
    grad_input = (grad_resid.astype(jnp.float32) + norm_back(inputs, grad_norm_in)).astype(
        jnp.bfloat16
    )
    return (
        block_output,
        grad_input,
        (grad_expand, grad_depthwise, grad_project, grad_qkv, grad_outproj),
    )


def body(block_input, w_expand, w_depthwise, w_project, w_qkv, w_out, grad_out):
    totals = None
    result = one_image(block_input[0], w_expand, w_depthwise, w_project, w_qkv, w_out, grad_out[0])
    outputs = [result[0]]
    inputs_grads = [result[1]]
    totals = result[2]
    summed = (
        lax.psum_scatter(totals[0], ("row", "col"), scatter_dimension=1, tiled=True),
        lax.psum_scatter(totals[1], ("row", "col"), scatter_dimension=1, tiled=True),
        lax.psum_scatter(totals[2], ("row", "col"), scatter_dimension=1, tiled=True),
        lax.psum_scatter(totals[3], ("row", "col"), scatter_dimension=1, tiled=True),
        lax.psum_scatter(totals[4], ("row", "col"), scatter_dimension=1, tiled=True),
    )
    return (
        jnp.stack(outputs),
        jnp.stack(inputs_grads),
        summed[0],
        summed[1],
        summed[2],
        summed[3],
        summed[4],
    )


def solution(mesh):
    return jax.shard_map(
        body,
        mesh=mesh,
        in_specs=(
            P(None, "row", "col", None),
            P(),
            P(),
            P(),
            P(),
            P(),
            P(None, "row", "col", None),
        ),
        out_specs=(
            P(None, "row", "col", None),
            P(None, "row", "col", None),
            P(None, ("row", "col")),
            P(None, ("row", "col")),
            P(None, ("row", "col")),
            P(None, ("row", "col")),
            P(None, ("row", "col")),
        ),
        check_vma=False,
    )
```

profile of v0, /device:TPU:0, one launch (start us, length us, event | category | flops | bytes accessed | tf_op | source)
XLA Modules:
  0.0 2285.4 jit_solution(3315459402878082237)
XLA Ops:
  9.9 5.0 multiply_convert_fusion.2
  19.8 14.6 all-to-all-start.2
  44.0 5.4 collective-permute-done.3
  52.3 5.6 fusion.10
  67.3 10.5 all-to-all-start
  86.6 14.9 all-to-all-done
  115.9 5.9 fusion.129
  128.4 8.7 fusion.71
  145.4 5.9 all-to-all-start.1
  166.4 8.6 fusion.74
  186.6 10.3 all-to-all-start.3
  202.4 18.4 all-to-all-done.3
  233.3 14.2 fusion.40
  249.1 6.1 convolution_bitcast_fusion
  263.9 6.5 collective-permute-start.7
  278.1 7.7 fusion.18
  294.6 348.7 %fusion = f32[512,16]{0,1:T(8,128)S(1)} fusion(f32[512,1536]{0,1:T(8,128)} %fusion.131), kind=kCustom, calls=%all-reduce-scatter | all-reduce-scatter fusion | flops 1048577 | bytes 3178496
  655.5 15.9 collective-permute-start.30
  671.4 5.2 collective-permute-start.29
  685.1 5.1 collective-permute-start.24
  740.0 45.5 %concatenate.71 = f32[512,524]{0,1:T(8,128)} concatenate(f32[512,12]{0,1:T(8,128)S(1)} %collective-permute-done.39, f32[512,16]{0,1:T(8,128)S(1)} %collective-permute-done.38, f32[512,16]{0,1:T(8,128)S(1)} %collective-permute-done.37, f32[512,16]{0,1:T(8,128)S(1)} %collective-permute-done.36, f32[512,16]{0,1:T(8,128)S(1)} %collective-permute-done.35, ...), dimensions={1} | concatenate | bytes 2146304
  787.0 208.7 %reduce-scatter.12.cloned.1.call-done = f32[16,9]{1,0:T(8,128)} async-done(((f32[2048,9]{1,0:T(8,128)}), f32[16,9]{1,0:T(8,128)}) %reduce-scatter.12.cloned.1.call-update) | async-done | bytes 592
  1001.4 635.7 %reduce-scatter.10.cloned.1.call-done = f32[512,16]{0,1:T(8,128)} async-done(((f32[512,2048]{0,1:T(8,128)}), f32[512,16]{0,1:T(8,128)}) %reduce-scatter.10.cloned.1.call-update) | async-done | bytes 32784 | tf_op jit(solution)/shard_map/reduce_scatter | solution.py:313
  1637.0 641.7 %reduce-scatter.8.cloned.1.call-done = f32[512,16]{0,1:T(8,128)} async-done(((f32[512,2048]{0,1:T(8,128)}), f32[512,16]{0,1:T(8,128)}) %reduce-scatter.8.cloned.1.call-update) | async-done | bytes 32784 | tf_op jit(solution)/shard_map/reduce_scatter | solution.py:311
  (200 shorter events, 215.6 us)
Async XLA Ops:
  16.3 18.2 collective-permute-start
  17.6 16.9 collective-permute-start.1
  19.8 47.5 %all-to-all-start.2 = ((bf16[128,4,1,512]{3,1,2,0:T(4,128)(2,1)}), bf16[128,4,1,512]{3,1,2,0:T(4,128)(2,1)}, u32[]{:S(2)}, u32[]{:S(2)}) async-start(bf16[128,4,1,512]{3,1,2,0:T(4,128)(2,1)} %bitcast.26), calls=%async_computation.2 | async-start | bytes 1048576 | tf_op jit(solution)/shard_map/all_to_all | solution.py:170
  67.3 34.2 %all-to-all-start = ((bf16[128,4,1,1536]{3,1,2,0:T(4,128)(2,1)}), bf16[128,4,1,1536]{3,1,2,0:T(4,128)(2,1)}, u32[]{:S(2)}, u32[]{:S(2)}) async-start(bf16[128,4,1,1536]{3,1,2,0:T(4,128)(2,1)} %bitcast.162), calls=%async_computation | async-start | bytes 3145728 | tf_op jit(solution)/shard_map/all_to_all | solution.py:169
  145.4 41.3 %all-to-all-start.1 = ((bf16[128,4,1,512]{3,1,2,0:T(4,128)(2,1)}), bf16[128,4,1,512]{3,1,2,0:T(4,128)(2,1)}, u32[]{:S(2)}, u32[]{:S(2)}) async-start(bf16[128,4,1,512]{3,1,2,0:T(4,128)(2,1)} %bitcast.174), calls=%async_computation.1 | async-start | bytes 1048576 | tf_op jit(solution)/shard_map/all_to_all | solution.py:181
  186.6 34.2 %all-to-all-start.3 = ((bf16[128,4,1,1536]{3,1,2,0:T(4,128)(2,1)}), bf16[128,4,1,1536]{3,1,2,0:T(4,128)(2,1)}, u32[]{:S(2)}, u32[]{:S(2)}) async-start(bf16[128,4,1,1536]{3,1,2,0:T(4,128)(2,1)} %copy.102), calls=%async_computation.3 | async-start | bytes 3145728 | tf_op jit(solution)/shard_map/all_to_all | solution.py:182
  197.0 541.7 %all-reduce.5.cloned.1.call-start = ((), (), s32[]{:S(2)}) async-start(), calls=%async_computation.10 | async-start | bytes 2097152
  199.8 796.0 %reduce-scatter.12.cloned.1.call-start = ((), (), s32[]{:S(2)}) async-start(), calls=%async_computation.9 | async-start | bytes 1056768
  249.1 1388.0 %reduce-scatter.10.cloned.1.call-start = ((), (), s32[]{:S(2)}) async-start(), calls=%async_computation.8 | async-start | bytes 4227072 | tf_op jit(solution)/shard_map/reduce_scatter | solution.py:313
  255.2 2023.5 %reduce-scatter.8.cloned.1.call-start = ((), (), s32[]{:S(2)}) async-start(), calls=%async_computation.7 | async-start | bytes 4227072 | tf_op jit(solution)/shard_map/reduce_scatter | solution.py:311
  650.3 21.1 collective-permute-start.34
  651.6 25.0 %collective-permute-start.33 = (f32[512,16]{0,1:T(8,128)S(1)}, f32[512,16]{0,1:T(8,128)S(1)}, u32[]{:S(2)}, u32[]{:S(2)}) collective-permute-start(f32[512,16]{0,1:T(8,128)S(1)} %fusion), channel_id=1, source_target_pairs={{0,26},{1,27},{2,28},{3,29},{4,30},{5,31},{6,32},{7,33},{8,34},{9,... | collective-permute-start | bytes 98312
  652.9 26.5 %collective-permute-start.32 = (f32[512,16]{0,1:T(8,128)S(1)}, f32[512,16]{0,1:T(8,128)S(1)}, u32[]{:S(2)}, u32[]{:S(2)}) collective-permute-start(f32[512,16]{0,1:T(8,128)S(1)} %fusion), channel_id=1, source_target_pairs={{0,25},{1,26},{2,27},{3,28},{4,29},{5,30},{6,31},{7,32},{8,33},{9,... | collective-permute-start | bytes 98312
  654.2 26.9 %collective-permute-start.31 = (f32[512,16]{0,1:T(8,128)S(1)}, f32[512,16]{0,1:T(8,128)S(1)}, u32[]{:S(2)}, u32[]{:S(2)}) collective-permute-start(f32[512,16]{0,1:T(8,128)S(1)} %fusion), channel_id=1, source_target_pairs={{0,24},{1,25},{2,26},{3,27},{4,28},{5,29},{6,30},{7,31},{8,32},{9,... | collective-permute-start | bytes 98312
  655.5 28.2 %collective-permute-start.30 = (f32[512,16]{0,1:T(8,128)S(1)}, f32[512,16]{0,1:T(8,128)S(1)}, u32[]{:S(2)}, u32[]{:S(2)}) collective-permute-start(f32[512,16]{0,1:T(8,128)S(1)} %fusion), channel_id=1, source_target_pairs={{0,23},{1,24},{2,25},{3,26},{4,27},{5,28},{6,29},{7,30},{8,31},{9,... | collective-permute-start | bytes 98312
  681.2 14.6 collective-permute-start.26
  685.1 15.3 collective-permute-start.24
  706.0 14.4 collective-permute-start.17
  707.9 16.8 collective-permute-start.16
  711.4 17.7 collective-permute-start.15
  713.1 18.1 collective-permute-start.14
  717.8 17.2 collective-permute-start.13
  720.5 19.5 collective-permute-start.12
  724.7 15.3 collective-permute-start.11
  (48 other events, 612.0 us)
Sparse Core Ops, SparseCore 0:
  202.6 151.2 all-reduce.4
  356.4 639.3 reduce-scatter.11
  998.7 638.2 reduce-scatter.9
  1639.9 638.7 reduce-scatter.7
where the time goes:
time: 2300 us; the launch traced here: 2290 us
  waiting for transfers between devices  1530 us (67%)
  blocking collectives  349 us (15%)
  starting transfers between devices  155 us (7%)
  local copies, waits for them, and re-layouts  116 us (5%)
  matrix products  84.1 us (4%)
  other arithmetic  32.5 us (1%)
    reduce_scatter x1, waiting for transfers between devices, body(): lax.psum_scatter(totals[0], ('row', 'col'), scatter_dimension=1, tiled=True)  642 us
    reduce_scatter x1, waiting for transfers between devices, body(): lax.psum_scatter(totals[2], ('row', 'col'), scatter_dimension=1, tiled=True)  636 us
    unnamed x1, blocking collectives  349 us
    unnamed x38, waiting for transfers between devices  209 us
    unnamed x34, starting transfers between devices  95.3 us
    unnamed x54, local copies, waits for them, and re-layouts  55.8 us
  transfers between devices with their start and end apart: 48, of which 10 were waited for; matrix products, arithmetic and copies ran while one was open for 23% of the time, Pallas kernels for 0%

commit v1 on v0

v1 whole, which is shorter than its diff:
```python
import functools
import itertools

import jax
import jax.numpy as jnp
from jax import lax
from jax.experimental import pallas as pl
from jax.experimental.pallas import tpu as pltpu
from jax.sharding import PartitionSpec as P

HEADS = 16
HDIM = 32
EPS = 1e-05
BF = jnp.bfloat16
F32 = jnp.float32
AX = ("row", "col")
WIDE = 40
CHUNK = 256

SIZES = dict(y_lo=2, z=4, core=2, x=4, y_hi=2)
STRIDES = dict(y_lo=64, z=16, core=8, x=2, y_hi=1)
CHIPS = ("y_lo", "z", "x", "y_hi")


def device_groups(axes):
    rest = [a for a in SIZES if a not in axes]
    found = []
    for at in itertools.product(*[range(SIZES[a]) for a in rest]):
        base = sum(v * STRIDES[a] for v, a in zip(at, rest))
        found.append(
            [
                base + sum(v * STRIDES[a] for v, a in zip(m, axes))
                for m in itertools.product(*[range(SIZES[a]) for a in axes])
            ]
        )
    return found


def other_core():
    return [(d, d ^ STRIDES["core"]) for d in range(128)]


def across_chips(x):
    return lax.all_to_all(x, AX, 0, 0, tiled=True, axis_index_groups=device_groups(CHIPS))


def shift(x, axis, step):
    n = lax.axis_size(axis)
    pairs = [(i, i + step) for i in range(n) if 0 <= i + step < n]
    return lax.ppermute(x, axis, pairs)


def halo(x, width):
    rows, cols, chans = x.shape
    above = shift(x[rows - width :], "row", 1)
    below = shift(x[:width], "row", -1)
    to_right = jnp.concatenate(
        [above[:, cols - width :], x[:, cols - width :], below[:, cols - width :]], 0
    )
    to_left = jnp.concatenate([above[:, :width], x[:, :width], below[:, :width]], 0)
    left = shift(to_right, "col", 1)
    right = shift(to_left, "col", -1)
    flat = lambda v: v.reshape(-1, chans)
    return flat(above), flat(below), flat(left), flat(right)


def place_halo(wide, centre, above, below, left, right, width, rows, cols):
    wide[...] = jnp.zeros(wide.shape, wide.dtype)
    wide[width : width + rows, 0:cols, :] = centre.reshape(rows, cols, -1)
    wide[0:width, 0:cols, :] = above.reshape(width, cols, -1)
    wide[width + rows :, 0:cols, :] = below.reshape(width, cols, -1)
    for r in range(rows + 2 * width):
        wide[r, WIDE - width :, :] = left[r * width : (r + 1) * width]
        wide[r, cols : cols + width, :] = right[r * width : (r + 1) * width]


def normalize(x):
    center = x - jnp.mean(x, -1, keepdims=True)
    ratio = lax.rsqrt(jnp.mean(center * center, -1, keepdims=True) + EPS)
    return center * ratio, ratio


def normalize_back(x, grad):
    scaled, ratio = normalize(x)
    return (
        grad
        - jnp.mean(grad, -1, keepdims=True)
        - scaled * jnp.mean(grad * scaled, -1, keepdims=True)
    ) * ratio


A0 = 0.7978845608028654
A1 = A0 * 0.044715


def gelu_parts(x):
    sq = x * x
    t = jnp.tanh(x * (A0 + A1 * sq))
    half = 0.5 + 0.5 * t
    slope = half + (0.5 * x) * ((1.0 - t * t) * (A0 + (3.0 * A1) * sq))
    return x * half, slope


def dot(a, b):
    return jnp.dot(a, b, preferred_element_type=F32)


def dot_nt(a, b):
    return lax.dot_general(a, b, (((1,), (1,)), ((), ())), preferred_element_type=F32)


def dot_tn(a, b):
    return lax.dot_general(a, b, (((0,), (0,)), ((), ())), preferred_element_type=F32)


def roll(x, by):
    return pltpu.roll(x, by % x.shape[0], 0)


def forward_kernel(
    x_ref, above_ref, below_ref, left_ref, right_ref, go_ref, we_ref, wd_ref, wp_ref,
    act_out, slope_c_out, slope_e_out, mid_out, resid_out, send_out,
    wide, normed, pre, act, slope_c, acc,
):
    step = pl.program_id(0)
    rows, cols = 16, 32

    @pl.when(step == 0)
    def _():
        place_halo(
            wide,
            x_ref[...].astype(F32), above_ref[...].astype(F32), below_ref[...].astype(F32),
            left_ref[...].astype(F32), right_ref[...].astype(F32), 2, rows, cols,
        )
        normed[...] = normalize(wide[...].reshape(-1, wide.shape[-1]))[0].astype(BF)
        acc[...] = jnp.zeros(acc.shape, F32)

    pre[...] = dot(normed[...], we_ref[...]).reshape(pre.shape)

    def expand_row(r, _):
        g, s = gelu_parts(pre[r])
        act[r] = g.astype(BF).astype(F32)
        pre[r] = s
        return 0

    lax.fori_loop(0, rows + 4, expand_row, 0)
    slope_e_out[...] = pre[2 : 2 + rows, 0:cols, :].astype(BF)
    act_out[...] = act[1 : rows + 3].reshape(act_out.shape).astype(BF)
    taps = [wd_ref[k : k + 1, :].astype(F32) for k in range(9)]

    def conv_row(r, _):
        lines = [act[r], act[r + 1], act[r + 2]]
        sums = [sum(lines[i] * taps[3 * i + j] for i in range(3)) for j in range(3)]
        conv = sums[1] + roll(sums[0], 1) + roll(sums[2], -1)
        g, s = gelu_parts(conv)
        slope_c[r] = s
        pre[r] = g
        return 0

    lax.fori_loop(0, rows + 2, conv_row, 0)
    slope_c_out[...] = slope_c[...].reshape(slope_c_out.shape).astype(BF)
    mid = pre[1 : 1 + rows, 0:cols, :].reshape(rows * cols, -1).astype(BF)
    mid_out[...] = mid
    acc[...] += dot(mid, wp_ref[...])

    @pl.when(step == pl.num_programs(0) - 1)
    def _():
        resid = (x_ref[...].astype(F32) + acc[...]).astype(BF)
        resid_out[...] = resid
        width = resid.shape[1]
        send_out[:, 0:width] = normalize(resid.astype(F32))[0].astype(BF)
        send_out[:, width:] = go_ref[...]


def forward_block(x, strips, go, w_expand, w_depthwise, w_project):
    tokens, width = x.shape
    hid = w_expand.shape[1]
    rows, cols = 16, 32
    whole = lambda a: pl.BlockSpec(a.shape, lambda j: (0,) * a.ndim)
    return pl.pallas_call(
        forward_kernel,
        name="mbconv_forward",
        grid=(hid // CHUNK,),
        in_specs=[
            whole(x), *[whole(s) for s in strips], whole(go),
            pl.BlockSpec((width, CHUNK), lambda j: (0, j)),
            pl.BlockSpec((9, CHUNK), lambda j: (0, j)),
            pl.BlockSpec((CHUNK, width), lambda j: (j, 0)),
        ],
        out_specs=[
            pl.BlockSpec(((rows + 2) * WIDE, CHUNK), lambda j: (0, j)),
            pl.BlockSpec(((rows + 2) * WIDE, CHUNK), lambda j: (0, j)),
            pl.BlockSpec((rows, cols, CHUNK), lambda j: (0, 0, j)),
            pl.BlockSpec((tokens, CHUNK), lambda j: (0, j)),
            pl.BlockSpec((tokens, width), lambda j: (0, 0)),
            pl.BlockSpec((tokens, 2 * width), lambda j: (0, 0)),
        ],
        out_shape=[
            jax.ShapeDtypeStruct(((rows + 2) * WIDE, hid), BF),
            jax.ShapeDtypeStruct(((rows + 2) * WIDE, hid), BF),
            jax.ShapeDtypeStruct((rows, cols, hid), BF),
            jax.ShapeDtypeStruct((tokens, hid), BF),
            jax.ShapeDtypeStruct((tokens, width), BF),
            jax.ShapeDtypeStruct((tokens, 2 * width), BF),
        ],
        scratch_shapes=[
            pltpu.VMEM((rows + 4, WIDE, width), F32),
            pltpu.VMEM(((rows + 4) * WIDE, width), BF),
            pltpu.VMEM((rows + 4, WIDE, CHUNK), F32),
            pltpu.VMEM((rows + 4, WIDE, CHUNK), F32),
            pltpu.VMEM((rows + 2, WIDE, CHUNK), F32),
            pltpu.VMEM((tokens, width), F32),
        ],
        compiler_params=pltpu.CompilerParams(vmem_limit_bytes=48 * 2**20),
        cost_estimate=pl.CostEstimate(
            flops=2 * (800 + 512) * 512 * 2048, bytes_accessed=20 * 2**20, transcendentals=3 * 2**20
        ),
    )(x, *strips, go, w_expand, w_depthwise, w_project)


def attention_kernel(in_ref, wq_ref, wo_ref, send_out, gq_out, att_out, qkv, gatt, att, gq):
    width = wo_ref.shape[0]
    groups = 8
    members = in_ref.shape[0] // groups
    scale = HDIM ** (-0.5)
    quads = width // 128

    def put(ref, at, value):
        value = value.astype(BF).astype(F32)
        for quad in range(quads):
            ref[at + quad] = value[:, quad * 128 : (quad + 1) * 128]

    for part in range(3):
        lanes = slice(part * width, (part + 1) * width)
        put(qkv, part * quads, dot(in_ref[:, 0:width], wq_ref[:, lanes]))
    put(gatt, 0, dot_nt(in_ref[:, width:], wo_ref[...]))
    per = 128 // HDIM
    head = lax.broadcasted_iota(jnp.int32, (members, 128), 1) // HDIM

    def spread(v):
        return jnp.concatenate([jnp.where(head == h, v, 0.0) for h in range(per)], 0).astype(BF)

    def gather(v):
        out = jnp.where(head == 0, v[0:members], 0.0)
        for h in range(1, per):
            out = jnp.where(head == h, v[h * members : (h + 1) * members], out)
        return out

    def one_group(g, _):
        at = pl.ds(g, members, stride=groups)
        for quad in range(quads):
            q = qkv[quad, at, :]
            k = qkv[quads + quad, at, :].astype(BF)
            v = qkv[2 * quads + quad, at, :].astype(BF)
            do = gatt[quad, at, :]
            qs, dos = spread(q), spread(do)
            scores = dot_nt(k, qs) * scale
            dp = dot_nt(v, dos)
            p = jnp.exp(scores - jnp.max(scores, 0, keepdims=True))
            p = p / jnp.sum(p, 0, keepdims=True)
            pb = p.astype(BF)
            ds = (p * (dp - jnp.sum(p * dp, 0, keepdims=True)) * scale).astype(BF)
            att[quad, at, :] = gather(dot_tn(pb, v))
            gq[quad, at, :] = gather(dot_tn(ds, k))
            gq[quads + quad, at, :] = dot(ds, qs)
            gq[2 * quads + quad, at, :] = dot(pb, dos)
        return 0

    lax.fori_loop(0, groups, one_group, 0)
    attended = jnp.concatenate([att[i] for i in range(quads)], 1).astype(BF)
    att_out[...] = attended
    send_out[:, 0:width] = dot(attended, wo_ref[...]).astype(BF)
    gqb = jnp.concatenate([gq[i] for i in range(3 * quads)], 1).astype(BF)
    gq_out[...] = gqb
    send_out[:, width:] = dot_nt(gqb, wq_ref[...]).astype(BF)


def attention_block(arrived, w_qkv, w_out):
    tokens = arrived.shape[0]
    width = w_out.shape[0]
    return pl.pallas_call(
        attention_kernel,
        name="grid_attention",
        out_shape=[
            jax.ShapeDtypeStruct((tokens, 2 * width), BF),
            jax.ShapeDtypeStruct((tokens, 3 * width), BF),
            jax.ShapeDtypeStruct((tokens, width), BF),
        ],
        scratch_shapes=[
            pltpu.VMEM((3 * width // 128, tokens, 128), F32),
            pltpu.VMEM((width // 128, tokens, 128), F32),
            pltpu.VMEM((width // 128, tokens, 128), F32),
            pltpu.VMEM((3 * width // 128, tokens, 128), F32),
        ],
        compiler_params=pltpu.CompilerParams(vmem_limit_bytes=48 * 2**20),
        cost_estimate=pl.CostEstimate(
            flops=2 * 512 * 512 * 512 * 8, bytes_accessed=7 * 2**20, transcendentals=2**20
        ),
    )(arrived, w_qkv, w_out)


def residual_kernel(home_ref, resid_ref, go_ref, out_ref, gr_ref):
    width = resid_ref.shape[1]
    resid = resid_ref[...].astype(F32)
    out_ref[...] = (resid + home_ref[:, 0:width].astype(F32)).astype(BF)
    back = normalize_back(resid, home_ref[:, width:].astype(F32))
    gr_ref[...] = (go_ref[...].astype(F32) + back).astype(BF)


def residual_block(home, resid, go):
    return pl.pallas_call(
        residual_kernel,
        name="residual",
        out_shape=[jax.ShapeDtypeStruct(resid.shape, BF)] * 2,
        compiler_params=pltpu.CompilerParams(vmem_limit_bytes=48 * 2**20),
    )(home, resid, go)


def backward_kernel(
    x_ref, gr_ref, above_ref, below_ref, left_ref, right_ref, act_ref, slope_c_ref, slope_e_ref,
    we_ref, wd_ref, wp_ref,
    gx_out, ge_out, gd_out,
    wide, grad_wide, normed, gmid, act, gpre, acc,
):
    step = pl.program_id(0)
    rows, cols = 16, 32

    @pl.when(step == 0)
    def _():
        place_halo(
            wide,
            gr_ref[...].astype(F32), above_ref[...].astype(F32), below_ref[...].astype(F32),
            left_ref[...].astype(F32), right_ref[...].astype(F32), 1, rows, cols,
        )
        grad_wide[...] = wide[...].reshape(grad_wide.shape).astype(BF)
        normed[...] = normalize(x_ref[...].astype(F32))[0].astype(BF)
        acc[...] = jnp.zeros(acc.shape, F32)

    gm = dot_nt(grad_wide[...], wp_ref[...]) * slope_c_ref[...].astype(F32)
    gmid[...] = gm.astype(BF).astype(F32).reshape(gmid.shape)
    act[...] = act_ref[...].astype(F32).reshape(act.shape)
    taps = [wd_ref[k : k + 1, :].astype(F32) for k in range(9)]
    lanes = wd_ref.shape[1]
    inside = lax.broadcasted_iota(jnp.int32, (WIDE, lanes), 0) < cols

    def one_row(r, sums):
        lines = [gmid[r + 2], gmid[r + 1], gmid[r]]
        parts = [sum(lines[i] * taps[3 * i + j] for i in range(3)) for j in range(3)]
        grad_act = parts[1] + roll(parts[0], -1) + roll(parts[2], 1)
        gpre[r] = (grad_act[0:cols] * slope_e_ref[r].astype(F32)).astype(BF)
        own = jnp.where(inside, lines[1], 0.0)
        moved = [roll(own, -1), own, roll(own, 1)]
        new = []
        for i in range(3):
            line = act[r + i]
            for j in range(3):
                prod = (line * moved[j]).reshape(WIDE // 8, 8, lanes)
                new.append(sums[3 * i + j] + jnp.sum(prod, 0))
        return tuple(new)

    zero = jnp.zeros((8, lanes), F32)
    sums = lax.fori_loop(0, rows, one_row, (zero,) * 9)
    gd_out[...] = jnp.zeros(gd_out.shape, F32)
    for k in range(9):
        gd_out[k : k + 1, :] = jnp.sum(sums[k], 0, keepdims=True)
    gp = gpre[...].reshape(rows * cols, lanes)
    ge_out[...] = dot_tn(gp, normed[...]).astype(BF)
    acc[...] += dot_nt(gp, we_ref[...])

    @pl.when(step == pl.num_programs(0) - 1)
    def _():
        back = normalize_back(x_ref[...].astype(F32), acc[...])
        gx_out[...] = (gr_ref[...].astype(F32) + back).astype(BF)


def backward_block(x, gr, strips, act, slope_c, slope_e, w_expand, w_depthwise, w_project):
    tokens, width = x.shape
    hid = w_expand.shape[1]
    rows, cols = 16, 32
    whole = lambda a: pl.BlockSpec(a.shape, lambda j: (0,) * a.ndim)
    return pl.pallas_call(
        backward_kernel,
        name="mbconv_backward",
        grid=(hid // CHUNK,),
        in_specs=[
            whole(x), whole(gr), *[whole(s) for s in strips],
            pl.BlockSpec(((rows + 2) * WIDE, CHUNK), lambda j: (0, j)),
            pl.BlockSpec(((rows + 2) * WIDE, CHUNK), lambda j: (0, j)),
            pl.BlockSpec((rows, cols, CHUNK), lambda j: (0, 0, j)),
            pl.BlockSpec((width, CHUNK), lambda j: (0, j)),
            pl.BlockSpec((9, CHUNK), lambda j: (0, j)),
            pl.BlockSpec((CHUNK, width), lambda j: (j, 0)),
        ],
        out_specs=[
            pl.BlockSpec((tokens, width), lambda j: (0, 0)),
            pl.BlockSpec((CHUNK, width), lambda j: (j, 0)),
            pl.BlockSpec((16, CHUNK), lambda j: (0, j)),
        ],
        out_shape=[
            jax.ShapeDtypeStruct((tokens, width), BF),
            jax.ShapeDtypeStruct((hid, width), BF),
            jax.ShapeDtypeStruct((16, hid), F32),
        ],
        scratch_shapes=[
            pltpu.VMEM((rows + 2, WIDE, width), F32),
            pltpu.VMEM(((rows + 2) * WIDE, width), BF),
            pltpu.VMEM((tokens, width), BF),
            pltpu.VMEM((rows + 2, WIDE, CHUNK), F32),
            pltpu.VMEM((rows + 2, WIDE, CHUNK), F32),
            pltpu.VMEM((rows, cols, CHUNK), BF),
            pltpu.VMEM((tokens, width), F32),
        ],
        compiler_params=pltpu.CompilerParams(vmem_limit_bytes=48 * 2**20),
        cost_estimate=pl.CostEstimate(
            flops=2 * (720 + 1024) * 512 * 2048, bytes_accessed=20 * 2**20, transcendentals=2**20
        ),
    )(x, gr, *strips, act, slope_c, slope_e, w_expand, w_depthwise, w_project)


def sum_to_owners(parts):
    rows, chans = parts.shape[1:]
    mine = lax.axis_index("row") % 2
    by_core = parts.reshape(8, 2, 8, rows, chans)
    kept = lax.dynamic_index_in_dim(by_core, mine, 1, keepdims=False)
    sent = lax.dynamic_index_in_dim(by_core, 1 - mine, 1, keepdims=False)
    got = lax.ppermute(sent, AX, other_core())
    pair = (kept.astype(F32) + got.astype(F32)).astype(BF).reshape(64, rows, chans)
    return jnp.sum(across_chips(pair).astype(F32), 0)


def body(block_input, w_expand, w_depthwise, w_project, w_qkv, w_out, grad_out):
    _, rows, cols, width = block_input.shape
    hid = w_expand.shape[1]
    tokens = rows * cols
    image = block_input[0]
    x = image.reshape(tokens, width)
    go = grad_out[0].reshape(tokens, width)
    act, slope_c, slope_e, mid, resid, send = forward_block(
        x, halo(image, 2), go, w_expand, w_depthwise, w_project
    )
    arrived = across_chips(send.reshape(64, 8, 2 * width)).reshape(tokens, 2 * width)
    back, gqkv, attended = attention_block(arrived, w_qkv, w_out)
    home = across_chips(back.reshape(64, 8, 2 * width)).reshape(tokens, 2 * width)
    grad_qkv = dot_tn(gqkv, arrived[:, :width]).astype(BF)
    grad_outproj = dot_tn(arrived[:, width:], attended).astype(BF)
    out, gr = residual_block(home, resid, go)
    grad_project = dot_tn(mid, gr).astype(BF)
    first = sum_to_owners(
        jnp.concatenate(
            [
                grad_project.reshape(128, -1, width),
                grad_qkv.reshape(128, -1, width),
                grad_outproj.reshape(128, -1, width),
            ],
            1,
        )
    )
    gx, grad_expand, grad_depth = backward_block(
        x, gr, halo(gr.reshape(rows, cols, width), 1), act, slope_c, slope_e,
        w_expand, w_depthwise, w_project,
    )
    depth = grad_depth.reshape(16, 128, 16).transpose(1, 0, 2).reshape(128, 1, 256)
    depth = jnp.pad(depth, ((0, 0), (0, 0), (0, width - 256))).astype(BF)
    second = sum_to_owners(jnp.concatenate([grad_expand.reshape(128, -1, width), depth], 1))
    own = hid // 128
    return (
        out.reshape(1, rows, cols, width),
        gx.reshape(1, rows, cols, width),
        second[:own].T,
        second[own, :256].reshape(16, 16)[:9],
        first[:own].T,
        first[own : own + 12].T,
        first[own + 12 :].T,
    )


def solution(mesh):
    tokens = P(None, "row", "col", None)
    split = P(None, AX)
    return jax.shard_map(
        body,
        mesh=mesh,
        in_specs=(tokens, P(), P(), P(), P(), P(), tokens),
        out_specs=(tokens, tokens, split, split, split, split, split),
        check_vma=False,
    )
```

time: 2300 us -> 245 us (0.11)
  waiting for transfers between devices: 1530 us -> 66.1 us
  blocking collectives: 349 us -> 30.5 us
  starting transfers between devices: 155 us -> 39.9 us
  local copies, waits for them, and re-layouts: 116 us -> 22.6 us
  matrix products: 84.1 us -> 6.15 us
  Pallas kernels: 0 us -> 66 us
    reduce_scatter x2 -> x0, waiting for transfers between devices: 1280 us -> none  [the longest x1 642 us: body(): lax.psum_scatter(totals[0], ('row', 'col'), scatter_dimension=1, tiled=True)]
    unnamed x1 -> x0, blocking collectives: 349 us -> none
    unnamed x38 -> x0, waiting for transfers between devices: 209 us -> none
    unnamed x34 -> x0, starting transfers between devices: 95.3 us -> none
    dot_general x17 -> x3, matrix products: 78.2 us -> 6.15 us  [dot_tn(): lax.dot_general(a, b, (((0,), (0,)), ((), ())), preferred_element_type=F32)]
    pallas_call x0 -> x4, Pallas kernels: none -> 66 us  [the longest x1 25.9 us: forward_block(): pl.pallas_call(forward_kernel, name='mbconv_forward', grid=(hid // CHUNK,...]
    unnamed x54 -> x31, local copies, waits for them, and re-layouts: 55.8 us -> 5.43 us
    all_to_all x0 -> x1, blocking collectives: none -> 30.5 us  [across_chips(): lax.all_to_all(x, AX, 0, 0, tiled=True, axis_index_groups=device_groups(C...]
  transfers between devices with their start and end apart: 48 -> 13, of which waited for: 10 -> 8; matrix products, arithmetic and copies ran while one was open for 23% -> 12% of each run, Pallas kernels for 0% -> 0%
where the time goes in v1:
time: 245 us; the launch traced here: 243 us
  waiting for transfers between devices  66.1 us (27%)
  Pallas kernels  66 us (27%)
  starting transfers between devices  39.9 us (16%)
  blocking collectives  30.5 us (12%)
  local copies, waits for them, and re-layouts  22.6 us (9%)
  other arithmetic  11.2 us (5%)
  matrix products  6.15 us (3%)
    all_to_all x3, waiting for transfers between devices, across_chips(): lax.all_to_all(x, AX, 0, 0, tiled=True, axis_index_groups=device_groups(C...  52.9 us
    all_to_all x1, blocking collectives, across_chips(): lax.all_to_all(x, AX, 0, 0, tiled=True, axis_index_groups=device_groups(C...  30.5 us
    pallas_call x1, Pallas kernels, forward_block(): pl.pallas_call(forward_kernel, name='mbconv_forward', grid=(hid // CHUNK,...  25.9 us
    pallas_call x1, Pallas kernels, backward_block(): pl.pallas_call(backward_kernel, name='mbconv_backward', grid=(hid // CHUN...  23.2 us
    all_to_all x3, starting transfers between devices, across_chips(): lax.all_to_all(x, AX, 0, 0, tiled=True, axis_index_groups=device_groups(C...  22.5 us
    pallas_call x1, Pallas kernels, attention_block(): pl.pallas_call(attention_kernel, name='grid_attention', out_shape=[jax.Sh...  16 us
    ppermute x8, starting transfers between devices, shift(): return lax.ppermute(x, axis, pairs)  15.9 us
    ppermute x8, waiting for transfers between devices, shift(): return lax.ppermute(x, axis, pairs)  13.2 us
  transfers between devices with their start and end apart: 13, of which 8 were waited for; matrix products, arithmetic and copies ran while one was open for 12% of the time, Pallas kernels for 0%

profile of v1, /device:TPU:0, one launch (start us, length us, event | category | flops | bytes accessed | tf_op | source)
XLA Modules:
  0.0 243.5 jit_solution(6105932125545014389)
XLA Ops:
  5.1 3.1 %collective-permute-done.1 = bf16[2,32,512]{2,1,0:T(8,128)(2,1)S(1)} collective-permute-done((bf16[2,32,512]{2,1,0:T(8,128)(2,1)S(1)}, bf16[2,32,512]{2,1,0:T(8,128)(2,1)S(1)}, u32[]{:S(2)}, u32[]{:S(2)}) %collective-permute-start.1) | collective-permute-done | bytes 65568 | tf_op jit(solution)/shard_map/ppermute | solution.py:50
  8.3 5.1 %collective-permute-start.2 = (bf16[20,2,512]{2,1,0:T(2,128)(2,1)S(1)}, bf16[20,2,512]{2,1,0:T(2,128)(2,1)S(1)}, u32[]{:S(2)}, u32[]{:S(2)}) collective-permute-start(bf16[20,2,512]{2,1,0:T(2,128)(2,1)S(1)} %pad_maximum_fusion.1), channel_id=1, source_target_pairs={{0,1},{1,2},{2,3},{3,4},{4,5},{5,6},{6,7},{8,9},{9,10},{10,11},{11... | collective-permute-start | bytes 122888 | tf_op jit(solution)/shard_map/ppermute | solution.py:50
  15.1 5.8 %collective-permute-done.3 = bf16[20,2,512]{2,1,0:T(2,128)(2,1)S(1)} collective-permute-done((bf16[20,2,512]{2,1,0:T(2,128)(2,1)S(1)}, bf16[20,2,512]{2,1,0:T(2,128)(2,1)S(1)}, u32[]{:S(2)}, u32[]{:S(2)}) %collective-permute-start.3) | collective-permute-done | bytes 40992 | tf_op jit(solution)/shard_map/ppermute | solution.py:50
  23.8 25.9 %mbconv_forward.1 = (bf16[720,2048]{1,0:T(8,128)(2,1)}, bf16[720,2048]{1,0:T(8,128)(2,1)}, bf16[16,32,2048]{2,1,0:T(8,128)(2,1)S(1)}, bf16[512,2048]{1,0:T(8,128...) custom-call(bf16[512,512]{1,0:T(8,128)(2,1)S(1)} %bitcast.72, bf16[64,512]{1,0:T(8,128)(2,1)S(1)} %bitcast.77, ...), custom_call_target="tpu_custom_call" | custom-call | flops 2751463424 | bytes 20971520 | tf_op jit(solution)/shard_map/mbconv_forward/pallas_call | solution.py:180
  49.7 30.5 %all_to_all.20 = bf16[64,8,1024]{2,1,0:T(8,128)(2,1)S(1)} all-to-all(bf16[64,8,1024]{2,1,0:T(8,128)(2,1)S(1)} %bitcast.68), channel_id=1, replica_groups={{0,1,2,3,4,5,6,7,16,17,18,19,20,21,22,23,32,33,34,35,36,37,38,39,48,49,..., dimensions={0} | all-to-all | bytes 2097152 | tf_op jit(solution)/shard_map/all_to_all | solution.py:44
  80.2 16.0 %grid_attention.1 = (bf16[512,1024]{1,0:T(8,128)(2,1)}, bf16[512,1536]{1,0:T(8,128)(2,1)S(1)}, bf16[512,512]{1,0:T(8,128)(2,1)S(1)}) custom-call(bf16[512,1024]{1,0:T(8,128)(2,1)S(1)} %bitcast.65, bf16[512,1536]{1,0:T(8,128)(2,1)} %wq_ref.1, bf16[512,512]{1,0:T(8,128)(2,1)S(1)} %copy-done.4), custom_call_target="tpu_custom_call" | custom-call | flops 2147483648 | bytes 7340032 | tf_op jit(solution)/shard_map/grid_attention/pallas_call | solution.py:281
  97.3 5.1 %all-to-all-start.1 = ((bf16[64,8,1024]{2,1,0:T(8,128)(2,1)}), bf16[64,8,1024]{2,1,0:T(8,128)(2,1)S(1)}, u32[]{:S(2)}, u32[]{:S(2)}) async-start(bf16[64,8,1024]{2,1,0:T(8,128)(2,1)} %bitcast.9), calls=%async_computation.1 | async-start | bytes 2097152 | tf_op jit(solution)/shard_map/all_to_all | solution.py:44
  104.9 3.6 %convolution_convert_fusion = bf16[1536,512]{1,0:T(8,128)(2,1)} fusion(bf16[512,1536]{1,0:T(8,128)(2,1)} %copy-done.9, bf16[512,1024]{1,0:T(8,128)(2,1)S(1)} %bitcast.67), kind=kOutput, calls=%fused_computation.7 | convolution fusion | flops 806092800 | bytes 3670016 | tf_op jit(solution)/shard_map/dot_general | solution.py:113
  108.5 3.7 %concatenate.38 = bf16[8,2,8,12,512]{4,3,2,1,0:T(8,128)(2,1)} reshape(bf16[1536,512]{1,0:T(8,128)(2,1)} %convolution_convert_fusion) | data formatting | bytes 3145728 | tf_op jit(solution)/shard_map/concatenate | solution.py:449
  112.3 7.9 %all-to-all-done.1 = bf16[64,8,1024]{2,1,0:T(8,128)(2,1)S(1)} async-done(((bf16[64,8,1024]{2,1,0:T(8,128)(2,1)}), bf16[64,8,1024]{2,1,0:T(8,128)(2,1)S(1)}, u32[]{:S(2)}, u32[]{:S(2)}) %all-to-all-start.1) | async-done | bytes 1048608 | tf_op jit(solution)/shard_map/all_to_all | solution.py:44
  126.6 2.9 %collective-permute-start.6 = (bf16[18,1,512]{2,0,1:T(8,128)(2,1)S(1)}, bf16[18,1,512]{2,0,1:T(8,128)(2,1)S(1)}, u32[]{:S(2)}, u32[]{:S(2)}) collective-permute-start(bf16[18,1,512]{2,0,1:T(8,128)(2,1)S(1)} %pad_maximum_fusion.3), channel_id=1, source_target_pairs={{0,1},{1,2},{2,3},{3,4},{4,5},{5,6},{6,7},{8,9},{9,10},{10,11},{11... | collective-permute-start | bytes 55304 | tf_op jit(solution)/shard_map/ppermute | solution.py:50
  129.5 1.5 collective-permute-start.7
  131.0 2.9 %pad_maximum_fusion = bf16[8,2,8,32,512]{4,3,2,1,0:T(8,128)(2,1)} fusion(bf16[8,2,8,4,512]{4,3,2,1,0:T(4,128)(2,1)S(1)} %concatenate.39, bf16[8,2,8,12,512]{4,3,2,1,0:T(8,128)(2,1)S(1)} %copy-done.10, bf16[8,2,8,16,512]{4,3,2,1,0:T(8,128)(2,1)S(1)} %bitcast.81), kind=kLoop, calls=%fused_computation | loop fusion | flops 12582912 | bytes 8388608 | tf_op jit(solution)/shard_map/concatenate | solution.py:449
  134.0 2.7 %collective-permute-done.7 = bf16[18,1,512]{2,0,1:T(8,128)(2,1)S(1)} collective-permute-done((bf16[18,1,512]{2,0,1:T(8,128)(2,1)S(1)}, bf16[18,1,512]{2,0,1:T(8,128)(2,1)S(1)}, u32[]{:S(2)}, u32[]{:S(2)}) %collective-permute-start.7) | collective-permute-done | bytes 18464 | tf_op jit(solution)/shard_map/ppermute | solution.py:50
  136.7 23.2 %mbconv_backward.1 = (bf16[512,512]{1,0:T(8,128)(2,1)}, bf16[2048,512]{1,0:T(8,128)(2,1)S(1)}, f32[16,2048]{1,0:T(8,128)S(1)}) custom-call(bf16[512,512]{1,0:T(8,128)(2,1)S(1)} %bitcast.73, bf16[512,512]{1,0:T(8,128)(2,1)S(1)} %get-tuple-element.25.gr_ref, bf16[32,512]{1,0:T(8,128)(2,1)S(1)} %bitcast.74, bf16[32,512]{1,0:T(8,128)(2,1)S(1)} %bitcast.75, ...), custom_call_target="tpu_custom_call" | custom-call | flops 3657433088 | bytes 20971520 | tf_op jit(solution)/shard_map/mbconv_backward/pallas_call | solution.py:381
  163.2 1.5 collective-permute-start.8
  164.7 3.2 %dynamic-slice_bitcast_fusion = bf16[8,8,32,512]{3,2,1,0:T(8,128)(2,1)} fusion(bf16[8,2,8,32,512]{4,3,2,1,0:T(8,128)(2,1)} %pad_maximum_fusion, s32[]{:T(128)S(6)} %select_n.21), kind=kLoop, calls=%fused_computation.11 | loop fusion | bytes 4194308 | tf_op jit(solution)/shard_map/jit(dynamic_index_in_dim)/squeeze | solution.py:425
  168.3 1.8 copy.56
  170.1 11.7 %all-to-all-start.2 = ((bf16[64,17,512]{2,1,0:T(8,128)(2,1)}), bf16[64,17,512]{2,1,0:T(8,128)(2,1)S(1)}, u32[]{:S(2)}, u32[]{:S(2)}) async-start(bf16[64,17,512]{2,1,0:T(8,128)(2,1)} %copy.56), calls=%async_computation.2 | async-start | bytes 3145728 | tf_op jit(solution)/shard_map/all_to_all | solution.py:44
  181.8 4.6 %fusion = bf16[8,8,32,512]{3,2,1,0:T(8,128)(2,1)} fusion(bf16[8,8,32,512]{3,2,1,0:T(8,128)(2,1)} %collective-permute-done.9, bf16[8,2,8,32,512]{4,3,2,1,0:T(8,128)(2,1)} %pad_maximum_fusion, s32[]{:T(128)S(6)} %select_n.20), kind=kLoop, calls=%fused_computation.2 | loop fusion | flops 4194304 | bytes 6291460 | tf_op jit(solution)/shard_map/convert_element_type | solution.py:427
  186.4 19.4 %all-to-all-done.2 = bf16[64,17,512]{2,1,0:T(8,128)(2,1)S(1)} async-done(((bf16[64,17,512]{2,1,0:T(8,128)(2,1)}), bf16[64,17,512]{2,1,0:T(8,128)(2,1)S(1)}, u32[]{:S(2)}, u32[]{:S(2)}) %all-to-all-start.2) | async-done | bytes 1114144 | tf_op jit(solution)/shard_map/all_to_all | solution.py:44
  207.0 5.7 %all-to-all-start.3 = ((bf16[64,32,512]{2,1,0:T(8,128)(2,1)}), bf16[64,32,512]{2,1,0:T(8,128)(2,1)S(1)}, u32[]{:S(2)}, u32[]{:S(2)}) async-start(bf16[64,32,512]{2,1,0:T(8,128)(2,1)} %bitcast.30), calls=%async_computation.3 | async-start | bytes 4194304 | tf_op jit(solution)/shard_map/all_to_all | solution.py:44
  212.7 1.7 convert_reduce_fusion.1
  215.7 25.6 %all-to-all-done.3 = bf16[64,32,512]{2,1,0:T(8,128)(2,1)S(1)} async-done(((bf16[64,32,512]{2,1,0:T(8,128)(2,1)}), bf16[64,32,512]{2,1,0:T(8,128)(2,1)S(1)}, u32[]{:S(2)}, u32[]{:S(2)}) %all-to-all-start.3) | async-done | bytes 2097184 | tf_op jit(solution)/shard_map/all_to_all | solution.py:44
  (78 shorter events, 27.4 us)
Async XLA Ops:
  1.5 6.7 %collective-permute-start = (bf16[2,32,512]{2,1,0:T(8,128)(2,1)S(1)}, bf16[2,32,512]{2,1,0:T(8,128)(2,1)S(1)}, u32[]{:S(2)}, u32[]{:S(2)}) collective-permute-start(bf16[2,32,512]{2,1,0:T(8,128)(2,1)S(1)} %get-tuple-element.42), channel_id=1, source_target_pairs={{0,8},{8,16},{16,24},{24,32},{32,40},{40,48},{48,56},{56,64},{64,7... | collective-permute-start | bytes 196616 | tf_op jit(solution)/shard_map/ppermute | solution.py:50
  2.8 5.4 %collective-permute-start.1 = (bf16[2,32,512]{2,1,0:T(8,128)(2,1)S(1)}, bf16[2,32,512]{2,1,0:T(8,128)(2,1)S(1)}, u32[]{:S(2)}, u32[]{:S(2)}) collective-permute-start(bf16[2,32,512]{2,1,0:T(8,128)(2,1)S(1)} %get-tuple-element.41), channel_id=1, source_target_pairs={{8,0},{16,8},{24,16},{32,24},{40,32},{48,40},{56,48},{64,56},{72,6... | collective-permute-start | bytes 196616 | tf_op jit(solution)/shard_map/ppermute | solution.py:50
  8.3 6.8 %collective-permute-start.2 = (bf16[20,2,512]{2,1,0:T(2,128)(2,1)S(1)}, bf16[20,2,512]{2,1,0:T(2,128)(2,1)S(1)}, u32[]{:S(2)}, u32[]{:S(2)}) collective-permute-start(bf16[20,2,512]{2,1,0:T(2,128)(2,1)S(1)} %pad_maximum_fusion.1), channel_id=1, source_target_pairs={{0,1},{1,2},{2,3},{3,4},{4,5},{5,6},{6,7},{8,9},{9,10},{10,11},{11... | collective-permute-start | bytes 122888 | tf_op jit(solution)/shard_map/ppermute | solution.py:50
  13.5 7.4 %collective-permute-start.3 = (bf16[20,2,512]{2,1,0:T(2,128)(2,1)S(1)}, bf16[20,2,512]{2,1,0:T(2,128)(2,1)S(1)}, u32[]{:S(2)}, u32[]{:S(2)}) collective-permute-start(bf16[20,2,512]{2,1,0:T(2,128)(2,1)S(1)} %pad_maximum_fusion.2), channel_id=1, source_target_pairs={{1,0},{2,1},{3,2},{4,3},{5,4},{6,5},{7,6},{9,8},{10,9},{11,10},{12... | collective-permute-start | bytes 122888 | tf_op jit(solution)/shard_map/ppermute | solution.py:50
  20.9 1.0 copy-start
  49.7 30.5 %copy-start.7 = (bf16[16,32,2048]{2,1,0:T(8,128)(2,1)}, bf16[16,32,2048]{2,1,0:T(8,128)(2,1)S(1)}, u32[]{:S(2)}) copy-start(bf16[16,32,2048]{2,1,0:T(8,128)(2,1)S(1)} %get-tuple-element.28.slope_e_ref) | copy-start | bytes 6291460
  49.7 30.5 %copy-start.4 = (bf16[512,512]{1,0:T(8,128)(2,1)S(1)}, bf16[512,512]{1,0:T(8,128)(2,1)}, u32[]{:S(2)}) copy-start(bf16[512,512]{1,0:T(8,128)(2,1)} %wo_ref.1) | copy-start | bytes 1572868
  96.2 1.1 copy-start.9
  97.3 22.8 %all-to-all-start.1 = ((bf16[64,8,1024]{2,1,0:T(8,128)(2,1)}), bf16[64,8,1024]{2,1,0:T(8,128)(2,1)S(1)}, u32[]{:S(2)}, u32[]{:S(2)}) async-start(bf16[64,8,1024]{2,1,0:T(8,128)(2,1)} %bitcast.9), calls=%async_computation.1 | async-start | bytes 2097152 | tf_op jit(solution)/shard_map/all_to_all | solution.py:44
  108.5 11.6 %copy-start.1 = (bf16[1,16,32,512]{3,2,1,0:T(8,128)(2,1)S(1)}, bf16[1,16,32,512]{3,2,1,0:T(8,128)(2,1)}, u32[]{:S(2)}) copy-start(bf16[1,16,32,512]{3,2,1,0:T(8,128)(2,1)} %param.13) | copy-start | bytes 1572868
  120.1 3.7 %copy-start.12 = (bf16[512,2048]{1,0:T(8,128)(2,1)S(1)}, bf16[512,2048]{1,0:T(8,128)(2,1)}, u32[]{:S(2)}) copy-start(bf16[512,2048]{1,0:T(8,128)(2,1)} %get-tuple-element.32) | copy-start | bytes 6291460
  121.1 5.4 %collective-permute-start.4 = (bf16[1,32,512]{2,0,1:T(2,128)(2,1)S(1)}, bf16[1,32,512]{2,0,1:T(2,128)(2,1)S(1)}, u32[]{:S(2)}, u32[]{:S(2)}) collective-permute-start(bf16[1,32,512]{2,0,1:T(2,128)(2,1)S(1)} %copy.47), channel_id=1, source_target_pairs={{0,8},{8,16},{16,24},{24,32},{32,40},{40,48},{48,56},{56,64},{64,7... | collective-permute-start | bytes 98312 | tf_op jit(solution)/shard_map/ppermute | solution.py:50
  122.5 4.0 %collective-permute-start.5 = (bf16[1,32,512]{2,0,1:T(2,128)(2,1)S(1)}, bf16[1,32,512]{2,0,1:T(2,128)(2,1)S(1)}, u32[]{:S(2)}, u32[]{:S(2)}) collective-permute-start(bf16[1,32,512]{2,0,1:T(2,128)(2,1)S(1)} %copy.48), channel_id=1, source_target_pairs={{8,0},{16,8},{24,16},{32,24},{40,32},{48,40},{56,48},{64,56},{72,6... | collective-permute-start | bytes 98312 | tf_op jit(solution)/shard_map/ppermute | solution.py:50
  123.8 7.1 %copy-start.10 = (bf16[8,2,8,12,512]{4,3,2,1,0:T(8,128)(2,1)S(1)}, bf16[8,2,8,12,512]{4,3,2,1,0:T(8,128)(2,1)}, u32[]{:S(2)}) copy-start(bf16[8,2,8,12,512]{4,3,2,1,0:T(8,128)(2,1)} %concatenate.38) | copy-start | bytes 4718596
  126.6 7.4 %collective-permute-start.6 = (bf16[18,1,512]{2,0,1:T(8,128)(2,1)S(1)}, bf16[18,1,512]{2,0,1:T(8,128)(2,1)S(1)}, u32[]{:S(2)}, u32[]{:S(2)}) collective-permute-start(bf16[18,1,512]{2,0,1:T(8,128)(2,1)S(1)} %pad_maximum_fusion.3), channel_id=1, source_target_pairs={{0,1},{1,2},{2,3},{3,4},{4,5},{5,6},{6,7},{8,9},{9,10},{10,11},{11... | collective-permute-start | bytes 55304 | tf_op jit(solution)/shard_map/ppermute | solution.py:50
  129.5 7.2 %collective-permute-start.7 = (bf16[18,1,512]{2,0,1:T(8,128)(2,1)S(1)}, bf16[18,1,512]{2,0,1:T(8,128)(2,1)S(1)}, u32[]{:S(2)}, u32[]{:S(2)}) collective-permute-start(bf16[18,1,512]{2,0,1:T(8,128)(2,1)S(1)} %pad_maximum_fusion.4), channel_id=1, source_target_pairs={{1,0},{2,1},{3,2},{4,3},{5,4},{6,5},{7,6},{9,8},{10,9},{11,10},{12... | collective-permute-start | bytes 55304 | tf_op jit(solution)/shard_map/ppermute | solution.py:50
  131.0 5.7 %copy-start.3 = (bf16[1,16,32,512]{3,2,1,0:T(8,128)(2,1)S(1)}, bf16[1,16,32,512]{3,2,1,0:T(8,128)(2,1)}, u32[]{:S(2)}) copy-start(bf16[1,16,32,512]{3,2,1,0:T(8,128)(2,1)} %param.7) | copy-start | bytes 1572868
  131.0 5.7 %copy-start.6 = (bf16[9,2048]{1,0:T(8,128)(2,1)S(1)}, bf16[9,2048]{1,0:T(8,128)(2,1)}, u32[]{:S(2)}) copy-start(bf16[9,2048]{1,0:T(8,128)(2,1)} %wd_ref.3) | copy-start | bytes 110596
  131.0 5.7 %copy-start.8 = (bf16[16,32,2048]{2,1,0:T(8,128)(2,1)S(1)}, bf16[16,32,2048]{2,1,0:T(8,128)(2,1)}, u32[]{:S(2)}) copy-start(bf16[16,32,2048]{2,1,0:T(8,128)(2,1)} %copy-done.7) | copy-start | bytes 6291460
  163.2 4.7 %collective-permute-start.8 = (bf16[8,8,17,512]{3,1,2,0:T(8,128)(2,1)}, bf16[8,8,17,512]{3,1,2,0:T(8,128)(2,1)S(1)}, u32[]{:S(2)}, u32[]{:S(2)}) collective-permute-start(bf16[8,8,17,512]{3,1,2,0:T(8,128)(2,1)} %fusion.3), channel_id=1, source_target_pairs={{0,8},{1,9},{2,10},{3,11},{4,12},{5,13},{6,14},{7,15},{8,0},{9,1},... | collective-permute-start | bytes 3342344 | tf_op jit(solution)/shard_map/ppermute | solution.py:426
  168.0 13.8 %collective-permute-start.9 = (bf16[8,8,32,512]{3,2,1,0:T(8,128)(2,1)}, bf16[8,8,32,512]{3,2,1,0:T(8,128)(2,1)}, u32[]{:S(2)}, u32[]{:S(2)}) collective-permute-start(bf16[8,8,32,512]{3,2,1,0:T(8,128)(2,1)} %dynamic-slice_bitcast_fusion), channel_id=1, source_target_pairs={{0,8},{1,9},{2,10},{3,11},{4,12},{5,13},{6,14},{7,15},{8,0},{9,1},... | collective-permute-start | bytes 6291464 | tf_op jit(solution)/shard_map/ppermute | solution.py:426
  170.1 35.7 %all-to-all-start.2 = ((bf16[64,17,512]{2,1,0:T(8,128)(2,1)}), bf16[64,17,512]{2,1,0:T(8,128)(2,1)S(1)}, u32[]{:S(2)}, u32[]{:S(2)}) async-start(bf16[64,17,512]{2,1,0:T(8,128)(2,1)} %copy.56), calls=%async_computation.2 | async-start | bytes 3145728 | tf_op jit(solution)/shard_map/all_to_all | solution.py:44
  205.8 1.2 copy-start.11
  207.0 34.4 %all-to-all-start.3 = ((bf16[64,32,512]{2,1,0:T(8,128)(2,1)}), bf16[64,32,512]{2,1,0:T(8,128)(2,1)S(1)}, u32[]{:S(2)}, u32[]{:S(2)}) async-start(bf16[64,32,512]{2,1,0:T(8,128)(2,1)} %bitcast.30), calls=%async_computation.3 | async-start | bytes 4194304 | tf_op jit(solution)/shard_map/all_to_all | solution.py:44
  (2 other events, 1.9 us)

commit v2 on v1

v2 whole, which is shorter than its diff:
```python
import functools
import itertools

import jax
import jax.numpy as jnp
from jax import lax
from jax.experimental import pallas as pl
from jax.experimental.pallas import tpu as pltpu
from jax.sharding import PartitionSpec as P

HEADS = 16
HDIM = 32
EPS = 1e-05
BF = jnp.bfloat16
F32 = jnp.float32
AX = ("row", "col")
WIDE = 40
CHUNK = 256

SIZES = dict(y_lo=2, z=4, core=2, x=4, y_hi=2)
STRIDES = dict(y_lo=64, z=16, core=8, x=2, y_hi=1)
CHIPS = ("y_lo", "z", "x", "y_hi")


def device_groups(axes):
    rest = [a for a in SIZES if a not in axes]
    found = []
    for at in itertools.product(*[range(SIZES[a]) for a in rest]):
        base = sum(v * STRIDES[a] for v, a in zip(at, rest))
        found.append(
            [
                base + sum(v * STRIDES[a] for v, a in zip(m, axes))
                for m in itertools.product(*[range(SIZES[a]) for a in axes])
            ]
        )
    return found


def other_core():
    return [(d, d ^ STRIDES["core"]) for d in range(128)]


def across_chips(x):
    return lax.all_to_all(x, AX, 0, 0, tiled=True, axis_index_groups=device_groups(CHIPS))


def shift(x, axis, step):
    n = lax.axis_size(axis)
    pairs = [(i, i + step) for i in range(n) if 0 <= i + step < n]
    return lax.ppermute(x, axis, pairs)


def halo(x, width):
    rows, cols, chans = x.shape
    above = shift(x[rows - width :], "row", 1)
    below = shift(x[:width], "row", -1)
    to_right = jnp.concatenate(
        [above[:, cols - width :], x[:, cols - width :], below[:, cols - width :]], 0
    )
    to_left = jnp.concatenate([above[:, :width], x[:, :width], below[:, :width]], 0)
    left = shift(to_right, "col", 1)
    right = shift(to_left, "col", -1)
    gap = jnp.zeros((rows + 2 * width, 8 - 2 * width, chans), x.dtype)
    sides = jnp.concatenate([right, gap, left], 1)
    flat = [v.reshape(-1, chans) for v in (above, below, sides)]
    return jnp.concatenate(flat, 0)


def place(wide, centre, strips, width, rows, cols):
    lanes = centre.shape[-1]
    n = width * cols
    wide[width : width + rows, 0:cols, :] = centre.reshape(rows, cols, lanes)
    wide[0:width, 0:cols, :] = strips[0:n].reshape(width, cols, lanes)
    wide[width + rows :, 0:cols, :] = strips[n : 2 * n].reshape(width, cols, lanes)
    wide[:, cols:, :] = strips[2 * n :].reshape(rows + 2 * width, WIDE - cols, lanes)


def normalize(x):
    center = x - jnp.mean(x, -1, keepdims=True)
    ratio = lax.rsqrt(jnp.mean(center * center, -1, keepdims=True) + EPS)
    return center * ratio, ratio


def normalize_back(x, grad):
    scaled, ratio = normalize(x)
    return (
        grad
        - jnp.mean(grad, -1, keepdims=True)
        - scaled * jnp.mean(grad * scaled, -1, keepdims=True)
    ) * ratio


A0 = 0.7978845608028654
A1 = A0 * 0.044715


def gelu_parts(x):
    inner = A0 + A1 * (x * x)
    half = 0.5 + 0.5 * jnp.tanh(x * inner)
    value = x * half
    return value, half + (value - value * half) * (6.0 * inner - 4.0 * A0)


def dot(a, b):
    return jnp.dot(a, b, preferred_element_type=F32)


def dot_nt(a, b):
    return lax.dot_general(a, b, (((1,), (1,)), ((), ())), preferred_element_type=F32)


def dot_tn(a, b):
    return lax.dot_general(a, b, (((0,), (0,)), ((), ())), preferred_element_type=F32)


def roll(x, by):
    return pltpu.roll(x, by % x.shape[0], 0)


def expand_kernel(x_ref, we_ref, act_out, slope_out, normed):
    @pl.when(pl.program_id(0) == 0)
    def _():
        normed[...] = normalize(x_ref[...].astype(F32))[0].astype(BF)

    for tile in range(0, x_ref.shape[0], 128):
        value, slope = gelu_parts(dot(normed[tile : tile + 128, :], we_ref[...]))
        act_out[tile : tile + 128, :] = value.astype(BF)
        slope_out[tile : tile + 128, :] = slope.astype(BF)


def expand_block(x, w_expand):
    tokens, width = x.shape
    hid = w_expand.shape[1]
    lanes = 512
    return pl.pallas_call(
        expand_kernel,
        name="expand",
        grid=(hid // lanes,),
        in_specs=[
            pl.BlockSpec((tokens, width), lambda j: (0, 0)),
            pl.BlockSpec((width, lanes), lambda j: (0, j)),
        ],
        out_specs=[pl.BlockSpec((tokens, lanes), lambda j: (0, j))] * 2,
        out_shape=[jax.ShapeDtypeStruct((tokens, hid), BF)] * 2,
        scratch_shapes=[pltpu.VMEM((tokens, width), BF)],
        compiler_params=pltpu.CompilerParams(vmem_limit_bytes=48 * 2**20),
        cost_estimate=pl.CostEstimate(
            flops=16 * 512 * 512 * 2048, bytes_accessed=8 * 2**20, transcendentals=2**20
        ),
    )(x, w_expand)


def forward_kernel(
    x_ref, strips_ref, go_ref, act_ref, we_ref, wd_ref, wp_ref,
    act_out, slope_out, mid_out, resid_out, send_out,
    normed, act, acc,
):
    step = pl.program_id(0)
    rows, cols = 16, 32

    @pl.when(step == 0)
    def _():
        normed[...] = normalize(strips_ref[...].astype(F32))[0].astype(BF)
        acc[...] = jnp.zeros(acc.shape, F32)

    strips = jax.nn.gelu(dot(normed[...], we_ref[...])).astype(BF).astype(F32)
    place(act, act_ref[...].astype(F32), strips, 2, rows, cols)
    act_out[...] = act[1 : rows + 3].reshape(act_out.shape).astype(BF)
    for lo in range(0, CHUNK, 128):
        lanes = slice(lo, lo + 128)
        taps = [wd_ref[k : k + 1, lanes].astype(F32) for k in range(9)]
        lines = [act[0, :, lanes], act[1, :, lanes]]
        held = None
        for r in range(rows + 2):
            lines = lines[-2:] + [act[r + 2, :, lanes]]
            sums = [sum(lines[i] * taps[3 * i + j] for i in range(3)) for j in range(3)]
            value, slope = gelu_parts(sums[1] + roll(sums[0], 1) + roll(sums[2], -1))
            if 1 <= r <= rows:
                mid_out[(r - 1) * cols : r * cols, lanes] = value[0:cols].astype(BF)
            if r % 2:
                pair = jnp.concatenate([held, slope], 0).astype(BF)
                slope_out[(r - 1) * WIDE : (r + 1) * WIDE, lanes] = pair
            held = slope
    acc[...] += dot(mid_out[...], wp_ref[...])

    @pl.when(step == pl.num_programs(0) - 1)
    def _():
        resid = (x_ref[...].astype(F32) + acc[...]).astype(BF)
        resid_out[...] = resid
        width = resid.shape[1]
        send_out[:, 0:width] = normalize(resid.astype(F32))[0].astype(BF)
        send_out[:, width:] = go_ref[...]


def forward_block(x, strips, go, act, w_expand, w_depthwise, w_project):
    tokens, width = x.shape
    hid = w_expand.shape[1]
    rows, cols = 16, 32
    whole = lambda a: pl.BlockSpec(a.shape, lambda j: (0,) * a.ndim)
    return pl.pallas_call(
        forward_kernel,
        name="mbconv_forward",
        grid=(hid // CHUNK,),
        in_specs=[
            whole(x), whole(strips), whole(go),
            pl.BlockSpec((tokens, CHUNK), lambda j: (0, j)),
            pl.BlockSpec((width, CHUNK), lambda j: (0, j)),
            pl.BlockSpec((9, CHUNK), lambda j: (0, j)),
            pl.BlockSpec((CHUNK, width), lambda j: (j, 0)),
        ],
        out_specs=[
            pl.BlockSpec(((rows + 2) * WIDE, CHUNK), lambda j: (0, j)),
            pl.BlockSpec(((rows + 2) * WIDE, CHUNK), lambda j: (0, j)),
            pl.BlockSpec((tokens, CHUNK), lambda j: (0, j)),
            pl.BlockSpec((tokens, width), lambda j: (0, 0)),
            pl.BlockSpec((tokens, 2 * width), lambda j: (0, 0)),
        ],
        out_shape=[
            jax.ShapeDtypeStruct(((rows + 2) * WIDE, hid), BF),
            jax.ShapeDtypeStruct(((rows + 2) * WIDE, hid), BF),
            jax.ShapeDtypeStruct((tokens, hid), BF),
            jax.ShapeDtypeStruct((tokens, width), BF),
            jax.ShapeDtypeStruct((tokens, 2 * width), BF),
        ],
        scratch_shapes=[
            pltpu.VMEM(strips.shape, BF),
            pltpu.VMEM((rows + 4, WIDE, CHUNK), F32),
            pltpu.VMEM((tokens, width), F32),
        ],
        compiler_params=pltpu.CompilerParams(vmem_limit_bytes=48 * 2**20),
        cost_estimate=pl.CostEstimate(
            flops=2 * (800 + 512) * 512 * 2048, bytes_accessed=20 * 2**20, transcendentals=3 * 2**20
        ),
    )(x, strips, go, act, w_expand, w_depthwise, w_project)


def attention_kernel(in_ref, wq_ref, wo_ref, send_out, gq_out, att_out, qkv, gatt, att, gq):
    width = wo_ref.shape[0]
    groups = 8
    members = in_ref.shape[0] // groups
    scale = HDIM ** (-0.5)
    quads = width // 128

    def put(ref, at, value):
        value = value.astype(BF).astype(F32)
        for quad in range(quads):
            ref[at + quad] = value[:, quad * 128 : (quad + 1) * 128]

    for part in range(3):
        lanes = slice(part * width, (part + 1) * width)
        put(qkv, part * quads, dot(in_ref[:, 0:width], wq_ref[:, lanes]))
    put(gatt, 0, dot_nt(in_ref[:, width:], wo_ref[...]))
    per = 128 // HDIM
    head = lax.broadcasted_iota(jnp.int32, (members, 128), 1) // HDIM

    def spread(v):
        return jnp.concatenate([jnp.where(head == h, v, 0.0) for h in range(per)], 0).astype(BF)

    def gather(v):
        out = jnp.where(head == 0, v[0:members], 0.0)
        for h in range(1, per):
            out = jnp.where(head == h, v[h * members : (h + 1) * members], out)
        return out

    def one_group(g, _):
        at = pl.ds(g, members, stride=groups)
        for quad in range(quads):
            q = qkv[quad, at, :]
            k = qkv[quads + quad, at, :].astype(BF)
            v = qkv[2 * quads + quad, at, :].astype(BF)
            do = gatt[quad, at, :]
            qs, dos = spread(q), spread(do)
            scores = dot_nt(k, qs) * scale
            dp = dot_nt(v, dos)
            p = jnp.exp(scores - jnp.max(scores, 0, keepdims=True))
            p = p / jnp.sum(p, 0, keepdims=True)
            pb = p.astype(BF)
            ds = (p * (dp - jnp.sum(p * dp, 0, keepdims=True)) * scale).astype(BF)
            att[quad, at, :] = gather(dot_tn(pb, v))
            gq[quad, at, :] = gather(dot_tn(ds, k))
            gq[quads + quad, at, :] = dot(ds, qs)
            gq[2 * quads + quad, at, :] = dot(pb, dos)
        return 0

    lax.fori_loop(0, groups, one_group, 0)
    attended = jnp.concatenate([att[i] for i in range(quads)], 1).astype(BF)
    att_out[...] = attended
    send_out[:, 0:width] = dot(attended, wo_ref[...]).astype(BF)
    gqb = jnp.concatenate([gq[i] for i in range(3 * quads)], 1).astype(BF)
    gq_out[...] = gqb
    send_out[:, width:] = dot_nt(gqb, wq_ref[...]).astype(BF)


def attention_block(arrived, w_qkv, w_out):
    tokens = arrived.shape[0]
    width = w_out.shape[0]
    return pl.pallas_call(
        attention_kernel,
        name="grid_attention",
        out_shape=[
            jax.ShapeDtypeStruct((tokens, 2 * width), BF),
            jax.ShapeDtypeStruct((tokens, 3 * width), BF),
            jax.ShapeDtypeStruct((tokens, width), BF),
        ],
        scratch_shapes=[
            pltpu.VMEM((3 * width // 128, tokens, 128), F32),
            pltpu.VMEM((width // 128, tokens, 128), F32),
            pltpu.VMEM((width // 128, tokens, 128), F32),
            pltpu.VMEM((3 * width // 128, tokens, 128), F32),
        ],
        compiler_params=pltpu.CompilerParams(vmem_limit_bytes=48 * 2**20),
        cost_estimate=pl.CostEstimate(
            flops=2 * 512 * 512 * 512 * 8, bytes_accessed=7 * 2**20, transcendentals=2**20
        ),
    )(arrived, w_qkv, w_out)


def residual_kernel(home_ref, resid_ref, go_ref, out_ref, gr_ref):
    width = resid_ref.shape[1]
    resid = resid_ref[...].astype(F32)
    out_ref[...] = (resid + home_ref[:, 0:width].astype(F32)).astype(BF)
    back = normalize_back(resid, home_ref[:, width:].astype(F32))
    gr_ref[...] = (go_ref[...].astype(F32) + back).astype(BF)


def residual_block(home, resid, go):
    return pl.pallas_call(
        residual_kernel,
        name="residual",
        out_shape=[jax.ShapeDtypeStruct(resid.shape, BF)] * 2,
        compiler_params=pltpu.CompilerParams(vmem_limit_bytes=48 * 2**20),
    )(home, resid, go)


def split_by_core(core, full, mine_out, other_out):
    half = full.shape[0] // 2
    own = pl.multiple_of(core * half, half)
    mine_out[...] = full[pl.ds(own, half), :]
    other_out[...] = full[pl.ds(pl.multiple_of(half - own, half), half), :].astype(BF)


def backward_kernel(
    core_ref, x_ref, gr_ref, strips_ref, act_ref, slope_c_ref, slope_e_ref, we_ref, wd_ref, wp_ref,
    gx_out, mine_out, other_out,
    wide, grad_wide, normed, gmid, act, gpre, full, taps_t, acc,
):
    step = pl.program_id(0)
    rows, cols = 16, 32
    width = x_ref.shape[1]

    @pl.when(step == 0)
    def _():
        place(wide, gr_ref[...].astype(F32), strips_ref[...].astype(F32), 1, rows, cols)
        grad_wide[...] = wide[...].reshape(grad_wide.shape).astype(BF)
        normed[...] = normalize(x_ref[...].astype(F32))[0].astype(BF)
        acc[...] = jnp.zeros(acc.shape, F32)
        taps_t[...] = jnp.zeros(taps_t.shape, F32)

    gm = dot_nt(grad_wide[...], wp_ref[...]) * slope_c_ref[...].astype(F32)
    gmid[...] = gm.reshape(gmid.shape)
    act[...] = act_ref[...].astype(F32).reshape(act.shape)
    inside = lax.broadcasted_iota(jnp.int32, (WIDE, 128), 0) < cols
    for lo in range(0, CHUNK, 128):
        lanes = slice(lo, lo + 128)
        taps = [wd_ref[k : k + 1, lanes].astype(F32) for k in range(9)]
        sums = [None] * 9
        grads = [gmid[0, :, lanes], gmid[1, :, lanes]]
        acts = [act[0, :, lanes], act[1, :, lanes]]
        for r in range(rows):
            grads = grads[-2:] + [gmid[r + 2, :, lanes]]
            acts = acts[-2:] + [act[r + 2, :, lanes]]
            parts = [sum(grads[2 - i] * taps[3 * i + j] for i in range(3)) for j in range(3)]
            grad_act = parts[1] + roll(parts[0], -1) + roll(parts[2], 1)
            at = slice(r * cols, (r + 1) * cols)
            gpre[at, lanes] = (grad_act[0:cols] * slope_e_ref[at, lanes].astype(F32)).astype(BF)
            own = jnp.where(inside, grads[1], 0.0)
            moved = [roll(own, -1), own, roll(own, 1)]
            for k in range(9):
                prod = jnp.sum((acts[k // 3] * moved[k % 3]).reshape(WIDE // 8, 8, 128), 0)
                sums[k] = prod if r == 0 else sums[k] + prod
        for k in range(9):
            taps_t[k : k + 1, lanes] = jnp.sum(sums[k], 0, keepdims=True)
    full[:, 0:width] = dot_tn(gpre[...], normed[...])
    full[:, width:] = taps_t[...].T
    split_by_core(core_ref[0], full, mine_out, other_out)
    acc[...] += dot_nt(gpre[...], we_ref[...])

    @pl.when(step == pl.num_programs(0) - 1)
    def _():
        back = normalize_back(x_ref[...].astype(F32), acc[...])
        gx_out[...] = (gr_ref[...].astype(F32) + back).astype(BF)


def backward_block(core, x, gr, strips, act, slope_c, slope_e, w_expand, w_depthwise, w_project):
    tokens, width = x.shape
    hid = w_expand.shape[1]
    rows, cols = 16, 32
    whole = lambda a: pl.BlockSpec(a.shape, lambda j, c: (0,) * a.ndim)
    return pl.pallas_call(
        backward_kernel,
        name="mbconv_backward",
        grid_spec=pltpu.PrefetchScalarGridSpec(
            num_scalar_prefetch=1,
            grid=(hid // CHUNK,),
            in_specs=[
                whole(x), whole(gr), whole(strips),
                pl.BlockSpec(((rows + 2) * WIDE, CHUNK), lambda j, c: (0, j)),
                pl.BlockSpec(((rows + 2) * WIDE, CHUNK), lambda j, c: (0, j)),
                pl.BlockSpec((tokens, CHUNK), lambda j, c: (0, j)),
                pl.BlockSpec((width, CHUNK), lambda j, c: (0, j)),
                pl.BlockSpec((9, CHUNK), lambda j, c: (0, j)),
                pl.BlockSpec((CHUNK, width), lambda j, c: (j, 0)),
            ],
            out_specs=[
                pl.BlockSpec((tokens, width), lambda j, c: (0, 0)),
                pl.BlockSpec((CHUNK // 2, width + 128), lambda j, c: (j, 0)),
                pl.BlockSpec((CHUNK // 2, width + 128), lambda j, c: (j, 0)),
            ],
            scratch_shapes=[
                pltpu.VMEM((rows + 2, WIDE, width), F32),
                pltpu.VMEM(((rows + 2) * WIDE, width), BF),
                pltpu.VMEM((tokens, width), BF),
                pltpu.VMEM((rows + 2, WIDE, CHUNK), F32),
                pltpu.VMEM((rows + 2, WIDE, CHUNK), F32),
                pltpu.VMEM((tokens, CHUNK), BF),
                pltpu.VMEM((CHUNK, width + 128), F32),
                pltpu.VMEM((128, CHUNK), F32),
                pltpu.VMEM((tokens, width), F32),
            ],
        ),
        out_shape=[
            jax.ShapeDtypeStruct((tokens, width), BF),
            jax.ShapeDtypeStruct((hid // 2, width + 128), F32),
            jax.ShapeDtypeStruct((hid // 2, width + 128), BF),
        ],
        compiler_params=pltpu.CompilerParams(vmem_limit_bytes=48 * 2**20),
        cost_estimate=pl.CostEstimate(
            flops=16 * 512 * 512 * 2048, bytes_accessed=20 * 2**20, transcendentals=2**20
        ),
    )(core, x, gr, strips, act, slope_c, slope_e, w_expand, w_depthwise, w_project)


def project_kernel(core_ref, mid_ref, gr_ref, mine_out, other_out, full):
    full[...] = dot_tn(mid_ref[...], gr_ref[...])
    split_by_core(core_ref[0], full, mine_out, other_out)


def project_grads(core, mid, gr):
    tokens, hid = mid.shape
    width = gr.shape[1]
    return pl.pallas_call(
        project_kernel,
        name="grad_project",
        grid_spec=pltpu.PrefetchScalarGridSpec(
            num_scalar_prefetch=1,
            grid=(hid // CHUNK,),
            in_specs=[
                pl.BlockSpec((tokens, CHUNK), lambda j, c: (0, j)),
                pl.BlockSpec((tokens, width), lambda j, c: (0, 0)),
            ],
            out_specs=[pl.BlockSpec((CHUNK // 2, width), lambda j, c: (j, 0))] * 2,
            scratch_shapes=[pltpu.VMEM((CHUNK, width), F32)],
        ),
        out_shape=[
            jax.ShapeDtypeStruct((hid // 2, width), F32),
            jax.ShapeDtypeStruct((hid // 2, width), BF),
        ],
        compiler_params=pltpu.CompilerParams(vmem_limit_bytes=48 * 2**20),
        cost_estimate=pl.CostEstimate(
            flops=2 * 512 * 512 * 2048, bytes_accessed=7 * 2**20, transcendentals=0
        ),
    )(core, mid, gr)


def attention_grads_kernel(
    core_ref, arrived_ref, gqkv_ref, att_ref, mine_out, other_out, qkv, outp, half_q, half_o, full
):
    width = att_ref.shape[1]
    qkv[...] = dot_tn(gqkv_ref[...], arrived_ref[:, 0:width])
    outp[...] = dot_tn(arrived_ref[:, width:], att_ref[...])
    nq, no = qkv.shape[0] // 16, outp.shape[0] // 16
    for j in range(8):
        for own in (True, False):
            core = core_ref[0] if own else 1 - core_ref[0]
            half_q[...] = qkv[pl.ds(pl.multiple_of((2 * j + core) * nq, 8), nq), :]
            half_o[...] = outp[pl.ds(pl.multiple_of((2 * j + core) * no, 8), no), :]
            for k in range(8):
                full[16 * k : 16 * k + 12, :] = half_q[12 * k : 12 * k + 12, :]
                full[16 * k + 12 : 16 * k + 16, :] = half_o[4 * k : 4 * k + 4, :]
            at = slice(128 * j, 128 * j + 128)
            if own:
                mine_out[at, :] = full[...]
            else:
                other_out[at, :] = full[...].astype(BF)


def attention_grads(core, arrived, gqkv, attended):
    tokens, width = attended.shape
    vmem = pl.BlockSpec(memory_space=pltpu.VMEM)
    return pl.pallas_call(
        attention_grads_kernel,
        name="attention_grads",
        in_specs=[pl.BlockSpec(memory_space=pltpu.SMEM), vmem, vmem, vmem],
        out_specs=[vmem, vmem],
        out_shape=[
            jax.ShapeDtypeStruct((1024, width), F32),
            jax.ShapeDtypeStruct((1024, width), BF),
        ],
        scratch_shapes=[
            pltpu.VMEM((3 * width, width), F32),
            pltpu.VMEM((width, width), F32),
            pltpu.VMEM((96, width), F32),
            pltpu.VMEM((32, width), F32),
            pltpu.VMEM((128, width), F32),
        ],
        compiler_params=pltpu.CompilerParams(vmem_limit_bytes=48 * 2**20),
        cost_estimate=pl.CostEstimate(
            flops=8 * 512 * 512 * 512, bytes_accessed=8 * 2**20, transcendentals=0
        ),
    )(core, arrived, gqkv, attended)


def add_pair(mine, other):
    got = lax.ppermute(other, AX, other_core())
    return (mine + got.astype(F32)).astype(BF).reshape(64, 16, -1)


def body(block_input, w_expand, w_depthwise, w_project, w_qkv, w_out, grad_out):
    _, rows, cols, width = block_input.shape
    tokens = rows * cols
    core = (lax.axis_index("row") % 2).astype(jnp.int32).reshape(1)
    image = block_input[0]
    x = image.reshape(tokens, width)
    go = grad_out[0].reshape(tokens, width)
    centre, slope_e = expand_block(x, w_expand)
    act, slope_c, mid, resid, send = forward_block(
        x, halo(image, 2), go, centre, w_expand, w_depthwise, w_project
    )
    arrived = across_chips(send.reshape(64, 8, 2 * width)).reshape(tokens, 2 * width)
    back, gqkv, attended = attention_block(arrived, w_qkv, w_out)
    home = across_chips(back.reshape(64, 8, 2 * width)).reshape(tokens, 2 * width)
    attention_pair = add_pair(*attention_grads(core, arrived, gqkv, attended))
    out, gr = residual_block(home, resid, go)
    project_pair = add_pair(*project_grads(core, mid, gr))
    first = jnp.concatenate([project_pair, attention_pair], 1)
    strips = halo(gr.reshape(rows, cols, width), 1)
    strips, first = lax.optimization_barrier((strips, first))
    first = across_chips(first)
    gx, mine, other = backward_block(
        core, x, gr, strips, act, slope_c, slope_e, w_expand, w_depthwise, w_project
    )
    second = add_pair(mine, other)
    second, first = lax.optimization_barrier((second, first))
    second = jnp.sum(across_chips(second).astype(F32), 0)
    first = jnp.sum(first.astype(F32), 0)
    return (
        out.reshape(1, rows, cols, width),
        gx.reshape(1, rows, cols, width),
        second[:, :width].T,
        second[:, width : width + 9].T,
        first[:16].T,
        first[16:28].T,
        first[28:].T,
    )


def solution(mesh):
    tokens = P(None, "row", "col", None)
    split = P(None, AX)
    return jax.shard_map(
        body,
        mesh=mesh,
        in_specs=(tokens, P(), P(), P(), P(), P(), tokens),
        out_specs=(tokens, tokens, split, split, split, split, split),
        check_vma=False,
    )
```

time: 245 us -> 211 us (0.86)
  waiting for transfers between devices: 66.1 us -> 37.7 us
  starting transfers between devices: 39.9 us -> 49.4 us
  local copies, waits for them, and re-layouts: 22.6 us -> 15.9 us
  matrix products: 6.15 us -> 0 us
    all_to_all x3, waiting for transfers between devices: 52.9 us -> 30.3 us  [across_chips(): lax.all_to_all(x, AX, 0, 0, tiled=True, axis_index_groups=device_groups(C...]
    pallas_call x1, Pallas kernels: 25.9 us -> 15.8 us  [forward_block(): pl.pallas_call(forward_kernel, name='mbconv_forward', grid=(hid // CHUNK,...]
    ppermute x8, waiting for transfers between devices: 13.2 us -> 4.75 us  [shift(): return lax.ppermute(x, axis, pairs)]
    pallas_call x1 -> x4, Pallas kernels: 23.2 us -> 31.4 us  [the longest x1 19.6 us: backward_block(): pl.pallas_call(backward_kernel, name='mbconv_backward', grid_spec=pltpu.P...]
    dot_general x3 -> x0, matrix products: 6.15 us -> none  [dot_tn(): lax.dot_general(a, b, (((0,), (0,)), ((), ())), preferred_element_type=F32)]
    concatenate x3 -> x2, local copies, waits for them, and re-layouts: 6.26 us -> 0.15 us  [halo(): sides = jnp.concatenate([right, gap, left], 1)]
    unnamed x31, local copies, waits for them, and re-layouts: 5.43 us -> 11.3 us
    ppermute x8, starting transfers between devices: 15.9 us -> 20.9 us  [shift(): return lax.ppermute(x, axis, pairs)]
  transfers between devices with their start and end apart: 13 -> 14, of which waited for: 8 -> 5; matrix products, arithmetic and copies ran while one was open for 12% -> 5% of each run, Pallas kernels for 0% -> 15%
where the time goes in v2:
time: 211 us; the launch traced here: 210 us
  Pallas kernels  64.2 us (30%)
  starting transfers between devices  49.4 us (23%)
  waiting for transfers between devices  37.7 us (18%)
  blocking collectives  32 us (15%)
  local copies, waits for them, and re-layouts  15.9 us (8%)
  other arithmetic  9.41 us (4%)
    all_to_all x1, blocking collectives, across_chips(): lax.all_to_all(x, AX, 0, 0, tiled=True, axis_index_groups=device_groups(C...  32 us
    all_to_all x3, waiting for transfers between devices, across_chips(): lax.all_to_all(x, AX, 0, 0, tiled=True, axis_index_groups=device_groups(C...  30.3 us
    all_to_all x3, starting transfers between devices, across_chips(): lax.all_to_all(x, AX, 0, 0, tiled=True, axis_index_groups=device_groups(C...  26.7 us
    ppermute x8, starting transfers between devices, shift(): return lax.ppermute(x, axis, pairs)  20.9 us
    pallas_call x1, Pallas kernels, backward_block(): pl.pallas_call(backward_kernel, name='mbconv_backward', grid_spec=pltpu.P...  19.6 us
    pallas_call x1, Pallas kernels, attention_block(): pl.pallas_call(attention_kernel, name='grid_attention', out_shape=[jax.Sh...  16 us
    pallas_call x1, Pallas kernels, forward_block(): pl.pallas_call(forward_kernel, name='mbconv_forward', grid=(hid // CHUNK,...  15.8 us
    unnamed x31, local copies, waits for them, and re-layouts  11.3 us
  transfers between devices with their start and end apart: 14, of which 5 were waited for; matrix products, arithmetic and copies ran while one was open for 5% of the time, Pallas kernels for 15%

profile of v2, /device:TPU:0, one launch (start us, length us, event | category | flops | bytes accessed | tf_op | source)
XLA Modules:
  0.0 209.6 jit_solution(10359186878995181064)
XLA Ops:
  5.2 3.0 %collective-permute-done.1 = bf16[2,32,512]{2,1,0:T(8,128)(2,1)S(1)} collective-permute-done((bf16[2,32,512]{2,1,0:T(8,128)(2,1)S(1)}, bf16[2,32,512]{2,1,0:T(8,128)(2,1)S(1)}, u32[]{:S(2)}, u32[]{:S(2)}) %collective-permute-start.1) | collective-permute-done | bytes 65568 | tf_op jit(solution)/shard_map/ppermute | solution.py:50
  9.7 6.1 %collective-permute-start.3 = (bf16[20,2,512]{2,1,0:T(2,128)(2,1)S(1)}, bf16[20,2,512]{2,1,0:T(2,128)(2,1)S(1)}, u32[]{:S(2)}, u32[]{:S(2)}) collective-permute-start(bf16[20,2,512]{2,1,0:T(2,128)(2,1)S(1)} %pad_maximum_fusion.4), channel_id=1, source_target_pairs={{0,1},{1,2},{2,3},{3,4},{4,5},{5,6},{6,7},{8,9},{9,10},{10,11},{11... | collective-permute-start | bytes 122888 | tf_op jit(solution)/shard_map/ppermute | solution.py:50
  16.8 5.0 %expand.1 = (bf16[512,2048]{1,0:T(8,128)(2,1)S(1)}, bf16[512,2048]{1,0:T(8,128)(2,1)S(1)}) custom-call(bf16[512,512]{1,0:T(8,128)(2,1)S(1)} %bitcast.47, bf16[512,2048]{1,0:T(8,128)(2,1)} %we_ref.5), custom_call_target="tpu_custom_call" | custom-call | flops 8589934592 | bytes 8388608 | tf_op jit(solution)/shard_map/expand/pallas_call | solution.py:135
  24.8 15.8 %mbconv_forward.1 = (bf16[720,2048]{1,0:T(8,128)(2,1)}, bf16[720,2048]{1,0:T(8,128)(2,1)}, bf16[512,2048]{1,0:T(8,128)(2,1)S(1)}, bf16[512,512]{1,0:T(8,128)(2,1)S(1)}, bf16[512,1024]{1,0:T(8,128)(2,1)S(1)}) custom-call(bf16[512,512]{1,0:T(8,128)(2,1)S(1)} %bitcast.48, bf16[288,512]{1,0:T(8,128)(2,1)S(1)} %pad_maximum_fusion.1.strips_ref, ...), custom_call_target="tpu_custom_call" | custom-call | flops 2751463424 | bytes 20971520 | tf_op jit(solution)/shard_map/mbconv_forward/pallas_call | solution.py:200
  40.6 32.0 %all_to_all.20 = bf16[64,8,1024]{2,1,0:T(8,128)(2,1)S(1)} all-to-all(bf16[64,8,1024]{2,1,0:T(8,128)(2,1)S(1)} %bitcast.43), channel_id=1, replica_groups={{0,1,2,3,4,5,6,7,16,17,18,19,20,21,22,23,32,33,34,35,36,37,38,39,48,49,..., dimensions={0} | all-to-all | bytes 2097152 | tf_op jit(solution)/shard_map/all_to_all | solution.py:44
  72.6 16.0 %grid_attention.1 = (bf16[512,1024]{1,0:T(8,128)(2,1)}, bf16[512,1536]{1,0:T(8,128)(2,1)S(1)}, bf16[512,512]{1,0:T(8,128)(2,1)S(1)}) custom-call(bf16[512,1024]{1,0:T(8,128)(2,1)S(1)} %bitcast.41, bf16[512,1536]{1,0:T(8,128)(2,1)} %wq_ref.1, bf16[512,512]{1,0:T(8,128)(2,1)S(1)} %copy-done.3), custom_call_target="tpu_custom_call" | custom-call | flops 2147483648 | bytes 7340032 | tf_op jit(solution)/shard_map/grid_attention/pallas_call | solution.py:297
  90.5 5.8 %all-to-all-start.1 = ((bf16[64,8,1024]{2,1,0:T(8,128)(2,1)}), bf16[64,8,1024]{2,1,0:T(8,128)(2,1)S(1)}, u32[]{:S(2)}, u32[]{:S(2)}) async-start(bf16[64,8,1024]{2,1,0:T(8,128)(2,1)} %bitcast.10), calls=%async_computation.1 | async-start | bytes 2097152 | tf_op jit(solution)/shard_map/all_to_all | solution.py:44
  98.9 3.6 %attention_grads.1 = (f32[1024,512]{1,0:T(8,128)}, bf16[1024,512]{1,0:T(8,128)(2,1)}) custom-call(s32[1]{0:T(128)} %bitcast.13.core_ref, bf16[512,1024]{1,0:T(8,128)(2,1)S(1)} %bitcast.42, bf16[512,1536]{1,0:T(8,128)(2,1)S(1)} %copy-done.6, bf16[512,512]{1,0:T(8,128)(2,1)S(1)} %copy-done.10), custom_call_target="tpu_custom_call" | custom-call | flops 1073741824 | bytes 8388608 | tf_op jit(solution)/shard_map/attention_grads/pallas_call | solution.py:500
  102.6 12.5 %all-to-all-done.1 = bf16[64,8,1024]{2,1,0:T(8,128)(2,1)S(1)} async-done(((bf16[64,8,1024]{2,1,0:T(8,128)(2,1)}), bf16[64,8,1024]{2,1,0:T(8,128)(2,1)S(1)}, u32[]{:S(2)}, u32[]{:S(2)}) %all-to-all-start.1) | async-done | bytes 1048608 | tf_op jit(solution)/shard_map/all_to_all | solution.py:44
  116.8 3.2 %grad_project.1 = (f32[1024,512]{1,0:T(8,128)S(1)}, bf16[1024,512]{1,0:T(8,128)(2,1)S(1)}) custom-call(s32[1]{0:T(128)} %bitcast.13.core_ref, bf16[512,2048]{1,0:T(8,128)(2,1)S(1)} %copy-done.8, bf16[512,512]{1,0:T(8,128)(2,1)S(1)} %get-tuple-element.35.gr_ref), custom_call_target="tpu_custom_call" | custom-call | flops 1073741824 | bytes 7340032 | tf_op jit(solution)/shard_map/grad_project/pallas_call | solution.py:451
  120.2 2.4 %collective-permute-start.4 = (bf16[1,32,512]{2,1,0:T(8,128)(2,1)S(1)}, bf16[1,32,512]{2,1,0:T(8,128)(2,1)S(1)}, u32[]{:S(2)}, u32[]{:S(2)}) collective-permute-start(bf16[1,32,512]{2,1,0:T(8,128)(2,1)S(1)} %get-tuple-element.69), channel_id=1, source_target_pairs={{0,8},{8,16},{16,24},{24,32},{32,40},{40,48},{48,56},{56,64},{64,7... | collective-permute-start | bytes 98312 | tf_op jit(solution)/shard_map/ppermute | solution.py:50
  123.9 1.7 collective-permute-done.5
  127.1 6.1 %collective-permute-start.7 = (bf16[18,1,512]{2,1,0:T(2,128)(2,1)S(1)}, bf16[18,1,512]{2,1,0:T(2,128)(2,1)S(1)}, u32[]{:S(2)}, u32[]{:S(2)}) collective-permute-start(bf16[18,1,512]{2,1,0:T(2,128)(2,1)S(1)} %pad_maximum_fusion.6), channel_id=1, source_target_pairs={{0,1},{1,2},{2,3},{3,4},{4,5},{5,6},{6,7},{8,9},{9,10},{10,11},{11... | collective-permute-start | bytes 55304 | tf_op jit(solution)/shard_map/ppermute | solution.py:50
  133.2 1.7 add_convert_fusion.1
  135.4 1.6 pad_maximum_fusion
  136.9 11.0 %all-to-all-start.2 = ((bf16[64,32,512]{2,1,0:T(8,128)(2,1)}), bf16[64,32,512]{2,1,0:T(8,128)(2,1)}, u32[]{:S(2)}, u32[]{:S(2)}) async-start(bf16[64,32,512]{2,1,0:T(8,128)(2,1)} %pad_maximum_fusion), calls=%async_computation.2 | async-start | bytes 4194304 | tf_op jit(solution)/shard_map/all_to_all | solution.py:44
  147.9 1.6 copy-done.13
  149.5 19.6 %mbconv_backward.1 = (bf16[512,512]{1,0:T(8,128)(2,1)}, f32[1024,640]{1,0:T(8,128)}, bf16[1024,640]{1,0:T(8,128)(2,1)S(1)}) custom-call(s32[1]{0:T(128)} %bitcast.13.core_ref, bf16[512,512]{1,0:T(8,128)(2,1)S(1)} %bitcast.49, bf16[512,512]{1,0:T(8,128)(2,1)S(1)} %get-tuple-element.35.gr_ref, bf16[208,512]{1,0:T(8,128)(2,1)S(1)} %pad_maximum_fusion.2.strips_ref, ...), custom_call_target="tpu_custom_call" | custom-call | flops 8589934592 | bytes 20971520 | tf_op jit(solution)/shard_map/mbconv_backward/pallas_call | solution.py:399
  169.1 1.7 collective-permute-start.10
  170.8 2.7 %collective-permute-done.10 = bf16[1024,640]{1,0:T(8,128)(2,1)S(1)} collective-permute-done((bf16[1024,640]{1,0:T(8,128)(2,1)S(1)}, bf16[1024,640]{1,0:T(8,128)(2,1)S(1)}, u32[]{:S(2)}, u32[]{:S(2)}) %collective-permute-start.10) | collective-permute-done | bytes 1310752 | tf_op jit(solution)/shard_map/ppermute | solution.py:524
  173.5 3.2 %add_convert_fusion = bf16[1024,640]{1,0:T(8,128)(2,1)} fusion(f32[1024,640]{1,0:T(8,128)} %get-tuple-element.48, bf16[1024,640]{1,0:T(8,128)(2,1)S(1)} %collective-permute-done.10), kind=kLoop, calls=%fused_computation.2 | loop fusion | flops 1966080 | bytes 5242880 | tf_op jit(solution)/shard_map/convert_element_type | solution.py:525
  176.6 9.9 %all-to-all-start.3 = ((bf16[64,16,640]{2,1,0:T(8,128)(2,1)}), bf16[64,16,640]{2,1,0:T(8,128)(2,1)S(1)}, u32[]{:S(2)}, u32[]{:S(2)}) async-start(bf16[64,16,640]{2,1,0:T(8,128)(2,1)} %bitcast.23), calls=%async_computation.3 | async-start | bytes 2621440 | tf_op jit(solution)/shard_map/all_to_all | solution.py:44
  186.5 1.9 convert_reduce_fusion
  190.3 17.8 %all-to-all-done.3 = bf16[64,16,640]{2,1,0:T(8,128)(2,1)S(1)} async-done(((bf16[64,16,640]{2,1,0:T(8,128)(2,1)}), bf16[64,16,640]{2,1,0:T(8,128)(2,1)S(1)}, u32[]{:S(2)}, u32[]{:S(2)}) %all-to-all-start.3) | async-done | bytes 1310752 | tf_op jit(solution)/shard_map/all_to_all | solution.py:44
  (74 shorter events, 22.9 us)
Async XLA Ops:
  1.5 3.6 %collective-permute-start = (bf16[2,32,512]{2,1,0:T(8,128)(2,1)S(1)}, bf16[2,32,512]{2,1,0:T(8,128)(2,1)S(1)}, u32[]{:S(2)}, u32[]{:S(2)}) collective-permute-start(bf16[2,32,512]{2,1,0:T(8,128)(2,1)S(1)} %get-tuple-element.73), channel_id=1, source_target_pairs={{0,8},{8,16},{16,24},{24,32},{32,40},{40,48},{48,56},{56,64},{64,7... | collective-permute-start | bytes 196616 | tf_op jit(solution)/shard_map/ppermute | solution.py:50
  2.8 5.4 %collective-permute-start.1 = (bf16[2,32,512]{2,1,0:T(8,128)(2,1)S(1)}, bf16[2,32,512]{2,1,0:T(8,128)(2,1)S(1)}, u32[]{:S(2)}, u32[]{:S(2)}) collective-permute-start(bf16[2,32,512]{2,1,0:T(8,128)(2,1)S(1)} %get-tuple-element.74), channel_id=1, source_target_pairs={{8,0},{16,8},{24,16},{32,24},{40,32},{48,40},{56,48},{64,56},{72,6... | collective-permute-start | bytes 196616 | tf_op jit(solution)/shard_map/ppermute | solution.py:50
  8.3 16.3 %collective-permute-start.2 = (bf16[20,2,512]{2,1,0:T(2,128)(2,1)S(1)}, bf16[20,2,512]{2,1,0:T(2,128)(2,1)S(1)}, u32[]{:S(2)}, u32[]{:S(2)}) collective-permute-start(bf16[20,2,512]{2,1,0:T(2,128)(2,1)S(1)} %pad_maximum_fusion.3), channel_id=1, source_target_pairs={{1,0},{2,1},{3,2},{4,3},{5,4},{6,5},{7,6},{9,8},{10,9},{11,10},{12... | collective-permute-start | bytes 122888 | tf_op jit(solution)/shard_map/ppermute | solution.py:50
  9.7 15.0 %collective-permute-start.3 = (bf16[20,2,512]{2,1,0:T(2,128)(2,1)S(1)}, bf16[20,2,512]{2,1,0:T(2,128)(2,1)S(1)}, u32[]{:S(2)}, u32[]{:S(2)}) collective-permute-start(bf16[20,2,512]{2,1,0:T(2,128)(2,1)S(1)} %pad_maximum_fusion.4), channel_id=1, source_target_pairs={{0,1},{1,2},{2,3},{3,4},{4,5},{5,6},{6,7},{8,9},{9,10},{10,11},{11... | collective-permute-start | bytes 122888 | tf_op jit(solution)/shard_map/ppermute | solution.py:50
  16.8 8.0 %copy-start = (bf16[1,16,32,512]{3,2,1,0:T(8,128)(2,1)S(1)}, bf16[1,16,32,512]{3,2,1,0:T(8,128)(2,1)}, u32[]{:S(2)}) copy-start(bf16[1,16,32,512]{3,2,1,0:T(8,128)(2,1)} %param.13) | copy-start | bytes 1572868
  16.8 8.0 %copy-start.4 = (bf16[9,2048]{1,0:T(8,128)(2,1)S(1)}, bf16[9,2048]{1,0:T(8,128)(2,1)}, u32[]{:S(2)}) copy-start(bf16[9,2048]{1,0:T(8,128)(2,1)} %wd_ref.3) | copy-start | bytes 110596
  21.8 1.4 copy-start.11
  40.6 32.0 %copy-start.7 = (bf16[512,2048]{1,0:T(8,128)(2,1)}, bf16[512,2048]{1,0:T(8,128)(2,1)S(1)}, u32[]{:S(2)}) copy-start(bf16[512,2048]{1,0:T(8,128)(2,1)S(1)} %get-tuple-element.36.mid_ref) | copy-start | bytes 6291460
  40.6 32.0 %copy-start.3 = (bf16[512,512]{1,0:T(8,128)(2,1)S(1)}, bf16[512,512]{1,0:T(8,128)(2,1)}, u32[]{:S(2)}) copy-start(bf16[512,512]{1,0:T(8,128)(2,1)} %wo_ref.1) | copy-start | bytes 1572868
  90.5 24.5 %all-to-all-start.1 = ((bf16[64,8,1024]{2,1,0:T(8,128)(2,1)}), bf16[64,8,1024]{2,1,0:T(8,128)(2,1)S(1)}, u32[]{:S(2)}, u32[]{:S(2)}) async-start(bf16[64,8,1024]{2,1,0:T(8,128)(2,1)} %bitcast.10), calls=%async_computation.1 | async-start | bytes 2097152 | tf_op jit(solution)/shard_map/all_to_all | solution.py:44
  96.5 1.4 copy-start.6
  102.5 30.6 %collective-permute-start.9 = (bf16[1024,512]{1,0:T(8,128)(2,1)}, bf16[1024,512]{1,0:T(8,128)(2,1)}, u32[]{:S(2)}, u32[]{:S(2)}) collective-permute-start(bf16[1024,512]{1,0:T(8,128)(2,1)} %get-tuple-element.42), channel_id=1, source_target_pairs={{0,8},{1,9},{2,10},{3,11},{4,12},{5,13},{6,14},{7,15},{8,0},{9,1},... | collective-permute-start | bytes 3145736 | tf_op jit(solution)/shard_map/ppermute | solution.py:524
  115.1 1.8 copy-start.8
  116.8 16.3 %copy-start.14 = (f32[1024,512]{1,0:T(8,128)S(1)}, f32[1024,512]{1,0:T(8,128)}, u32[]{:S(2)}) copy-start(f32[1024,512]{1,0:T(8,128)} %get-tuple-element.41) | copy-start | bytes 6291460
  120.0 14.9 %collective-permute-start.8 = (bf16[1024,512]{1,0:T(8,128)(2,1)S(1)}, bf16[1024,512]{1,0:T(8,128)(2,1)S(1)}, u32[]{:S(2)}, u32[]{:S(2)}) collective-permute-start(bf16[1024,512]{1,0:T(8,128)(2,1)S(1)} %get-tuple-element.38), channel_id=1, source_target_pairs={{0,8},{1,9},{2,10},{3,11},{4,12},{5,13},{6,14},{7,15},{8,0},{9,1},... | collective-permute-start | bytes 3145736 | tf_op jit(solution)/shard_map/ppermute | solution.py:524
  120.2 3.8 %collective-permute-start.4 = (bf16[1,32,512]{2,1,0:T(8,128)(2,1)S(1)}, bf16[1,32,512]{2,1,0:T(8,128)(2,1)S(1)}, u32[]{:S(2)}, u32[]{:S(2)}) collective-permute-start(bf16[1,32,512]{2,1,0:T(8,128)(2,1)S(1)} %get-tuple-element.69), channel_id=1, source_target_pairs={{0,8},{8,16},{16,24},{24,32},{32,40},{40,48},{48,56},{56,64},{64,7... | collective-permute-start | bytes 98312 | tf_op jit(solution)/shard_map/ppermute | solution.py:50
  122.5 3.1 %collective-permute-start.5 = (bf16[1,32,512]{2,1,0:T(8,128)(2,1)S(1)}, bf16[1,32,512]{2,1,0:T(8,128)(2,1)S(1)}, u32[]{:S(2)}, u32[]{:S(2)}) collective-permute-start(bf16[1,32,512]{2,1,0:T(8,128)(2,1)S(1)} %get-tuple-element.70), channel_id=1, source_target_pairs={{8,0},{16,8},{24,16},{32,24},{40,32},{48,40},{56,48},{64,56},{72,6... | collective-permute-start | bytes 98312 | tf_op jit(solution)/shard_map/ppermute | solution.py:50
  125.7 9.1 %collective-permute-start.6 = (bf16[18,1,512]{2,1,0:T(2,128)(2,1)S(1)}, bf16[18,1,512]{2,1,0:T(2,128)(2,1)S(1)}, u32[]{:S(2)}, u32[]{:S(2)}) collective-permute-start(bf16[18,1,512]{2,1,0:T(2,128)(2,1)S(1)} %pad_maximum_fusion.5), channel_id=1, source_target_pairs={{1,0},{2,1},{3,2},{4,3},{5,4},{6,5},{7,6},{9,8},{10,9},{11,10},{12... | collective-permute-start | bytes 55304 | tf_op jit(solution)/shard_map/ppermute | solution.py:50
  127.1 7.8 %collective-permute-start.7 = (bf16[18,1,512]{2,1,0:T(2,128)(2,1)S(1)}, bf16[18,1,512]{2,1,0:T(2,128)(2,1)S(1)}, u32[]{:S(2)}, u32[]{:S(2)}) collective-permute-start(bf16[18,1,512]{2,1,0:T(2,128)(2,1)S(1)} %pad_maximum_fusion.6), channel_id=1, source_target_pairs={{0,1},{1,2},{2,3},{3,4},{4,5},{5,6},{6,7},{8,9},{9,10},{10,11},{11... | collective-permute-start | bytes 55304 | tf_op jit(solution)/shard_map/ppermute | solution.py:50
  136.9 11.0 %copy-start.2 = (bf16[1,16,32,512]{3,2,1,0:T(8,128)(2,1)S(1)}, bf16[1,16,32,512]{3,2,1,0:T(8,128)(2,1)}, u32[]{:S(2)}) copy-start(bf16[1,16,32,512]{3,2,1,0:T(8,128)(2,1)} %param.7) | copy-start | bytes 1572868
  136.9 39.7 %all-to-all-start.2 = ((bf16[64,32,512]{2,1,0:T(8,128)(2,1)}), bf16[64,32,512]{2,1,0:T(8,128)(2,1)}, u32[]{:S(2)}, u32[]{:S(2)}) async-start(bf16[64,32,512]{2,1,0:T(8,128)(2,1)} %pad_maximum_fusion), calls=%async_computation.2 | async-start | bytes 4194304 | tf_op jit(solution)/shard_map/all_to_all | solution.py:44
  147.9 1.6 copy-start.13
  169.1 4.3 %collective-permute-start.10 = (bf16[1024,640]{1,0:T(8,128)(2,1)S(1)}, bf16[1024,640]{1,0:T(8,128)(2,1)S(1)}, u32[]{:S(2)}, u32[]{:S(2)}) collective-permute-start(bf16[1024,640]{1,0:T(8,128)(2,1)S(1)} %get-tuple-element.49), channel_id=1, source_target_pairs={{0,8},{1,9},{2,10},{3,11},{4,12},{5,13},{6,14},{7,15},{8,0},{9,1},... | collective-permute-start | bytes 3932168 | tf_op jit(solution)/shard_map/ppermute | solution.py:524
  176.6 31.4 %all-to-all-start.3 = ((bf16[64,16,640]{2,1,0:T(8,128)(2,1)}), bf16[64,16,640]{2,1,0:T(8,128)(2,1)S(1)}, u32[]{:S(2)}, u32[]{:S(2)}) async-start(bf16[64,16,640]{2,1,0:T(8,128)(2,1)} %bitcast.23), calls=%async_computation.3 | async-start | bytes 2621440 | tf_op jit(solution)/shard_map/all_to_all | solution.py:44
  (5 other events, 5.4 us)

commit v3 on v2

--- a/solution.py
+++ b/solution.py
@@ -16,6 +16,7 @@
 AX = ("row", "col")
 WIDE = 40
 CHUNK = 256
+MIB = 2**20
 
 SIZES = dict(y_lo=2, z=4, core=2, x=4, y_hi=2)
 STRIDES = dict(y_lo=64, z=16, core=8, x=2, y_hi=1)
@@ -50,10 +51,11 @@
     return lax.ppermute(x, axis, pairs)
 
 
-def halo(x, width):
+def halo(x, width, ahead):
     rows, cols, chans = x.shape
     above = shift(x[rows - width :], "row", 1)
     below = shift(x[:width], "row", -1)
+    above, below, _ = lax.optimization_barrier((above, below, ahead))
     to_right = jnp.concatenate(
         [above[:, cols - width :], x[:, cols - width :], below[:, cols - width :]], 0
     )
@@ -67,9 +69,10 @@
 
 
 def place(wide, centre, strips, width, rows, cols):
-    lanes = centre.shape[-1]
+    lanes = strips.shape[-1]
     n = width * cols
-    wide[width : width + rows, 0:cols, :] = centre.reshape(rows, cols, lanes)
+    if centre is not None:
+        wide[width : width + rows, 0:cols, :] = centre.reshape(rows, cols, lanes)
     wide[0:width, 0:cols, :] = strips[0:n].reshape(width, cols, lanes)
     wide[width + rows :, 0:cols, :] = strips[n : 2 * n].reshape(width, cols, lanes)
     wide[:, cols:, :] = strips[2 * n :].reshape(rows + 2 * width, WIDE - cols, lanes)
@@ -94,11 +97,19 @@
 A1 = A0 * 0.044715
 
 
-def gelu_parts(x):
+def gelu_half(x):
     inner = A0 + A1 * (x * x)
-    half = 0.5 + 0.5 * jnp.tanh(x * inner)
+    return inner, 0.5 + 0.5 * jnp.tanh(x * inner)
+
+
+def gelu(x):
+    return x * gelu_half(x)[1]
+
+
+def gelu_slope(x):
+    inner, half = gelu_half(x)
     value = x * half
-    return value, half + (value - value * half) * (6.0 * inner - 4.0 * A0)
+    return half + (value - value * half) * (6.0 * inner - 4.0 * A0)
 
 
 def dot(a, b):
@@ -113,46 +124,49 @@
     return lax.dot_general(a, b, (((0,), (0,)), ((), ())), preferred_element_type=F32)
 
 
+def in_hbm(*arrays):
+    return [pltpu.with_memory_space_constraint(a, pltpu.HBM) for a in arrays]
+
+
 def roll(x, by):
     return pltpu.roll(x, by % x.shape[0], 0)
 
 
-def expand_kernel(x_ref, we_ref, act_out, slope_out, normed):
+def expand_kernel(x_ref, we_ref, act_out, normed):
     @pl.when(pl.program_id(0) == 0)
     def _():
         normed[...] = normalize(x_ref[...].astype(F32))[0].astype(BF)
 
     for tile in range(0, x_ref.shape[0], 128):
-        value, slope = gelu_parts(dot(normed[tile : tile + 128, :], we_ref[...]))
-        act_out[tile : tile + 128, :] = value.astype(BF)
-        slope_out[tile : tile + 128, :] = slope.astype(BF)
-
-
-def expand_block(x, w_expand):
+        at = slice(tile, tile + 128)
+        act_out[at, :] = gelu(dot(normed[at, :], we_ref[...])).astype(BF)
+
+
+def expand_block(x, w_expand, part, parts):
     tokens, width = x.shape
-    hid = w_expand.shape[1]
     lanes = 512
+    steps = w_expand.shape[1] // lanes // parts
     return pl.pallas_call(
         expand_kernel,
         name="expand",
-        grid=(hid // lanes,),
+        grid=(steps,),
         in_specs=[
             pl.BlockSpec((tokens, width), lambda j: (0, 0)),
-            pl.BlockSpec((width, lanes), lambda j: (0, j)),
-        ],
-        out_specs=[pl.BlockSpec((tokens, lanes), lambda j: (0, j))] * 2,
-        out_shape=[jax.ShapeDtypeStruct((tokens, hid), BF)] * 2,
+            pl.BlockSpec((width, lanes), lambda j: (0, j + part * steps)),
+        ],
+        out_specs=pl.BlockSpec((tokens, lanes), lambda j: (0, j)),
+        out_shape=jax.ShapeDtypeStruct((tokens, steps * lanes), BF),
         scratch_shapes=[pltpu.VMEM((tokens, width), BF)],
-        compiler_params=pltpu.CompilerParams(vmem_limit_bytes=48 * 2**20),
+        compiler_params=pltpu.CompilerParams(vmem_limit_bytes=8 * MIB),
         cost_estimate=pl.CostEstimate(
-            flops=16 * 512 * 512 * 2048, bytes_accessed=8 * 2**20, transcendentals=2**20
-        ),
-    )(x, w_expand)
+            flops=8 * 512 * 512 * 2048, bytes_accessed=3 * 2**20, transcendentals=2**19
+        ),
+    )(*in_hbm(x, w_expand))
 
 
 def forward_kernel(
-    x_ref, strips_ref, go_ref, act_ref, we_ref, wd_ref, wp_ref,
-    act_out, slope_out, mid_out, resid_out, send_out,
+    x_ref, strips_ref, go_ref, act0_ref, act1_ref, we_ref, wd_ref, wp_ref,
+    mid_out, resid_out, send_out,
     normed, act, acc,
 ):
     step = pl.program_id(0)
@@ -160,11 +174,94 @@
 
     @pl.when(step == 0)
     def _():
-        normed[...] = normalize(strips_ref[...].astype(F32))[0].astype(BF)
+        every = normalize(strips_ref[...].astype(F32))[0]
+        sides = 4 * cols + 8
+        near = [every[cols : 3 * cols], every[sides : sides + 8 * (rows + 2)]]
+        normed[...] = jnp.concatenate(near, 0).astype(BF)
         acc[...] = jnp.zeros(acc.shape, F32)
 
-    strips = jax.nn.gelu(dot(normed[...], we_ref[...])).astype(BF).astype(F32)
-    place(act, act_ref[...].astype(F32), strips, 2, rows, cols)
+    strips = gelu(dot(normed[...], we_ref[...])).astype(BF).astype(F32)
+    centre = jnp.where(step < pl.num_programs(0) // 2, act0_ref[...], act1_ref[...])
+    place(act, centre.astype(F32), strips, 1, rows, cols)
+    for lo in range(0, CHUNK, 128):
+        lanes = slice(lo, lo + 128)
+        taps = [wd_ref[k : k + 1, lanes].astype(F32) for k in range(9)]
+        lines = [act[0, :, lanes], act[1, :, lanes]]
+        for r in range(rows):
+            lines = lines[-2:] + [act[r + 2, :, lanes]]
+            sums = [sum(lines[i] * taps[3 * i + j] for i in range(3)) for j in range(3)]
+            conv = sums[1] + roll(sums[0], 1) + roll(sums[2], -1)
+            mid_out[r * cols : (r + 1) * cols, lanes] = gelu(conv[0:cols]).astype(BF)
+    acc[...] += dot(mid_out[...], wp_ref[...])
+
+    @pl.when(step == pl.num_programs(0) - 1)
+    def _():
+        resid = (x_ref[...].astype(F32) + acc[...]).astype(BF)
+        resid_out[...] = resid
+        width = resid.shape[1]
+        send_out[:, 0:width] = normalize(resid.astype(F32))[0].astype(BF)
+        send_out[:, width:] = go_ref[...]
+
+
+def forward_block(x, strips, go, act0, act1, w_expand, w_depthwise, w_project):
+    tokens, width = x.shape
+    hid = w_expand.shape[1]
+    rows, cols = 16, 32
+    steps = hid // CHUNK
+    whole = lambda a: pl.BlockSpec(a.shape, lambda j: (0,) * a.ndim)
+    return pl.pallas_call(
+        forward_kernel,
+        name="mbconv_forward",
+        grid=(steps,),
+        in_specs=[
+            whole(x), whole(strips), whole(go),
+            pl.BlockSpec((tokens, CHUNK), lambda j: (0, jnp.minimum(j, steps // 2 - 1))),
+            pl.BlockSpec((tokens, CHUNK), lambda j: (0, jnp.maximum(j - steps // 2, 0))),
+            pl.BlockSpec((width, CHUNK), lambda j: (0, j)),
+            pl.BlockSpec((9, CHUNK), lambda j: (0, j)),
+            pl.BlockSpec((CHUNK, width), lambda j: (j, 0)),
+        ],
+        out_specs=[
+            pl.BlockSpec((tokens, CHUNK), lambda j: (0, j)),
+            pl.BlockSpec((tokens, width), lambda j: (0, 0)),
+            pl.BlockSpec((tokens, 2 * width), lambda j: (0, 0)),
+        ],
+        out_shape=[
+            pltpu.HBM((tokens, hid), BF),
+            pltpu.HBM((tokens, width), BF),
+            pltpu.HBM((tokens, 2 * width), BF),
+        ],
+        scratch_shapes=[
+            pltpu.VMEM((2 * cols + 8 * (rows + 2), width), BF),
+            pltpu.VMEM((rows + 2, WIDE, CHUNK), F32),
+            pltpu.VMEM((tokens, width), F32),
+        ],
+        compiler_params=pltpu.CompilerParams(vmem_limit_bytes=14 * MIB),
+        cost_estimate=pl.CostEstimate(
+            flops=2 * 700 * 512 * 2048, bytes_accessed=10 * 2**20, transcendentals=2**20
+        ),
+    )(*in_hbm(x), strips, *in_hbm(go), act0, act1, *in_hbm(w_expand, w_depthwise, w_project))
+
+
+def slopes_kernel(
+    x_ref, strips_ref, we_ref, wd_ref, act_out, slope_c_out, slope_e_out, normed, normed_s, act
+):
+    rows, cols = 16, 32
+
+    @pl.when(pl.program_id(0) == 0)
+    def _():
+        normed[...] = normalize(x_ref[...].astype(F32))[0].astype(BF)
+        normed_s[...] = normalize(strips_ref[...].astype(F32))[0].astype(BF)
+
+    for tile in range(0, x_ref.shape[0], 128):
+        at = slice(tile, tile + 128)
+        pre = dot(normed[at, :], we_ref[...])
+        slope_e_out[at, :] = gelu_slope(pre).astype(BF)
+        act[2 + tile // cols : 2 + (tile + 128) // cols, 0:cols, :] = (
+            gelu(pre).astype(BF).astype(F32).reshape(128 // cols, cols, CHUNK)
+        )
+    strips = gelu(dot(normed_s[...], we_ref[...])).astype(BF).astype(F32)
+    place(act, None, strips, 2, rows, cols)
     act_out[...] = act[1 : rows + 3].reshape(act_out.shape).astype(BF)
     for lo in range(0, CHUNK, 128):
         lanes = slice(lo, lo + 128)
@@ -174,64 +271,48 @@
         for r in range(rows + 2):
             lines = lines[-2:] + [act[r + 2, :, lanes]]
             sums = [sum(lines[i] * taps[3 * i + j] for i in range(3)) for j in range(3)]
-            value, slope = gelu_parts(sums[1] + roll(sums[0], 1) + roll(sums[2], -1))
-            if 1 <= r <= rows:
-                mid_out[(r - 1) * cols : r * cols, lanes] = value[0:cols].astype(BF)
+            slope = gelu_slope(sums[1] + roll(sums[0], 1) + roll(sums[2], -1))
             if r % 2:
                 pair = jnp.concatenate([held, slope], 0).astype(BF)
-                slope_out[(r - 1) * WIDE : (r + 1) * WIDE, lanes] = pair
+                slope_c_out[(r - 1) * WIDE : (r + 1) * WIDE, lanes] = pair
             held = slope
-    acc[...] += dot(mid_out[...], wp_ref[...])
-
-    @pl.when(step == pl.num_programs(0) - 1)
-    def _():
-        resid = (x_ref[...].astype(F32) + acc[...]).astype(BF)
-        resid_out[...] = resid
-        width = resid.shape[1]
-        send_out[:, 0:width] = normalize(resid.astype(F32))[0].astype(BF)
-        send_out[:, width:] = go_ref[...]
-
-
-def forward_block(x, strips, go, act, w_expand, w_depthwise, w_project):
+
+
+def slopes_block(x, strips, w_expand, w_depthwise):
     tokens, width = x.shape
     hid = w_expand.shape[1]
     rows, cols = 16, 32
+    wide = (rows + 2) * WIDE
     whole = lambda a: pl.BlockSpec(a.shape, lambda j: (0,) * a.ndim)
     return pl.pallas_call(
-        forward_kernel,
-        name="mbconv_forward",
+        slopes_kernel,
+        name="gelu_slopes",
         grid=(hid // CHUNK,),
         in_specs=[
-            whole(x), whole(strips), whole(go),
-            pl.BlockSpec((tokens, CHUNK), lambda j: (0, j)),
+            whole(x), whole(strips),
             pl.BlockSpec((width, CHUNK), lambda j: (0, j)),
             pl.BlockSpec((9, CHUNK), lambda j: (0, j)),
-            pl.BlockSpec((CHUNK, width), lambda j: (j, 0)),
         ],
         out_specs=[
-            pl.BlockSpec(((rows + 2) * WIDE, CHUNK), lambda j: (0, j)),
-            pl.BlockSpec(((rows + 2) * WIDE, CHUNK), lambda j: (0, j)),
+            pl.BlockSpec((wide, CHUNK), lambda j: (0, j)),
+            pl.BlockSpec((wide, CHUNK), lambda j: (0, j)),
             pl.BlockSpec((tokens, CHUNK), lambda j: (0, j)),
-            pl.BlockSpec((tokens, width), lambda j: (0, 0)),
-            pl.BlockSpec((tokens, 2 * width), lambda j: (0, 0)),
         ],
         out_shape=[
-            jax.ShapeDtypeStruct(((rows + 2) * WIDE, hid), BF),
-            jax.ShapeDtypeStruct(((rows + 2) * WIDE, hid), BF),
-            jax.ShapeDtypeStruct((tokens, hid), BF),
-            jax.ShapeDtypeStruct((tokens, width), BF),
-            jax.ShapeDtypeStruct((tokens, 2 * width), BF),
+            pltpu.HBM((wide, hid), BF),
+            pltpu.HBM((wide, hid), BF),
+            pltpu.HBM((tokens, hid), BF),
         ],
         scratch_shapes=[
+            pltpu.VMEM((tokens, width), BF),
             pltpu.VMEM(strips.shape, BF),
             pltpu.VMEM((rows + 4, WIDE, CHUNK), F32),
-            pltpu.VMEM((tokens, width), F32),
-        ],
-        compiler_params=pltpu.CompilerParams(vmem_limit_bytes=48 * 2**20),
+        ],
+        compiler_params=pltpu.CompilerParams(vmem_limit_bytes=16 * MIB),
         cost_estimate=pl.CostEstimate(
-            flops=2 * (800 + 512) * 512 * 2048, bytes_accessed=20 * 2**20, transcendentals=3 * 2**20
-        ),
-    )(x, strips, go, act, w_expand, w_depthwise, w_project)
+            flops=2 * 10**10, bytes_accessed=12 * 2**20, transcendentals=3 * 2**20
+        ),
+    )(*in_hbm(x), strips, *in_hbm(w_expand, w_depthwise))
 
 
 def attention_kernel(in_ref, wq_ref, wo_ref, send_out, gq_out, att_out, qkv, gatt, att, gq):
@@ -298,9 +379,9 @@
         attention_kernel,
         name="grid_attention",
         out_shape=[
-            jax.ShapeDtypeStruct((tokens, 2 * width), BF),
-            jax.ShapeDtypeStruct((tokens, 3 * width), BF),
-            jax.ShapeDtypeStruct((tokens, width), BF),
+            pltpu.HBM((tokens, 2 * width), BF),
+            pltpu.HBM((tokens, 3 * width), BF),
+            pltpu.HBM((tokens, width), BF),
         ],
         scratch_shapes=[
             pltpu.VMEM((3 * width // 128, tokens, 128), F32),
@@ -308,11 +389,11 @@
             pltpu.VMEM((width // 128, tokens, 128), F32),
             pltpu.VMEM((3 * width // 128, tokens, 128), F32),
         ],
-        compiler_params=pltpu.CompilerParams(vmem_limit_bytes=48 * 2**20),
+        compiler_params=pltpu.CompilerParams(vmem_limit_bytes=22 * MIB),
         cost_estimate=pl.CostEstimate(
             flops=2 * 512 * 512 * 512 * 8, bytes_accessed=7 * 2**20, transcendentals=2**20
         ),
-    )(arrived, w_qkv, w_out)
+    )(arrived, *in_hbm(w_qkv, w_out))
 
 
 def residual_kernel(home_ref, resid_ref, go_ref, out_ref, gr_ref):
@@ -328,21 +409,24 @@
         residual_kernel,
         name="residual",
         out_shape=[jax.ShapeDtypeStruct(resid.shape, BF)] * 2,
-        compiler_params=pltpu.CompilerParams(vmem_limit_bytes=48 * 2**20),
-    )(home, resid, go)
+        compiler_params=pltpu.CompilerParams(vmem_limit_bytes=8 * MIB),
+    )(home, *in_hbm(resid, go))
 
 
 def split_by_core(core, full, mine_out, other_out):
-    half = full.shape[0] // 2
-    own = pl.multiple_of(core * half, half)
-    mine_out[...] = full[pl.ds(own, half), :]
-    other_out[...] = full[pl.ds(pl.multiple_of(half - own, half), half), :].astype(BF)
+    half = 128
+    for j in range(full.shape[0] // (2 * half)):
+        at = slice(j * half, (j + 1) * half)
+        own = pl.multiple_of((2 * j + core) * half, half)
+        other = pl.multiple_of((2 * j + 1 - core) * half, half)
+        mine_out[at, :] = full[pl.ds(own, half), :]
+        other_out[at, :] = full[pl.ds(other, half), :].astype(BF)
 
 
 def backward_kernel(
-    core_ref, x_ref, gr_ref, strips_ref, act_ref, slope_c_ref, slope_e_ref, we_ref, wd_ref, wp_ref,
-    gx_out, mine_out, other_out,
-    wide, grad_wide, normed, gmid, act, gpre, full, taps_t, acc,
+    core_ref, x_ref, gr_ref, strips_ref, act_ref, slope_c_ref, slope_e_ref, wd_ref, wp_ref,
+    gpre, mine_out, other_out,
+    wide, grad_wide, normed, gmid, act, full, taps_t,
 ):
     step = pl.program_id(0)
     rows, cols = 16, 32
@@ -353,7 +437,6 @@
         place(wide, gr_ref[...].astype(F32), strips_ref[...].astype(F32), 1, rows, cols)
         grad_wide[...] = wide[...].reshape(grad_wide.shape).astype(BF)
         normed[...] = normalize(x_ref[...].astype(F32))[0].astype(BF)
-        acc[...] = jnp.zeros(acc.shape, F32)
         taps_t[...] = jnp.zeros(taps_t.shape, F32)
 
     gm = dot_nt(grad_wide[...], wp_ref[...]) * slope_c_ref[...].astype(F32)
@@ -383,17 +466,11 @@
     full[:, 0:width] = dot_tn(gpre[...], normed[...])
     full[:, width:] = taps_t[...].T
     split_by_core(core_ref[0], full, mine_out, other_out)
-    acc[...] += dot_nt(gpre[...], we_ref[...])
-
-    @pl.when(step == pl.num_programs(0) - 1)
-    def _():
-        back = normalize_back(x_ref[...].astype(F32), acc[...])
-        gx_out[...] = (gr_ref[...].astype(F32) + back).astype(BF)
-
-
-def backward_block(core, x, gr, strips, act, slope_c, slope_e, w_expand, w_depthwise, w_project):
+
+
+def backward_block(core, x, gr, strips, act, slope_c, slope_e, w_depthwise, w_project):
     tokens, width = x.shape
-    hid = w_expand.shape[1]
+    hid = w_project.shape[0]
     rows, cols = 16, 32
     whole = lambda a: pl.BlockSpec(a.shape, lambda j, c: (0,) * a.ndim)
     return pl.pallas_call(
@@ -407,12 +484,11 @@
                 pl.BlockSpec(((rows + 2) * WIDE, CHUNK), lambda j, c: (0, j)),
                 pl.BlockSpec(((rows + 2) * WIDE, CHUNK), lambda j, c: (0, j)),
                 pl.BlockSpec((tokens, CHUNK), lambda j, c: (0, j)),
-                pl.BlockSpec((width, CHUNK), lambda j, c: (0, j)),
                 pl.BlockSpec((9, CHUNK), lambda j, c: (0, j)),
                 pl.BlockSpec((CHUNK, width), lambda j, c: (j, 0)),
             ],
             out_specs=[
-                pl.BlockSpec((tokens, width), lambda j, c: (0, 0)),
+                pl.BlockSpec((tokens, CHUNK), lambda j, c: (0, j)),
                 pl.BlockSpec((CHUNK // 2, width + 128), lambda j, c: (j, 0)),
                 pl.BlockSpec((CHUNK // 2, width + 128), lambda j, c: (j, 0)),
             ],
@@ -422,22 +498,70 @@
                 pltpu.VMEM((tokens, width), BF),
                 pltpu.VMEM((rows + 2, WIDE, CHUNK), F32),
                 pltpu.VMEM((rows + 2, WIDE, CHUNK), F32),
-                pltpu.VMEM((tokens, CHUNK), BF),
                 pltpu.VMEM((CHUNK, width + 128), F32),
                 pltpu.VMEM((128, CHUNK), F32),
-                pltpu.VMEM((tokens, width), F32),
             ],
         ),
         out_shape=[
-            jax.ShapeDtypeStruct((tokens, width), BF),
+            pltpu.HBM((tokens, hid), BF),
             jax.ShapeDtypeStruct((hid // 2, width + 128), F32),
             jax.ShapeDtypeStruct((hid // 2, width + 128), BF),
         ],
-        compiler_params=pltpu.CompilerParams(vmem_limit_bytes=48 * 2**20),
+        compiler_params=pltpu.CompilerParams(vmem_limit_bytes=18 * MIB),
         cost_estimate=pl.CostEstimate(
             flops=16 * 512 * 512 * 2048, bytes_accessed=20 * 2**20, transcendentals=2**20
         ),
-    )(core, x, gr, strips, act, slope_c, slope_e, w_expand, w_depthwise, w_project)
+    )(core, *in_hbm(x), gr, strips, *in_hbm(act, slope_c, slope_e, w_depthwise, w_project))
+
+
+def input_kernel(gpre_ref, we_ref, x_ref, gr_ref, gx_out):
+    back = normalize_back(x_ref[...].astype(F32), dot_nt(gpre_ref[...], we_ref[...]))
+    gx_out[...] = (gr_ref[...].astype(F32) + back).astype(BF)
+
+
+def input_grads(gpre, w_expand, x, gr):
+    tokens, width = x.shape
+    hid = w_expand.shape[1]
+    tile = 128
+    return pl.pallas_call(
+        input_kernel,
+        name="grad_input",
+        grid=(tokens // tile,),
+        in_specs=[
+            pl.BlockSpec((tile, hid), lambda i: (i, 0)),
+            pl.BlockSpec((width, hid), lambda i: (0, 0)),
+            pl.BlockSpec((tile, width), lambda i: (i, 0)),
+            pl.BlockSpec((tile, width), lambda i: (i, 0)),
+        ],
+        out_specs=pl.BlockSpec((tile, width), lambda i: (i, 0)),
+        out_shape=jax.ShapeDtypeStruct((tokens, width), BF),
+        compiler_params=pltpu.CompilerParams(vmem_limit_bytes=12 * MIB),
+        cost_estimate=pl.CostEstimate(
+            flops=4 * 512 * 512 * 2048, bytes_accessed=6 * 2**20, transcendentals=0
+        ),
+    )(*in_hbm(gpre, w_expand, x, gr))
+
+
+def finish_kernel(parts_ref, expand_out, depth_out):
+    total = jnp.sum(parts_ref[...].astype(F32), 0)
+    own, lanes = total.shape
+    width = expand_out.shape[0]
+    square = jnp.concatenate([total, jnp.zeros((128 - own, lanes), F32)], 0)
+    expand_out[...] = square[:, 0:width].T[:, 0:own]
+    depth_out[...] = square[:, width:].T[0:9, 0:own]
+
+
+def finish(parts):
+    _, own, lanes = parts.shape
+    return pl.pallas_call(
+        finish_kernel,
+        name="last_sum",
+        out_shape=[
+            jax.ShapeDtypeStruct((lanes - 128, own), F32),
+            jax.ShapeDtypeStruct((9, own), F32),
+        ],
+        compiler_params=pltpu.CompilerParams(vmem_limit_bytes=10 * MIB),
+    )(parts)
 
 
 def project_kernel(core_ref, mid_ref, gr_ref, mine_out, other_out, full):
@@ -448,28 +572,29 @@
 def project_grads(core, mid, gr):
     tokens, hid = mid.shape
     width = gr.shape[1]
+    lanes = 512
     return pl.pallas_call(
         project_kernel,
         name="grad_project",
         grid_spec=pltpu.PrefetchScalarGridSpec(
             num_scalar_prefetch=1,
-            grid=(hid // CHUNK,),
+            grid=(hid // lanes,),
             in_specs=[
-                pl.BlockSpec((tokens, CHUNK), lambda j, c: (0, j)),
+                pl.BlockSpec((tokens, lanes), lambda j, c: (0, j)),
                 pl.BlockSpec((tokens, width), lambda j, c: (0, 0)),
             ],
-            out_specs=[pl.BlockSpec((CHUNK // 2, width), lambda j, c: (j, 0))] * 2,
-            scratch_shapes=[pltpu.VMEM((CHUNK, width), F32)],
+            out_specs=[pl.BlockSpec((lanes // 2, width), lambda j, c: (j, 0))] * 2,
+            scratch_shapes=[pltpu.VMEM((lanes, width), F32)],
         ),
         out_shape=[
             jax.ShapeDtypeStruct((hid // 2, width), F32),
             jax.ShapeDtypeStruct((hid // 2, width), BF),
         ],
-        compiler_params=pltpu.CompilerParams(vmem_limit_bytes=48 * 2**20),
+        compiler_params=pltpu.CompilerParams(vmem_limit_bytes=8 * MIB),
         cost_estimate=pl.CostEstimate(
             flops=2 * 512 * 512 * 2048, bytes_accessed=7 * 2**20, transcendentals=0
         ),
-    )(core, mid, gr)
+    )(core, *in_hbm(mid), gr)
 
 
 def attention_grads_kernel(
@@ -513,11 +638,11 @@
             pltpu.VMEM((32, width), F32),
             pltpu.VMEM((128, width), F32),
         ],
-        compiler_params=pltpu.CompilerParams(vmem_limit_bytes=48 * 2**20),
+        compiler_params=pltpu.CompilerParams(vmem_limit_bytes=14 * MIB),
         cost_estimate=pl.CostEstimate(
             flops=8 * 512 * 512 * 512, bytes_accessed=8 * 2**20, transcendentals=0
         ),
-    )(core, arrived, gqkv, attended)
+    )(core, *in_hbm(arrived, gqkv, attended))
 
 
 def add_pair(mine, other):
@@ -532,32 +657,37 @@
     image = block_input[0]
     x = image.reshape(tokens, width)
     go = grad_out[0].reshape(tokens, width)
-    centre, slope_e = expand_block(x, w_expand)
-    act, slope_c, mid, resid, send = forward_block(
-        x, halo(image, 2), go, centre, w_expand, w_depthwise, w_project
+    act0 = expand_block(x, w_expand, 0, 2)
+    act1 = expand_block(x, w_expand, 1, 2)
+    strips, (act0, act1) = halo(image, 2, act0), (act0, act1)
+    mid, resid, send = forward_block(
+        x, strips, go, act0, act1, w_expand, w_depthwise, w_project
     )
     arrived = across_chips(send.reshape(64, 8, 2 * width)).reshape(tokens, 2 * width)
+    slopes = slopes_block(x, strips, w_expand, w_depthwise)
+    arrived, (act, slope_c, slope_e) = lax.optimization_barrier((arrived, slopes))
     back, gqkv, attended = attention_block(arrived, w_qkv, w_out)
     home = across_chips(back.reshape(64, 8, 2 * width)).reshape(tokens, 2 * width)
     attention_pair = add_pair(*attention_grads(core, arrived, gqkv, attended))
     out, gr = residual_block(home, resid, go)
-    project_pair = add_pair(*project_grads(core, mid, gr))
-    first = jnp.concatenate([project_pair, attention_pair], 1)
-    strips = halo(gr.reshape(rows, cols, width), 1)
+    mine, other = project_grads(core, mid, gr)
+    strips = halo(gr.reshape(rows, cols, width), 1, mine)
+    first = jnp.concatenate([add_pair(mine, other), attention_pair], 1)
     strips, first = lax.optimization_barrier((strips, first))
     first = across_chips(first)
-    gx, mine, other = backward_block(
-        core, x, gr, strips, act, slope_c, slope_e, w_expand, w_depthwise, w_project
+    gpre, mine, other = backward_block(
+        core, x, gr, strips, act, slope_c, slope_e, w_depthwise, w_project
     )
+    gx = input_grads(gpre, w_expand, x, gr)
     second = add_pair(mine, other)
     second, first = lax.optimization_barrier((second, first))
-    second = jnp.sum(across_chips(second).astype(F32), 0)
+    grad_expand, grad_depth = finish(across_chips(second))
     first = jnp.sum(first.astype(F32), 0)
     return (
         out.reshape(1, rows, cols, width),
         gx.reshape(1, rows, cols, width),
-        second[:, :width].T,
-        second[:, width : width + 9].T,
+        grad_expand,
+        grad_depth,
         first[:16].T,
         first[16:28].T,
         first[28:].T,

time: 211 us -> 195 us (0.924)
  blocking collectives: 32 us -> 0 us
  Pallas kernels: 64.2 us -> 84.1 us
  local copies, waits for them, and re-layouts: 15.9 us -> 4.73 us
  starting transfers between devices: 49.4 us -> 54.9 us
  waiting for transfers between devices: 37.7 us -> 42.2 us
  other arithmetic: 9.41 us -> 7.19 us
    all_to_all x1 -> x0, blocking collectives: 32 us -> none  [across_chips(): lax.all_to_all(x, AX, 0, 0, tiled=True, axis_index_groups=device_groups(C...]
    pallas_call x3 -> x7, Pallas kernels: 36.9 us -> 57.2 us  [the longest x1 16.9 us: attention_block(): pl.pallas_call(attention_kernel, name='grid_attention', out_shape=[pltpu....]
    unnamed x31 -> x7, local copies, waits for them, and re-layouts: 11.3 us -> 0.73 us
    all_to_all x3 -> x4, starting transfers between devices: 26.7 us -> 35.2 us  [across_chips(): lax.all_to_all(x, AX, 0, 0, tiled=True, axis_index_groups=device_groups(C...]
    pallas_call x1, Pallas kernels: 19.6 us -> 16.2 us  [backward_block(): pl.pallas_call(backward_kernel, name='mbconv_backward', grid_spec=pltpu.P...]
    ppermute x8, waiting for transfers between devices: 4.75 us -> 7.96 us  [shift(): return lax.ppermute(x, axis, pairs)]
    all_to_all x3 -> x4, waiting for transfers between devices: 30.3 us -> 31.2 us  [across_chips(): lax.all_to_all(x, AX, 0, 0, tiled=True, axis_index_groups=device_groups(C...]
  transfers between devices with their start and end apart: 14 -> 15, of which waited for: 5 -> 7; matrix products, arithmetic and copies ran while one was open for 5% -> 4% of each run, Pallas kernels for 15% -> 28%
where the time goes in v3:
time: 195 us; the launch traced here: 194 us
  Pallas kernels  84.1 us (43%)
  starting transfers between devices  54.9 us (28%)
  waiting for transfers between devices  42.2 us (22%)
  other arithmetic  7.19 us (4%)
  local copies, waits for them, and re-layouts  4.73 us (2%)
    all_to_all x4, starting transfers between devices, across_chips(): lax.all_to_all(x, AX, 0, 0, tiled=True, axis_index_groups=device_groups(C...  35.2 us
    all_to_all x4, waiting for transfers between devices, across_chips(): lax.all_to_all(x, AX, 0, 0, tiled=True, axis_index_groups=device_groups(C...  31.2 us
    ppermute x8, starting transfers between devices, shift(): return lax.ppermute(x, axis, pairs)  19.3 us
    pallas_call x1, Pallas kernels, attention_block(): pl.pallas_call(attention_kernel, name='grid_attention', out_shape=[pltpu....  16.9 us
    pallas_call x1, Pallas kernels, backward_block(): pl.pallas_call(backward_kernel, name='mbconv_backward', grid_spec=pltpu.P...  16.2 us
    pallas_call x1, Pallas kernels, slopes_block(): pl.pallas_call(slopes_kernel, name='gelu_slopes', grid=(hid // CHUNK,), i...  15.2 us
    pallas_call x1, Pallas kernels, forward_block(): pl.pallas_call(forward_kernel, name='mbconv_forward', grid=(steps,), in_s...  12.2 us
    ppermute x8, waiting for transfers between devices, shift(): return lax.ppermute(x, axis, pairs)  7.96 us
  transfers between devices with their start and end apart: 15, of which 7 were waited for; matrix products, arithmetic and copies ran while one was open for 4% of the time, Pallas kernels for 28%

profile of v3, /device:TPU:0, one launch (start us, length us, event | category | flops | bytes accessed | tf_op | source)
XLA Modules:
  0.0 194.0 jit_solution(3151445962798953704)
XLA Ops:
  2.8 3.0 %collective-permute-start = (bf16[2,32,512]{2,1,0:T(8,128)(2,1)S(1)}, bf16[2,32,512]{2,1,0:T(8,128)(2,1)S(1)}, u32[]{:S(2)}, u32[]{:S(2)}) collective-permute-start(bf16[2,32,512]{2,1,0:T(8,128)(2,1)S(1)} %get-tuple-element.85), channel_id=1, source_target_pairs={{0,8},{8,16},{16,24},{24,32},{32,40},{40,48},{48,56},{56,64},{64,7... | collective-permute-start | bytes 196616 | tf_op jit(solution)/shard_map/ppermute | solution.py:51
  5.9 2.7 %expand.2.act0_ref = bf16[512,1024]{1,0:T(8,128)(2,1)S(1)} custom-call(bf16[512,512]{1,0:T(8,128)(2,1)} %bitcast.46, bf16[512,2048]{1,0:T(8,128)(2,1)} %we_ref.9), custom_call_target="tpu_custom_call" | custom-call | flops 4294967296 | bytes 3145728 | tf_op jit(solution)/shard_map/expand/pallas_call | solution.py:149
  9.7 5.2 %collective-permute-start.3 = (bf16[20,2,512]{2,1,0:T(2,128)(2,1)S(1)}, bf16[20,2,512]{2,1,0:T(2,128)(2,1)S(1)}, u32[]{:S(2)}, u32[]{:S(2)}) collective-permute-start(bf16[20,2,512]{2,1,0:T(2,128)(2,1)S(1)} %pad_maximum_fusion.4), channel_id=1, source_target_pairs={{0,1},{1,2},{2,3},{3,4},{4,5},{5,6},{6,7},{8,9},{9,10},{10,11},{11... | collective-permute-start | bytes 122888 | tf_op jit(solution)/shard_map/ppermute | solution.py:51
  16.2 2.7 %expand.3.act1_ref = bf16[512,1024]{1,0:T(8,128)(2,1)S(1)} custom-call(bf16[512,512]{1,0:T(8,128)(2,1)} %bitcast.48, bf16[512,2048]{1,0:T(8,128)(2,1)} %we_ref.9), custom_call_target="tpu_custom_call" | custom-call | flops 4294967296 | bytes 3145728 | tf_op jit(solution)/shard_map/expand/pallas_call | solution.py:149
  19.0 3.5 %collective-permute-done.2 = bf16[20,2,512]{2,1,0:T(2,128)(2,1)S(1)} collective-permute-done((bf16[20,2,512]{2,1,0:T(2,128)(2,1)S(1)}, bf16[20,2,512]{2,1,0:T(2,128)(2,1)S(1)}, u32[]{:S(2)}, u32[]{:S(2)}) %collective-permute-start.2) | collective-permute-done | bytes 40992 | tf_op jit(solution)/shard_map/ppermute | solution.py:51
  22.6 12.2 %mbconv_forward.1 = (bf16[512,2048]{1,0:T(8,128)(2,1)}, bf16[512,512]{1,0:T(8,128)(2,1)}, bf16[512,1024]{1,0:T(8,128)(2,1)}) custom-call(bf16[512,512]{1,0:T(8,128)(2,1)} %bitcast.49, bf16[288,512]{1,0:T(8,128)(2,1)S(1)} %pad_maximum_fusion.1.strips_ref, bf16[512,512]{1,0:T(8,128)(2,1)} %bitcast.42, bf16[512,1024]{1,0:T(8,128)(2,1)S(1)} %expand.2.act0_ref, ...), custom_call_target="tpu_custom_call" | custom-call | flops 1468006400 | bytes 10485760 | tf_op jit(solution)/shard_map/mbconv_forward/pallas_call | solution.py:212
  34.8 12.1 %all-to-all-start = ((bf16[64,8,1024]{2,1,0:T(8,128)(2,1)}), bf16[64,8,1024]{2,1,0:T(8,128)(2,1)S(1)}, u32[]{:S(2)}, u32[]{:S(2)}) async-start(bf16[64,8,1024]{2,1,0:T(8,128)(2,1)} %bitcast.45), calls=%async_computation | async-start | bytes 2097152 | tf_op jit(solution)/shard_map/all_to_all | solution.py:45
  46.9 15.2 %gelu_slopes.1 = (bf16[720,2048]{1,0:T(8,128)(2,1)}, bf16[720,2048]{1,0:T(8,128)(2,1)}, bf16[512,2048]{1,0:T(8,128)(2,1)}) custom-call(bf16[512,512]{1,0:T(8,128)(2,1)} %bitcast.50, bf16[288,512]{1,0:T(8,128)(2,1)S(1)} %pad_maximum_fusion.1.strips_ref, bf16[512,2048]{1,0:T(8,128)(2,1)} %we_ref.9, bf16[9,2048]{1,0:T(8,128)(2,1)} %wd_ref.5), custom_call_target="tpu_custom_call" | custom-call | flops 20000000000 | bytes 12582912 | tf_op jit(solution)/shard_map/gelu_slopes/pallas_call | solution.py:287
  62.1 3.0 %all-to-all-done = bf16[64,8,1024]{2,1,0:T(8,128)(2,1)S(1)} async-done(((bf16[64,8,1024]{2,1,0:T(8,128)(2,1)}), bf16[64,8,1024]{2,1,0:T(8,128)(2,1)S(1)}, u32[]{:S(2)}, u32[]{:S(2)}) %all-to-all-start) | async-done | bytes 1048608 | tf_op jit(solution)/shard_map/all_to_all | solution.py:45
  65.1 16.9 %grid_attention.1 = (bf16[512,1024]{1,0:T(8,128)(2,1)}, bf16[512,1536]{1,0:T(8,128)(2,1)}, bf16[512,512]{1,0:T(8,128)(2,1)}) custom-call(bf16[512,1024]{1,0:T(8,128)(2,1)S(1)} %bitcast.37, bf16[512,1536]{1,0:T(8,128)(2,1)} %wq_ref.1, bf16[512,512]{1,0:T(8,128)(2,1)} %wo_ref.1), custom_call_target="tpu_custom_call" | custom-call | flops 2147483648 | bytes 7340032 | tf_op jit(solution)/shard_map/grid_attention/pallas_call | solution.py:378
  82.0 7.4 %all-to-all-start.1 = ((bf16[64,8,1024]{2,1,0:T(8,128)(2,1)}), bf16[64,8,1024]{2,1,0:T(8,128)(2,1)S(1)}, u32[]{:S(2)}, u32[]{:S(2)}) async-start(bf16[64,8,1024]{2,1,0:T(8,128)(2,1)} %bitcast.44), calls=%async_computation.1 | async-start | bytes 2097152 | tf_op jit(solution)/shard_map/all_to_all | solution.py:45
  89.5 4.8 %attention_grads.1 = (f32[1024,512]{1,0:T(8,128)S(1)}, bf16[1024,512]{1,0:T(8,128)(2,1)}) custom-call(s32[1]{0:T(128)} %bitcast.13.core_ref, bf16[512,1024]{1,0:T(8,128)(2,1)} %bitcast.38, bf16[512,1536]{1,0:T(8,128)(2,1)} %get-tuple-element.55.gqkv_ref, bf16[512,512]{1,0:T(8,128)(2,1)} %get-tuple-element.56.att_ref), custom_call_target="tpu_custom_call" | custom-call | flops 1073741824 | bytes 8388608 | tf_op jit(solution)/shard_map/attention_grads/pallas_call | solution.py:625
  94.3 12.6 %all-to-all-done.1 = bf16[64,8,1024]{2,1,0:T(8,128)(2,1)S(1)} async-done(((bf16[64,8,1024]{2,1,0:T(8,128)(2,1)}), bf16[64,8,1024]{2,1,0:T(8,128)(2,1)S(1)}, u32[]{:S(2)}, u32[]{:S(2)}) %all-to-all-start.1) | async-done | bytes 1048608 | tf_op jit(solution)/shard_map/all_to_all | solution.py:45
  110.3 3.0 %collective-permute-start.4 = (bf16[1,32,512]{2,1,0:T(8,128)(2,1)S(1)}, bf16[1,32,512]{2,1,0:T(8,128)(2,1)S(1)}, u32[]{:S(2)}, u32[]{:S(2)}) collective-permute-start(bf16[1,32,512]{2,1,0:T(8,128)(2,1)S(1)} %get-tuple-element.81), channel_id=1, source_target_pairs={{0,8},{8,16},{16,24},{24,32},{32,40},{40,48},{48,56},{56,64},{64,7... | collective-permute-start | bytes 98312 | tf_op jit(solution)/shard_map/ppermute | solution.py:51
  113.4 3.8 %grad_project.1 = (f32[1024,512]{1,0:T(8,128)S(1)}, bf16[1024,512]{1,0:T(8,128)(2,1)S(1)}) custom-call(s32[1]{0:T(128)} %bitcast.13.core_ref, bf16[512,2048]{1,0:T(8,128)(2,1)} %get-tuple-element.50.mid_ref, bf16[512,512]{1,0:T(8,128)(2,1)S(1)} %get-tuple-element.49.gr_ref), custom_call_target="tpu_custom_call" | custom-call | flops 1073741824 | bytes 7340032 | tf_op jit(solution)/shard_map/grad_project/pallas_call | solution.py:576
  117.6 2.9 %collective-permute-start.7 = (bf16[18,1,512]{2,1,0:T(2,128)(2,1)S(1)}, bf16[18,1,512]{2,1,0:T(2,128)(2,1)S(1)}, u32[]{:S(2)}, u32[]{:S(2)}) collective-permute-start(bf16[18,1,512]{2,1,0:T(2,128)(2,1)S(1)} %pad_maximum_fusion.6), channel_id=1, source_target_pairs={{0,1},{1,2},{2,3},{3,4},{4,5},{5,6},{6,7},{8,9},{9,10},{10,11},{11... | collective-permute-start | bytes 55304 | tf_op jit(solution)/shard_map/ppermute | solution.py:51
  123.5 4.5 %collective-permute-done.6 = bf16[18,1,512]{2,1,0:T(2,128)(2,1)S(1)} collective-permute-done((bf16[18,1,512]{2,1,0:T(2,128)(2,1)S(1)}, bf16[18,1,512]{2,1,0:T(2,128)(2,1)S(1)}, u32[]{:S(2)}, u32[]{:S(2)}) %collective-permute-start.6) | collective-permute-done | bytes 18464 | tf_op jit(solution)/shard_map/ppermute | solution.py:51
  129.9 9.9 %all-to-all-start.2 = ((bf16[64,32,512]{2,1,0:T(8,128)(2,1)}), bf16[64,32,512]{2,1,0:T(8,128)(2,1)}, u32[]{:S(2)}, u32[]{:S(2)}) async-start(bf16[64,32,512]{2,1,0:T(8,128)(2,1)} %pad_maximum_fusion), calls=%async_computation.2 | async-start | bytes 4194304 | tf_op jit(solution)/shard_map/all_to_all | solution.py:45
  139.9 16.2 %mbconv_backward.1 = (bf16[512,2048]{1,0:T(8,128)(2,1)}, f32[1024,640]{1,0:T(8,128)S(1)}, bf16[1024,640]{1,0:T(8,128)(2,1)S(1)}) custom-call(s32[1]{0:T(128)} %bitcast.13.core_ref, bf16[512,512]{1,0:T(8,128)(2,1)} %bitcast.51, bf16[512,512]{1,0:T(8,128)(2,1)S(1)} %copy-done.2, bf16[208,512]{1,0:T(8,128)(2,1)S(1)} %pad_maximum_fusion.2.strips_ref, ...), custom_call_target="tpu_custom_call" | custom-call | flops 8589934592 | bytes 20971520 | tf_op jit(solution)/shard_map/mbconv_backward/pallas_call | solution.py:476
  156.2 3.0 %collective-permute-done.10 = bf16[1024,640]{1,0:T(8,128)(2,1)S(1)} collective-permute-done((bf16[1024,640]{1,0:T(8,128)(2,1)S(1)}, bf16[1024,640]{1,0:T(8,128)(2,1)S(1)}, u32[]{:S(2)}, u32[]{:S(2)}) %collective-permute-start.10) | collective-permute-done | bytes 1310752 | tf_op jit(solution)/shard_map/ppermute | solution.py:649
  160.6 6.8 %all-to-all-done.2 = bf16[64,32,512]{2,1,0:T(8,128)(2,1)} async-done(((bf16[64,32,512]{2,1,0:T(8,128)(2,1)}), bf16[64,32,512]{2,1,0:T(8,128)(2,1)}, u32[]{:S(2)}, u32[]{:S(2)}) %all-to-all-start.2) | async-done | bytes 2097184 | tf_op jit(solution)/shard_map/all_to_all | solution.py:45
  167.4 5.7 %all-to-all-start.3 = ((bf16[64,16,640]{2,1,0:T(8,128)(2,1)}), bf16[64,16,640]{2,1,0:T(8,128)(2,1)S(1)}, u32[]{:S(2)}, u32[]{:S(2)}) async-start(bf16[64,16,640]{2,1,0:T(8,128)(2,1)} %bitcast.23), calls=%async_computation.3 | async-start | bytes 2621440 | tf_op jit(solution)/shard_map/all_to_all | solution.py:45
  173.2 6.6 %grad_input.1 = bf16[512,512]{1,0:T(8,128)(2,1)} custom-call(bf16[512,2048]{1,0:T(8,128)(2,1)} %get-tuple-element.63.gpre_ref, bf16[512,2048]{1,0:T(8,128)(2,1)} %we_ref.9, bf16[512,512]{1,0:T(8,128)(2,1)} %bitcast.52, bf16[512,512]{1,0:T(8,128)(2,1)} %copy-done.1), custom_call_target="tpu_custom_call" | custom-call | flops 2147483648 | bytes 6291456 | tf_op jit(solution)/shard_map/grad_input/pallas_call | solution.py:526
  183.6 8.8 %all-to-all-done.3.parts_ref = bf16[64,16,640]{2,1,0:T(8,128)(2,1)S(1)} async-done(((bf16[64,16,640]{2,1,0:T(8,128)(2,1)}), bf16[64,16,640]{2,1,0:T(8,128)(2,1)S(1)}, u32[]{:S(2)}, u32[]{:S(2)}) %all-to-all-start.3) | async-done | bytes 1310752 | tf_op jit(solution)/shard_map/all_to_all | solution.py:45
  (51 shorter events, 20.5 us)
Async XLA Ops:
  1.5 8.0 %collective-permute-start.1 = (bf16[2,32,512]{2,1,0:T(8,128)(2,1)S(1)}, bf16[2,32,512]{2,1,0:T(8,128)(2,1)S(1)}, u32[]{:S(2)}, u32[]{:S(2)}) collective-permute-start(bf16[2,32,512]{2,1,0:T(8,128)(2,1)S(1)} %get-tuple-element.84), channel_id=1, source_target_pairs={{8,0},{16,8},{24,16},{32,24},{40,32},{48,40},{56,48},{64,56},{72,6... | collective-permute-start | bytes 196616 | tf_op jit(solution)/shard_map/ppermute | solution.py:51
  2.8 6.7 %collective-permute-start = (bf16[2,32,512]{2,1,0:T(8,128)(2,1)S(1)}, bf16[2,32,512]{2,1,0:T(8,128)(2,1)S(1)}, u32[]{:S(2)}, u32[]{:S(2)}) collective-permute-start(bf16[2,32,512]{2,1,0:T(8,128)(2,1)S(1)} %get-tuple-element.85), channel_id=1, source_target_pairs={{0,8},{8,16},{16,24},{24,32},{32,40},{40,48},{48,56},{56,64},{64,7... | collective-permute-start | bytes 196616 | tf_op jit(solution)/shard_map/ppermute | solution.py:51
  9.7 9.3 %collective-permute-start.3 = (bf16[20,2,512]{2,1,0:T(2,128)(2,1)S(1)}, bf16[20,2,512]{2,1,0:T(2,128)(2,1)S(1)}, u32[]{:S(2)}, u32[]{:S(2)}) collective-permute-start(bf16[20,2,512]{2,1,0:T(2,128)(2,1)S(1)} %pad_maximum_fusion.4), channel_id=1, source_target_pairs={{0,1},{1,2},{2,3},{3,4},{4,5},{5,6},{6,7},{8,9},{9,10},{10,11},{11... | collective-permute-start | bytes 122888 | tf_op jit(solution)/shard_map/ppermute | solution.py:51
  14.9 7.5 %collective-permute-start.2 = (bf16[20,2,512]{2,1,0:T(2,128)(2,1)S(1)}, bf16[20,2,512]{2,1,0:T(2,128)(2,1)S(1)}, u32[]{:S(2)}, u32[]{:S(2)}) collective-permute-start(bf16[20,2,512]{2,1,0:T(2,128)(2,1)S(1)} %pad_maximum_fusion.3), channel_id=1, source_target_pairs={{1,0},{2,1},{3,2},{4,3},{5,4},{6,5},{7,6},{9,8},{10,9},{11,10},{12... | collective-permute-start | bytes 122888 | tf_op jit(solution)/shard_map/ppermute | solution.py:51
  34.8 30.3 %all-to-all-start = ((bf16[64,8,1024]{2,1,0:T(8,128)(2,1)}), bf16[64,8,1024]{2,1,0:T(8,128)(2,1)S(1)}, u32[]{:S(2)}, u32[]{:S(2)}) async-start(bf16[64,8,1024]{2,1,0:T(8,128)(2,1)} %bitcast.45), calls=%async_computation | async-start | bytes 2097152 | tf_op jit(solution)/shard_map/all_to_all | solution.py:45
  65.1 16.9 %copy-start = (bf16[64,8,1024]{2,1,0:T(8,128)(2,1)}, bf16[64,8,1024]{2,1,0:T(8,128)(2,1)S(1)}, u32[]{:S(2)}) copy-start(bf16[64,8,1024]{2,1,0:T(8,128)(2,1)S(1)} %all-to-all-done) | copy-start | bytes 3145732
  82.0 24.8 %all-to-all-start.1 = ((bf16[64,8,1024]{2,1,0:T(8,128)(2,1)}), bf16[64,8,1024]{2,1,0:T(8,128)(2,1)S(1)}, u32[]{:S(2)}, u32[]{:S(2)}) async-start(bf16[64,8,1024]{2,1,0:T(8,128)(2,1)} %bitcast.44), calls=%async_computation.1 | async-start | bytes 2097152 | tf_op jit(solution)/shard_map/all_to_all | solution.py:45
  94.3 27.6 %collective-permute-start.9 = (bf16[1024,512]{1,0:T(8,128)(2,1)}, bf16[1024,512]{1,0:T(8,128)(2,1)}, u32[]{:S(2)}, u32[]{:S(2)}) collective-permute-start(bf16[1024,512]{1,0:T(8,128)(2,1)} %get-tuple-element.58), channel_id=1, source_target_pairs={{0,8},{1,9},{2,10},{3,11},{4,12},{5,13},{6,14},{7,15},{8,0},{9,1},... | collective-permute-start | bytes 3145736 | tf_op jit(solution)/shard_map/ppermute | solution.py:649
  109.0 8.2 %copy-start.1 = (bf16[512,512]{1,0:T(8,128)(2,1)}, bf16[512,512]{1,0:T(8,128)(2,1)S(1)}, u32[]{:S(2)}) copy-start(bf16[512,512]{1,0:T(8,128)(2,1)S(1)} %get-tuple-element.49.gr_ref) | copy-start | bytes 1572868
  109.0 8.5 %collective-permute-start.5 = (bf16[1,32,512]{2,1,0:T(8,128)(2,1)S(1)}, bf16[1,32,512]{2,1,0:T(8,128)(2,1)S(1)}, u32[]{:S(2)}, u32[]{:S(2)}) collective-permute-start(bf16[1,32,512]{2,1,0:T(8,128)(2,1)S(1)} %get-tuple-element.80), channel_id=1, source_target_pairs={{8,0},{16,8},{24,16},{32,24},{40,32},{48,40},{56,48},{64,56},{72,6... | collective-permute-start | bytes 98312 | tf_op jit(solution)/shard_map/ppermute | solution.py:51
  110.3 7.2 %collective-permute-start.4 = (bf16[1,32,512]{2,1,0:T(8,128)(2,1)S(1)}, bf16[1,32,512]{2,1,0:T(8,128)(2,1)S(1)}, u32[]{:S(2)}, u32[]{:S(2)}) collective-permute-start(bf16[1,32,512]{2,1,0:T(8,128)(2,1)S(1)} %get-tuple-element.81), channel_id=1, source_target_pairs={{0,8},{8,16},{16,24},{24,32},{32,40},{40,48},{48,56},{56,64},{64,7... | collective-permute-start | bytes 98312 | tf_op jit(solution)/shard_map/ppermute | solution.py:51
  117.2 10.9 %collective-permute-start.8 = (bf16[1024,512]{1,0:T(8,128)(2,1)S(1)}, bf16[1024,512]{1,0:T(8,128)(2,1)S(1)}, u32[]{:S(2)}, u32[]{:S(2)}) collective-permute-start(bf16[1024,512]{1,0:T(8,128)(2,1)S(1)} %get-tuple-element.54), channel_id=1, source_target_pairs={{0,8},{1,9},{2,10},{3,11},{4,12},{5,13},{6,14},{7,15},{8,0},{9,1},... | collective-permute-start | bytes 3145736 | tf_op jit(solution)/shard_map/ppermute | solution.py:649
  117.6 5.9 %collective-permute-start.7 = (bf16[18,1,512]{2,1,0:T(2,128)(2,1)S(1)}, bf16[18,1,512]{2,1,0:T(2,128)(2,1)S(1)}, u32[]{:S(2)}, u32[]{:S(2)}) collective-permute-start(bf16[18,1,512]{2,1,0:T(2,128)(2,1)S(1)} %pad_maximum_fusion.6), channel_id=1, source_target_pairs={{0,1},{1,2},{2,3},{3,4},{4,5},{5,6},{6,7},{8,9},{9,10},{10,11},{11... | collective-permute-start | bytes 55304 | tf_op jit(solution)/shard_map/ppermute | solution.py:51
  120.6 7.4 %collective-permute-start.6 = (bf16[18,1,512]{2,1,0:T(2,128)(2,1)S(1)}, bf16[18,1,512]{2,1,0:T(2,128)(2,1)S(1)}, u32[]{:S(2)}, u32[]{:S(2)}) collective-permute-start(bf16[18,1,512]{2,1,0:T(2,128)(2,1)S(1)} %pad_maximum_fusion.5), channel_id=1, source_target_pairs={{1,0},{2,1},{3,2},{4,3},{5,4},{6,5},{7,6},{9,8},{10,9},{11,10},{12... | collective-permute-start | bytes 55304 | tf_op jit(solution)/shard_map/ppermute | solution.py:51
  129.9 10.0 %copy-start.2 = (bf16[512,512]{1,0:T(8,128)(2,1)S(1)}, bf16[512,512]{1,0:T(8,128)(2,1)}, u32[]{:S(2)}) copy-start(bf16[512,512]{1,0:T(8,128)(2,1)} %copy-done.1) | copy-start | bytes 1572868
  129.9 37.5 %all-to-all-start.2 = ((bf16[64,32,512]{2,1,0:T(8,128)(2,1)}), bf16[64,32,512]{2,1,0:T(8,128)(2,1)}, u32[]{:S(2)}, u32[]{:S(2)}) async-start(bf16[64,32,512]{2,1,0:T(8,128)(2,1)} %pad_maximum_fusion), calls=%async_computation.2 | async-start | bytes 4194304 | tf_op jit(solution)/shard_map/all_to_all | solution.py:45
  156.1 3.1 %collective-permute-start.10 = (bf16[1024,640]{1,0:T(8,128)(2,1)S(1)}, bf16[1024,640]{1,0:T(8,128)(2,1)S(1)}, u32[]{:S(2)}, u32[]{:S(2)}) collective-permute-start(bf16[1024,640]{1,0:T(8,128)(2,1)S(1)} %get-tuple-element.65), channel_id=1, source_target_pairs={{0,8},{1,9},{2,10},{3,11},{4,12},{5,13},{6,14},{7,15},{8,0},{9,1},... | collective-permute-start | bytes 3932168 | tf_op jit(solution)/shard_map/ppermute | solution.py:649
  167.4 25.0 %all-to-all-start.3 = ((bf16[64,16,640]{2,1,0:T(8,128)(2,1)}), bf16[64,16,640]{2,1,0:T(8,128)(2,1)S(1)}, u32[]{:S(2)}, u32[]{:S(2)}) async-start(bf16[64,16,640]{2,1,0:T(8,128)(2,1)} %bitcast.23), calls=%async_computation.3 | async-start | bytes 2621440 | tf_op jit(solution)/shard_map/all_to_all | solution.py:45

commit v4 on v3

--- a/solution.py
+++ b/solution.py
@@ -132,7 +132,9 @@
     return pltpu.roll(x, by % x.shape[0], 0)
 
 
-def expand_kernel(x_ref, we_ref, act_out, normed):
+def expand_kernel(x_ref, we_ref, *refs):
+    act_out, normed = refs[-2:]
+
     @pl.when(pl.program_id(0) == 0)
     def _():
         normed[...] = normalize(x_ref[...].astype(F32))[0].astype(BF)
@@ -142,10 +144,12 @@
         act_out[at, :] = gelu(dot(normed[at, :], we_ref[...])).astype(BF)
 
 
-def expand_block(x, w_expand, part, parts):
+def expand_block(x, w_expand, part, parts, held=None):
     tokens, width = x.shape
+    hid = w_expand.shape[1]
     lanes = 512
-    steps = w_expand.shape[1] // lanes // parts
+    steps = hid // lanes // parts
+    held = [] if held is None else [held]
     return pl.pallas_call(
         expand_kernel,
         name="expand",
@@ -153,76 +157,106 @@
         in_specs=[
             pl.BlockSpec((tokens, width), lambda j: (0, 0)),
             pl.BlockSpec((width, lanes), lambda j: (0, j + part * steps)),
-        ],
-        out_specs=pl.BlockSpec((tokens, lanes), lambda j: (0, j)),
-        out_shape=jax.ShapeDtypeStruct((tokens, steps * lanes), BF),
+            *[pl.BlockSpec(memory_space=pl.ANY) for _ in held],
+        ],
+        out_specs=pl.BlockSpec((tokens, lanes), lambda j: (0, j + part * steps)),
+        out_shape=jax.ShapeDtypeStruct((tokens, hid), BF),
         scratch_shapes=[pltpu.VMEM((tokens, width), BF)],
+        input_output_aliases={2: 0} if held else {},
         compiler_params=pltpu.CompilerParams(vmem_limit_bytes=8 * MIB),
         cost_estimate=pl.CostEstimate(
             flops=8 * 512 * 512 * 2048, bytes_accessed=3 * 2**20, transcendentals=2**19
         ),
-    )(*in_hbm(x, w_expand))
+    )(*in_hbm(x, w_expand), *held)
+
+
+FORWARD = 512
 
 
 def forward_kernel(
-    x_ref, strips_ref, go_ref, act0_ref, act1_ref, we_ref, wd_ref, wp_ref,
+    x_hbm, strips_ref, go_hbm, act_ref, we_ref, wd_ref, wp_ref,
     mid_out, resid_out, send_out,
-    normed, act, acc,
+    normed, edge, acc, x_ref, go_ref, sems,
 ):
     step = pl.program_id(0)
     rows, cols = 16, 32
+    width = x_ref.shape[1]
+    load_x = pltpu.make_async_copy(x_hbm, x_ref, sems.at[0])
+    load_go = pltpu.make_async_copy(go_hbm, go_ref, sems.at[1])
 
     @pl.when(step == 0)
     def _():
+        load_x.start()
+        load_go.start()
         every = normalize(strips_ref[...].astype(F32))[0]
         sides = 4 * cols + 8
         near = [every[cols : 3 * cols], every[sides : sides + 8 * (rows + 2)]]
         normed[...] = jnp.concatenate(near, 0).astype(BF)
-        acc[...] = jnp.zeros(acc.shape, F32)
-
-    strips = gelu(dot(normed[...], we_ref[...])).astype(BF).astype(F32)
-    centre = jnp.where(step < pl.num_programs(0) // 2, act0_ref[...], act1_ref[...])
-    place(act, centre.astype(F32), strips, 1, rows, cols)
-    for lo in range(0, CHUNK, 128):
+
+    edge[...] = gelu(dot(normed[...], we_ref[...]))
+    for lo in range(0, FORWARD, 128):
         lanes = slice(lo, lo + 128)
         taps = [wd_ref[k : k + 1, lanes].astype(F32) for k in range(9)]
-        lines = [act[0, :, lanes], act[1, :, lanes]]
+
+        def line(r):
+            if r == 0:
+                centre = edge[0:cols, lanes]
+            elif r == rows + 1:
+                centre = edge[cols : 2 * cols, lanes]
+            else:
+                centre = act_ref[(r - 1) * cols : r * cols, lanes].astype(F32)
+            side = edge[2 * cols + 8 * r : 2 * cols + 8 * (r + 1), lanes]
+            whole = jnp.concatenate([centre, side], 0)
+            return roll(whole, 1)[0:cols], centre, roll(whole, -1)[0:cols]
+
+        lines = [line(0), line(1)]
         for r in range(rows):
-            lines = lines[-2:] + [act[r + 2, :, lanes]]
-            sums = [sum(lines[i] * taps[3 * i + j] for i in range(3)) for j in range(3)]
-            conv = sums[1] + roll(sums[0], 1) + roll(sums[2], -1)
-            mid_out[r * cols : (r + 1) * cols, lanes] = gelu(conv[0:cols]).astype(BF)
-    acc[...] += dot(mid_out[...], wp_ref[...])
+            lines = lines[-2:] + [line(r + 2)]
+            conv = sum(lines[k // 3][k % 3] * taps[k] for k in range(9))
+            mid_out[r * cols : (r + 1) * cols, lanes] = gelu(conv).astype(BF)
+        if lo % 256:
+            at = slice(lo - 128, lo + 128)
+            part = dot(mid_out[:, at], wp_ref[at, :])
+            product = part if lo == 128 else product + part
+
+    @pl.when(step == 0)
+    def _():
+        acc[...] = product
+
+    @pl.when(step > 0)
+    def _():
+        acc[...] += product
 
     @pl.when(step == pl.num_programs(0) - 1)
     def _():
+        load_x.wait()
         resid = (x_ref[...].astype(F32) + acc[...]).astype(BF)
         resid_out[...] = resid
-        width = resid.shape[1]
         send_out[:, 0:width] = normalize(resid.astype(F32))[0].astype(BF)
+        load_go.wait()
         send_out[:, width:] = go_ref[...]
 
 
-def forward_block(x, strips, go, act0, act1, w_expand, w_depthwise, w_project):
+def forward_block(x, strips, go, act, w_expand, w_depthwise, w_project):
     tokens, width = x.shape
     hid = w_expand.shape[1]
     rows, cols = 16, 32
-    steps = hid // CHUNK
+    near = 2 * cols + 8 * (rows + 2)
+    anywhere = pl.BlockSpec(memory_space=pl.ANY)
     whole = lambda a: pl.BlockSpec(a.shape, lambda j: (0,) * a.ndim)
     return pl.pallas_call(
         forward_kernel,
         name="mbconv_forward",
-        grid=(steps,),
+        grid=(hid // FORWARD,),
         in_specs=[
-            whole(x), whole(strips), whole(go),
-            pl.BlockSpec((tokens, CHUNK), lambda j: (0, jnp.minimum(j, steps // 2 - 1))),
-            pl.BlockSpec((tokens, CHUNK), lambda j: (0, jnp.maximum(j - steps // 2, 0))),
-            pl.BlockSpec((width, CHUNK), lambda j: (0, j)),
-            pl.BlockSpec((9, CHUNK), lambda j: (0, j)),
-            pl.BlockSpec((CHUNK, width), lambda j: (j, 0)),
+            anywhere, whole(strips), anywhere,
+            pl.BlockSpec((tokens, FORWARD), lambda j: (0, j)),
+            pl.BlockSpec((width, FORWARD), lambda j: (0, j)),
+            pl.BlockSpec((9, FORWARD), lambda j: (0, j)),
+            pl.BlockSpec((FORWARD, width), lambda j: (j, 0)),
         ],
         out_specs=[
-            pl.BlockSpec((tokens, CHUNK), lambda j: (0, j)),
+            pl.BlockSpec((tokens, FORWARD), lambda j: (0, j)),
             pl.BlockSpec((tokens, width), lambda j: (0, 0)),
             pl.BlockSpec((tokens, 2 * width), lambda j: (0, 0)),
         ],
@@ -232,15 +266,18 @@
             pltpu.HBM((tokens, 2 * width), BF),
         ],
         scratch_shapes=[
-            pltpu.VMEM((2 * cols + 8 * (rows + 2), width), BF),
-            pltpu.VMEM((rows + 2, WIDE, CHUNK), F32),
+            pltpu.VMEM((near, width), BF),
+            pltpu.VMEM((near, FORWARD), F32),
             pltpu.VMEM((tokens, width), F32),
-        ],
-        compiler_params=pltpu.CompilerParams(vmem_limit_bytes=14 * MIB),
+            pltpu.VMEM((tokens, width), BF),
+            pltpu.VMEM((tokens, width), BF),
+            pltpu.SemaphoreType.DMA((2,)),
+        ],
+        compiler_params=pltpu.CompilerParams(vmem_limit_bytes=18 * MIB),
         cost_estimate=pl.CostEstimate(
             flops=2 * 700 * 512 * 2048, bytes_accessed=10 * 2**20, transcendentals=2**20
         ),
-    )(*in_hbm(x), strips, *in_hbm(go), act0, act1, *in_hbm(w_expand, w_depthwise, w_project))
+    )(*in_hbm(x), strips, *in_hbm(go), act, *in_hbm(w_expand, w_depthwise, w_project))
 
 
 def slopes_kernel(
@@ -315,22 +352,31 @@
     )(*in_hbm(x), strips, *in_hbm(w_expand, w_depthwise))
 
 
-def attention_kernel(in_ref, wq_ref, wo_ref, send_out, gq_out, att_out, qkv, gatt, att, gq):
-    width = wo_ref.shape[0]
+def attention_kernel(
+    in_ref, wq_hbm, wo_hbm, send_hbm, gq_hbm, att_hbm,
+    wq, wo, qkv, gatt, att, gq, send, gqb, attended, sems,
+):
+    tokens, width = attended.shape
     groups = 8
-    members = in_ref.shape[0] // groups
+    members = tokens // groups
+    quads = width // 128
     scale = HDIM ** (-0.5)
-    quads = width // 128
+    load_wo = pltpu.make_async_copy(wo_hbm, wo, sems.at[0])
+    load_wq = pltpu.make_async_copy(wq_hbm, wq, sems.at[1])
+    load_wo.start()
+    load_wq.start()
 
     def put(ref, at, value):
         value = value.astype(BF).astype(F32)
         for quad in range(quads):
             ref[at + quad] = value[:, quad * 128 : (quad + 1) * 128]
 
+    load_wo.wait()
+    put(gatt, 0, dot_nt(in_ref[:, width:], wo[...]))
+    load_wq.wait()
     for part in range(3):
         lanes = slice(part * width, (part + 1) * width)
-        put(qkv, part * quads, dot(in_ref[:, 0:width], wq_ref[:, lanes]))
-    put(gatt, 0, dot_nt(in_ref[:, width:], wo_ref[...]))
+        put(qkv, part * quads, dot(in_ref[:, 0:width], wq[:, lanes]))
     per = 128 // HDIM
     head = lax.broadcasted_iota(jnp.int32, (members, 128), 1) // HDIM
 
@@ -345,51 +391,74 @@
 
     def one_group(g, _):
         at = pl.ds(g, members, stride=groups)
-        for quad in range(quads):
-            q = qkv[quad, at, :]
-            k = qkv[quads + quad, at, :].astype(BF)
-            v = qkv[2 * quads + quad, at, :].astype(BF)
-            do = gatt[quad, at, :]
-            qs, dos = spread(q), spread(do)
-            scores = dot_nt(k, qs) * scale
-            dp = dot_nt(v, dos)
-            p = jnp.exp(scores - jnp.max(scores, 0, keepdims=True))
-            p = p / jnp.sum(p, 0, keepdims=True)
-            pb = p.astype(BF)
-            ds = (p * (dp - jnp.sum(p * dp, 0, keepdims=True)) * scale).astype(BF)
-            att[quad, at, :] = gather(dot_tn(pb, v))
-            gq[quad, at, :] = gather(dot_tn(ds, k))
-            gq[quads + quad, at, :] = dot(ds, qs)
-            gq[2 * quads + quad, at, :] = dot(pb, dos)
+        every = range(quads)
+        q = [spread(qkv[i, at, :]) for i in every]
+        k = [qkv[quads + i, at, :].astype(BF) for i in every]
+        v = [qkv[2 * quads + i, at, :].astype(BF) for i in every]
+        do = [spread(gatt[i, at, :]) for i in every]
+        scores = [dot_nt(k[i], q[i]) * scale for i in every]
+        dp = [dot_nt(v[i], do[i]) for i in every]
+        p = [jnp.exp(s - jnp.max(s, 0, keepdims=True)) for s in scores]
+        p = [e * (1.0 / jnp.sum(e, 0, keepdims=True)) for e in p]
+        pb = [e.astype(BF) for e in p]
+        ds = [
+            (p[i] * (dp[i] - jnp.sum(p[i] * dp[i], 0, keepdims=True)) * scale).astype(BF)
+            for i in every
+        ]
+        for i in every:
+            att[i, at, :] = gather(dot_tn(pb[i], v[i]))
+            gq[i, at, :] = gather(dot_tn(ds[i], k[i]))
+            gq[quads + i, at, :] = dot(ds[i], q[i])
+            gq[2 * quads + i, at, :] = dot(pb[i], do[i])
         return 0
 
     lax.fori_loop(0, groups, one_group, 0)
-    attended = jnp.concatenate([att[i] for i in range(quads)], 1).astype(BF)
-    att_out[...] = attended
-    send_out[:, 0:width] = dot(attended, wo_ref[...]).astype(BF)
-    gqb = jnp.concatenate([gq[i] for i in range(3 * quads)], 1).astype(BF)
-    gq_out[...] = gqb
-    send_out[:, width:] = dot_nt(gqb, wq_ref[...]).astype(BF)
+    attended[...] = jnp.concatenate([att[i] for i in range(quads)], 1).astype(BF)
+    store_att = pltpu.make_async_copy(attended, att_hbm, sems.at[2])
+    store_att.start()
+    gqb[...] = jnp.concatenate([gq[i] for i in range(3 * quads)], 1).astype(BF)
+    store_gq = pltpu.make_async_copy(gqb, gq_hbm, sems.at[3])
+    store_gq.start()
+    stores = []
+    for half in range(2):
+        at = pl.ds(half * tokens // 2, tokens // 2)
+        rows = slice(half * tokens // 2, (half + 1) * tokens // 2)
+        send[rows, 0:width] = dot(attended[rows, :], wo[...]).astype(BF)
+        send[rows, width:] = dot_nt(gqb[rows, :], wq[...]).astype(BF)
+        store = pltpu.make_async_copy(send.at[at], send_hbm.at[at], sems.at[4 + half])
+        store.start()
+        stores.append(store)
+    for store in [store_att, store_gq, *stores]:
+        store.wait()
 
 
 def attention_block(arrived, w_qkv, w_out):
     tokens = arrived.shape[0]
     width = w_out.shape[0]
+    anywhere = pl.BlockSpec(memory_space=pl.ANY)
     return pl.pallas_call(
         attention_kernel,
         name="grid_attention",
+        in_specs=[pl.BlockSpec(memory_space=pltpu.VMEM), anywhere, anywhere],
+        out_specs=[anywhere] * 3,
         out_shape=[
             pltpu.HBM((tokens, 2 * width), BF),
             pltpu.HBM((tokens, 3 * width), BF),
             pltpu.HBM((tokens, width), BF),
         ],
         scratch_shapes=[
+            pltpu.VMEM((width, 3 * width), BF),
+            pltpu.VMEM((width, width), BF),
             pltpu.VMEM((3 * width // 128, tokens, 128), F32),
             pltpu.VMEM((width // 128, tokens, 128), F32),
             pltpu.VMEM((width // 128, tokens, 128), F32),
             pltpu.VMEM((3 * width // 128, tokens, 128), F32),
-        ],
-        compiler_params=pltpu.CompilerParams(vmem_limit_bytes=22 * MIB),
+            pltpu.VMEM((tokens, 2 * width), BF),
+            pltpu.VMEM((tokens, 3 * width), BF),
+            pltpu.VMEM((tokens, width), BF),
+            pltpu.SemaphoreType.DMA((6,)),
+        ],
+        compiler_params=pltpu.CompilerParams(vmem_limit_bytes=24 * MIB),
         cost_estimate=pl.CostEstimate(
             flops=2 * 512 * 512 * 512 * 8, bytes_accessed=7 * 2**20, transcendentals=2**20
         ),
@@ -544,11 +613,10 @@
 
 def finish_kernel(parts_ref, expand_out, depth_out):
     total = jnp.sum(parts_ref[...].astype(F32), 0)
-    own, lanes = total.shape
-    width = expand_out.shape[0]
-    square = jnp.concatenate([total, jnp.zeros((128 - own, lanes), F32)], 0)
-    expand_out[...] = square[:, 0:width].T[:, 0:own]
-    depth_out[...] = square[:, width:].T[0:9, 0:own]
+    own, width = expand_out.shape
+    expand_out[...] = total[:, 0:width]
+    square = jnp.concatenate([total[:, width:], jnp.zeros((128 - own, 128), F32)], 0)
+    depth_out[...] = square.T[0:9, 0:own]
 
 
 def finish(parts):
@@ -557,8 +625,8 @@
         finish_kernel,
         name="last_sum",
         out_shape=[
-            jax.ShapeDtypeStruct((lanes - 128, own), F32),
-            jax.ShapeDtypeStruct((9, own), F32),
+            pltpu.HBM((own, lanes - 128), F32),
+            pltpu.HBM((9, own), F32),
         ],
         compiler_params=pltpu.CompilerParams(vmem_limit_bytes=10 * MIB),
     )(parts)
@@ -658,11 +726,9 @@
     x = image.reshape(tokens, width)
     go = grad_out[0].reshape(tokens, width)
     act0 = expand_block(x, w_expand, 0, 2)
-    act1 = expand_block(x, w_expand, 1, 2)
-    strips, (act0, act1) = halo(image, 2, act0), (act0, act1)
-    mid, resid, send = forward_block(
-        x, strips, go, act0, act1, w_expand, w_depthwise, w_project
-    )
+    centre = expand_block(x, w_expand, 1, 2, act0)
+    strips = halo(image, 2, act0)
+    mid, resid, send = forward_block(x, strips, go, centre, w_expand, w_depthwise, w_project)
     arrived = across_chips(send.reshape(64, 8, 2 * width)).reshape(tokens, 2 * width)
     slopes = slopes_block(x, strips, w_expand, w_depthwise)
     arrived, (act, slope_c, slope_e) = lax.optimization_barrier((arrived, slopes))
@@ -686,7 +752,7 @@
     return (
         out.reshape(1, rows, cols, width),
         gx.reshape(1, rows, cols, width),
-        grad_expand,
+        grad_expand.T,
         grad_depth,
         first[:16].T,
         first[16:28].T,

time: 195 us -> 187 us (0.959)
  Pallas kernels: 84.1 us -> 76.8 us
    pallas_call x3, Pallas kernels: 30 us -> 22.8 us  [the longest x1 11 us: attention_block(): pl.pallas_call(attention_kernel, name='grid_attention', in_specs=[pl.Bloc...]
  transfers between devices with their start and end apart: 15 -> 15, of which waited for: 7 -> 7; matrix products, arithmetic and copies ran while one was open for 4% -> 4% of each run, Pallas kernels for 28% -> 29%
where the time goes in v4:
time: 187 us; the launch traced here: 186 us
  Pallas kernels  76.8 us (41%)
  starting transfers between devices  54.8 us (29%)
  waiting for transfers between devices  42.4 us (23%)
  other arithmetic  7.19 us (4%)
  local copies, waits for them, and re-layouts  4.01 us (2%)
    all_to_all x4, starting transfers between devices, across_chips(): lax.all_to_all(x, AX, 0, 0, tiled=True, axis_index_groups=device_groups(C...  35 us
    all_to_all x4, waiting for transfers between devices, across_chips(): lax.all_to_all(x, AX, 0, 0, tiled=True, axis_index_groups=device_groups(C...  31.3 us
    ppermute x8, starting transfers between devices, shift(): return lax.ppermute(x, axis, pairs)  19.3 us
    pallas_call x1, Pallas kernels, backward_block(): pl.pallas_call(backward_kernel, name='mbconv_backward', grid_spec=pltpu.P...  16.2 us
    pallas_call x1, Pallas kernels, slopes_block(): pl.pallas_call(slopes_kernel, name='gelu_slopes', grid=(hid // CHUNK,), i...  15.2 us
    pallas_call x1, Pallas kernels, attention_block(): pl.pallas_call(attention_kernel, name='grid_attention', in_specs=[pl.Bloc...  11 us
    pallas_call x1, Pallas kernels, forward_block(): pl.pallas_call(forward_kernel, name='mbconv_forward', grid=(hid // FORWAR...  10.9 us
    ppermute x8, waiting for transfers between devices, shift(): return lax.ppermute(x, axis, pairs)  8.04 us
  transfers between devices with their start and end apart: 15, of which 7 were waited for; matrix products, arithmetic and copies ran while one was open for 4% of the time, Pallas kernels for 29%

profile of v4, /device:TPU:0, one launch (start us, length us, event | category | flops | bytes accessed | tf_op | source)
XLA Modules:
  0.0 186.1 jit_solution(8823842249755135254)
XLA Ops:
  2.8 3.0 %collective-permute-start = (bf16[2,32,512]{2,1,0:T(8,128)(2,1)S(1)}, bf16[2,32,512]{2,1,0:T(8,128)(2,1)S(1)}, u32[]{:S(2)}, u32[]{:S(2)}) collective-permute-start(bf16[2,32,512]{2,1,0:T(8,128)(2,1)S(1)} %get-tuple-element.78), channel_id=1, source_target_pairs={{0,8},{8,16},{16,24},{24,32},{32,40},{40,48},{48,56},{56,64},{64,7... | collective-permute-start | bytes 196616 | tf_op jit(solution)/shard_map/ppermute | solution.py:51
  5.9 2.7 %expand.2.refs_0_ = bf16[512,2048]{1,0:T(8,128)(2,1)S(1)} custom-call(bf16[512,512]{1,0:T(8,128)(2,1)} %bitcast.47, bf16[512,2048]{1,0:T(8,128)(2,1)} %we_ref.9), custom_call_target="tpu_custom_call" | custom-call | flops 4294967296 | bytes 3145728 | tf_op jit(solution)/shard_map/expand/pallas_call | solution.py:153
  9.7 5.2 %collective-permute-start.3 = (bf16[20,2,512]{2,1,0:T(2,128)(2,1)S(1)}, bf16[20,2,512]{2,1,0:T(2,128)(2,1)S(1)}, u32[]{:S(2)}, u32[]{:S(2)}) collective-permute-start(bf16[20,2,512]{2,1,0:T(2,128)(2,1)S(1)} %pad_maximum_fusion.4), channel_id=1, source_target_pairs={{0,1},{1,2},{2,3},{3,4},{4,5},{5,6},{6,7},{8,9},{9,10},{10,11},{11... | collective-permute-start | bytes 122888 | tf_op jit(solution)/shard_map/ppermute | solution.py:51
  16.3 2.7 %expand.3.act_ref = bf16[512,2048]{1,0:T(8,128)(2,1)S(1)} custom-call(bf16[512,512]{1,0:T(8,128)(2,1)} %bitcast.49, bf16[512,2048]{1,0:T(8,128)(2,1)} %we_ref.9, bf16[512,2048]{1,0:T(8,128)(2,1)S(1)} %expand.2.refs_0_), custom_call_target="tpu_custom_call", output_to_operand_aliasing={{}: (2, {})} | custom-call | flops 4294967296 | bytes 3145728 | tf_op jit(solution)/shard_map/expand/pallas_call | solution.py:153
  19.0 3.6 %collective-permute-done.2 = bf16[20,2,512]{2,1,0:T(2,128)(2,1)S(1)} collective-permute-done((bf16[20,2,512]{2,1,0:T(2,128)(2,1)S(1)}, bf16[20,2,512]{2,1,0:T(2,128)(2,1)S(1)}, u32[]{:S(2)}, u32[]{:S(2)}) %collective-permute-start.2) | collective-permute-done | bytes 40992 | tf_op jit(solution)/shard_map/ppermute | solution.py:51
  22.7 10.9 %mbconv_forward.1 = (bf16[512,2048]{1,0:T(8,128)(2,1)}, bf16[512,512]{1,0:T(8,128)(2,1)}, bf16[512,1024]{1,0:T(8,128)(2,1)}) custom-call(bf16[512,512]{1,0:T(8,128)(2,1)} %bitcast.50, bf16[288,512]{1,0:T(8,128)(2,1)S(1)} %pad_maximum_fusion.1.strips_ref, bf16[512,512]{1,0:T(8,128)(2,1)} %bitcast.43, bf16[512,2048]{1,0:T(8,128)(2,1)S(1)} %expand.3.act_ref, ...), custom_call_target="tpu_custom_call" | custom-call | flops 1468006400 | bytes 10485760 | tf_op jit(solution)/shard_map/mbconv_forward/pallas_call | solution.py:247
  33.6 12.0 %all-to-all-start = ((bf16[64,8,1024]{2,1,0:T(8,128)(2,1)}), bf16[64,8,1024]{2,1,0:T(8,128)(2,1)S(1)}, u32[]{:S(2)}, u32[]{:S(2)}) async-start(bf16[64,8,1024]{2,1,0:T(8,128)(2,1)} %bitcast.46), calls=%async_computation | async-start | bytes 2097152 | tf_op jit(solution)/shard_map/all_to_all | solution.py:45
  45.7 15.2 %gelu_slopes.1 = (bf16[720,2048]{1,0:T(8,128)(2,1)}, bf16[720,2048]{1,0:T(8,128)(2,1)}, bf16[512,2048]{1,0:T(8,128)(2,1)}) custom-call(bf16[512,512]{1,0:T(8,128)(2,1)} %bitcast.51, bf16[288,512]{1,0:T(8,128)(2,1)S(1)} %pad_maximum_fusion.1.strips_ref, bf16[512,2048]{1,0:T(8,128)(2,1)} %we_ref.9, bf16[9,2048]{1,0:T(8,128)(2,1)} %wd_ref.5), custom_call_target="tpu_custom_call" | custom-call | flops 20000000000 | bytes 12582912 | tf_op jit(solution)/shard_map/gelu_slopes/pallas_call | solution.py:324
  60.8 3.1 %all-to-all-done = bf16[64,8,1024]{2,1,0:T(8,128)(2,1)S(1)} async-done(((bf16[64,8,1024]{2,1,0:T(8,128)(2,1)}), bf16[64,8,1024]{2,1,0:T(8,128)(2,1)S(1)}, u32[]{:S(2)}, u32[]{:S(2)}) %all-to-all-start) | async-done | bytes 1048608 | tf_op jit(solution)/shard_map/all_to_all | solution.py:45
  63.9 11.0 %grid_attention.1 = (bf16[512,1024]{1,0:T(8,128)(2,1)}, bf16[512,1536]{1,0:T(8,128)(2,1)}, bf16[512,512]{1,0:T(8,128)(2,1)}) custom-call(bf16[512,1024]{1,0:T(8,128)(2,1)S(1)} %bitcast.38, bf16[512,1536]{1,0:T(8,128)(2,1)} %wq_hbm.1, bf16[512,512]{1,0:T(8,128)(2,1)} %wo_hbm.1), custom_call_target="tpu_custom_call" | custom-call | flops 2147483648 | bytes 7340032 | tf_op jit(solution)/shard_map/grid_attention/pallas_call | solution.py:439
  74.9 7.3 %all-to-all-start.1 = ((bf16[64,8,1024]{2,1,0:T(8,128)(2,1)}), bf16[64,8,1024]{2,1,0:T(8,128)(2,1)S(1)}, u32[]{:S(2)}, u32[]{:S(2)}) async-start(bf16[64,8,1024]{2,1,0:T(8,128)(2,1)} %bitcast.45), calls=%async_computation.1 | async-start | bytes 2097152 | tf_op jit(solution)/shard_map/all_to_all | solution.py:45
  82.4 4.8 %attention_grads.1 = (f32[1024,512]{1,0:T(8,128)S(1)}, bf16[1024,512]{1,0:T(8,128)(2,1)}) custom-call(s32[1]{0:T(128)} %bitcast.13.core_ref, bf16[512,1024]{1,0:T(8,128)(2,1)} %bitcast.39, bf16[512,1536]{1,0:T(8,128)(2,1)} %get-tuple-element.55.gqkv_ref, bf16[512,512]{1,0:T(8,128)(2,1)} %get-tuple-element.56.att_ref), custom_call_target="tpu_custom_call" | custom-call | flops 1073741824 | bytes 8388608 | tf_op jit(solution)/shard_map/attention_grads/pallas_call | solution.py:693
  87.2 12.6 %all-to-all-done.1 = bf16[64,8,1024]{2,1,0:T(8,128)(2,1)S(1)} async-done(((bf16[64,8,1024]{2,1,0:T(8,128)(2,1)}), bf16[64,8,1024]{2,1,0:T(8,128)(2,1)S(1)}, u32[]{:S(2)}, u32[]{:S(2)}) %all-to-all-start.1) | async-done | bytes 1048608 | tf_op jit(solution)/shard_map/all_to_all | solution.py:45
  103.2 3.0 %collective-permute-start.4 = (bf16[1,32,512]{2,1,0:T(8,128)(2,1)S(1)}, bf16[1,32,512]{2,1,0:T(8,128)(2,1)S(1)}, u32[]{:S(2)}, u32[]{:S(2)}) collective-permute-start(bf16[1,32,512]{2,1,0:T(8,128)(2,1)S(1)} %get-tuple-element.74), channel_id=1, source_target_pairs={{0,8},{8,16},{16,24},{24,32},{32,40},{40,48},{48,56},{56,64},{64,7... | collective-permute-start | bytes 98312 | tf_op jit(solution)/shard_map/ppermute | solution.py:51
  106.3 3.8 %grad_project.1 = (f32[1024,512]{1,0:T(8,128)S(1)}, bf16[1024,512]{1,0:T(8,128)(2,1)S(1)}) custom-call(s32[1]{0:T(128)} %bitcast.13.core_ref, bf16[512,2048]{1,0:T(8,128)(2,1)} %get-tuple-element.50.mid_ref, bf16[512,512]{1,0:T(8,128)(2,1)S(1)} %get-tuple-element.49.gr_ref), custom_call_target="tpu_custom_call" | custom-call | flops 1073741824 | bytes 7340032 | tf_op jit(solution)/shard_map/grad_project/pallas_call | solution.py:644
  110.5 2.9 %collective-permute-start.7 = (bf16[18,1,512]{2,1,0:T(2,128)(2,1)S(1)}, bf16[18,1,512]{2,1,0:T(2,128)(2,1)S(1)}, u32[]{:S(2)}, u32[]{:S(2)}) collective-permute-start(bf16[18,1,512]{2,1,0:T(2,128)(2,1)S(1)} %pad_maximum_fusion.6), channel_id=1, source_target_pairs={{0,1},{1,2},{2,3},{3,4},{4,5},{5,6},{6,7},{8,9},{9,10},{10,11},{11... | collective-permute-start | bytes 55304 | tf_op jit(solution)/shard_map/ppermute | solution.py:51
  116.4 4.5 %collective-permute-done.6 = bf16[18,1,512]{2,1,0:T(2,128)(2,1)S(1)} collective-permute-done((bf16[18,1,512]{2,1,0:T(2,128)(2,1)S(1)}, bf16[18,1,512]{2,1,0:T(2,128)(2,1)S(1)}, u32[]{:S(2)}, u32[]{:S(2)}) %collective-permute-start.6) | collective-permute-done | bytes 18464 | tf_op jit(solution)/shard_map/ppermute | solution.py:51
  122.8 9.9 %all-to-all-start.2 = ((bf16[64,32,512]{2,1,0:T(8,128)(2,1)}), bf16[64,32,512]{2,1,0:T(8,128)(2,1)}, u32[]{:S(2)}, u32[]{:S(2)}) async-start(bf16[64,32,512]{2,1,0:T(8,128)(2,1)} %pad_maximum_fusion), calls=%async_computation.2 | async-start | bytes 4194304 | tf_op jit(solution)/shard_map/all_to_all | solution.py:45
  132.8 16.2 %mbconv_backward.1 = (bf16[512,2048]{1,0:T(8,128)(2,1)}, f32[1024,640]{1,0:T(8,128)S(1)}, bf16[1024,640]{1,0:T(8,128)(2,1)S(1)}) custom-call(s32[1]{0:T(128)} %bitcast.13.core_ref, bf16[512,512]{1,0:T(8,128)(2,1)} %bitcast.52, bf16[512,512]{1,0:T(8,128)(2,1)S(1)} %copy-done.2, bf16[208,512]{1,0:T(8,128)(2,1)S(1)} %pad_maximum_fusion.2.strips_ref, ...), custom_call_target="tpu_custom_call" | custom-call | flops 8589934592 | bytes 20971520 | tf_op jit(solution)/shard_map/mbconv_backward/pallas_call | solution.py:545
  149.1 3.0 %collective-permute-done.10 = bf16[1024,640]{1,0:T(8,128)(2,1)S(1)} collective-permute-done((bf16[1024,640]{1,0:T(8,128)(2,1)S(1)}, bf16[1024,640]{1,0:T(8,128)(2,1)S(1)}, u32[]{:S(2)}, u32[]{:S(2)}) %collective-permute-start.10) | collective-permute-done | bytes 1310752 | tf_op jit(solution)/shard_map/ppermute | solution.py:717
  153.5 6.8 %all-to-all-done.2 = bf16[64,32,512]{2,1,0:T(8,128)(2,1)} async-done(((bf16[64,32,512]{2,1,0:T(8,128)(2,1)}), bf16[64,32,512]{2,1,0:T(8,128)(2,1)}, u32[]{:S(2)}, u32[]{:S(2)}) %all-to-all-start.2) | async-done | bytes 2097184 | tf_op jit(solution)/shard_map/all_to_all | solution.py:45
  160.3 5.7 %all-to-all-start.3 = ((bf16[64,16,640]{2,1,0:T(8,128)(2,1)}), bf16[64,16,640]{2,1,0:T(8,128)(2,1)S(1)}, u32[]{:S(2)}, u32[]{:S(2)}) async-start(bf16[64,16,640]{2,1,0:T(8,128)(2,1)} %bitcast.23), calls=%async_computation.3 | async-start | bytes 2621440 | tf_op jit(solution)/shard_map/all_to_all | solution.py:45
  166.1 6.6 %grad_input.1 = bf16[512,512]{1,0:T(8,128)(2,1)} custom-call(bf16[512,2048]{1,0:T(8,128)(2,1)} %get-tuple-element.63.gpre_ref, bf16[512,2048]{1,0:T(8,128)(2,1)} %we_ref.9, bf16[512,512]{1,0:T(8,128)(2,1)} %bitcast.53, bf16[512,512]{1,0:T(8,128)(2,1)} %copy-done.1), custom_call_target="tpu_custom_call" | custom-call | flops 2147483648 | bytes 6291456 | tf_op jit(solution)/shard_map/grad_input/pallas_call | solution.py:595
  176.5 8.8 %all-to-all-done.3.parts_ref = bf16[64,16,640]{2,1,0:T(8,128)(2,1)S(1)} async-done(((bf16[64,16,640]{2,1,0:T(8,128)(2,1)}), bf16[64,16,640]{2,1,0:T(8,128)(2,1)S(1)}, u32[]{:S(2)}, u32[]{:S(2)}) %all-to-all-start.3) | async-done | bytes 1310752 | tf_op jit(solution)/shard_map/all_to_all | solution.py:45
  (50 shorter events, 19.8 us)
Async XLA Ops:
  1.5 8.1 %collective-permute-start.1 = (bf16[2,32,512]{2,1,0:T(8,128)(2,1)S(1)}, bf16[2,32,512]{2,1,0:T(8,128)(2,1)S(1)}, u32[]{:S(2)}, u32[]{:S(2)}) collective-permute-start(bf16[2,32,512]{2,1,0:T(8,128)(2,1)S(1)} %get-tuple-element.77), channel_id=1, source_target_pairs={{8,0},{16,8},{24,16},{32,24},{40,32},{48,40},{56,48},{64,56},{72,6... | collective-permute-start | bytes 196616 | tf_op jit(solution)/shard_map/ppermute | solution.py:51
  2.8 6.8 %collective-permute-start = (bf16[2,32,512]{2,1,0:T(8,128)(2,1)S(1)}, bf16[2,32,512]{2,1,0:T(8,128)(2,1)S(1)}, u32[]{:S(2)}, u32[]{:S(2)}) collective-permute-start(bf16[2,32,512]{2,1,0:T(8,128)(2,1)S(1)} %get-tuple-element.78), channel_id=1, source_target_pairs={{0,8},{8,16},{16,24},{24,32},{32,40},{40,48},{48,56},{56,64},{64,7... | collective-permute-start | bytes 196616 | tf_op jit(solution)/shard_map/ppermute | solution.py:51
  9.7 9.2 %collective-permute-start.3 = (bf16[20,2,512]{2,1,0:T(2,128)(2,1)S(1)}, bf16[20,2,512]{2,1,0:T(2,128)(2,1)S(1)}, u32[]{:S(2)}, u32[]{:S(2)}) collective-permute-start(bf16[20,2,512]{2,1,0:T(2,128)(2,1)S(1)} %pad_maximum_fusion.4), channel_id=1, source_target_pairs={{0,1},{1,2},{2,3},{3,4},{4,5},{5,6},{6,7},{8,9},{9,10},{10,11},{11... | collective-permute-start | bytes 122888 | tf_op jit(solution)/shard_map/ppermute | solution.py:51
  15.0 7.5 %collective-permute-start.2 = (bf16[20,2,512]{2,1,0:T(2,128)(2,1)S(1)}, bf16[20,2,512]{2,1,0:T(2,128)(2,1)S(1)}, u32[]{:S(2)}, u32[]{:S(2)}) collective-permute-start(bf16[20,2,512]{2,1,0:T(2,128)(2,1)S(1)} %pad_maximum_fusion.3), channel_id=1, source_target_pairs={{1,0},{2,1},{3,2},{4,3},{5,4},{6,5},{7,6},{9,8},{10,9},{11,10},{12... | collective-permute-start | bytes 122888 | tf_op jit(solution)/shard_map/ppermute | solution.py:51
  33.6 30.3 %all-to-all-start = ((bf16[64,8,1024]{2,1,0:T(8,128)(2,1)}), bf16[64,8,1024]{2,1,0:T(8,128)(2,1)S(1)}, u32[]{:S(2)}, u32[]{:S(2)}) async-start(bf16[64,8,1024]{2,1,0:T(8,128)(2,1)} %bitcast.46), calls=%async_computation | async-start | bytes 2097152 | tf_op jit(solution)/shard_map/all_to_all | solution.py:45
  63.9 11.0 %copy-start = (bf16[64,8,1024]{2,1,0:T(8,128)(2,1)}, bf16[64,8,1024]{2,1,0:T(8,128)(2,1)S(1)}, u32[]{:S(2)}) copy-start(bf16[64,8,1024]{2,1,0:T(8,128)(2,1)S(1)} %all-to-all-done) | copy-start | bytes 3145732
  74.9 24.8 %all-to-all-start.1 = ((bf16[64,8,1024]{2,1,0:T(8,128)(2,1)}), bf16[64,8,1024]{2,1,0:T(8,128)(2,1)S(1)}, u32[]{:S(2)}, u32[]{:S(2)}) async-start(bf16[64,8,1024]{2,1,0:T(8,128)(2,1)} %bitcast.45), calls=%async_computation.1 | async-start | bytes 2097152 | tf_op jit(solution)/shard_map/all_to_all | solution.py:45
  87.2 27.6 %collective-permute-start.9 = (bf16[1024,512]{1,0:T(8,128)(2,1)}, bf16[1024,512]{1,0:T(8,128)(2,1)}, u32[]{:S(2)}, u32[]{:S(2)}) collective-permute-start(bf16[1024,512]{1,0:T(8,128)(2,1)} %get-tuple-element.58), channel_id=1, source_target_pairs={{0,8},{1,9},{2,10},{3,11},{4,12},{5,13},{6,14},{7,15},{8,0},{9,1},... | collective-permute-start | bytes 3145736 | tf_op jit(solution)/shard_map/ppermute | solution.py:717
  101.9 8.2 %copy-start.1 = (bf16[512,512]{1,0:T(8,128)(2,1)}, bf16[512,512]{1,0:T(8,128)(2,1)S(1)}, u32[]{:S(2)}) copy-start(bf16[512,512]{1,0:T(8,128)(2,1)S(1)} %get-tuple-element.49.gr_ref) | copy-start | bytes 1572868
  101.9 8.5 %collective-permute-start.5 = (bf16[1,32,512]{2,1,0:T(8,128)(2,1)S(1)}, bf16[1,32,512]{2,1,0:T(8,128)(2,1)S(1)}, u32[]{:S(2)}, u32[]{:S(2)}) collective-permute-start(bf16[1,32,512]{2,1,0:T(8,128)(2,1)S(1)} %get-tuple-element.73), channel_id=1, source_target_pairs={{8,0},{16,8},{24,16},{32,24},{40,32},{48,40},{56,48},{64,56},{72,6... | collective-permute-start | bytes 98312 | tf_op jit(solution)/shard_map/ppermute | solution.py:51
  103.2 7.2 %collective-permute-start.4 = (bf16[1,32,512]{2,1,0:T(8,128)(2,1)S(1)}, bf16[1,32,512]{2,1,0:T(8,128)(2,1)S(1)}, u32[]{:S(2)}, u32[]{:S(2)}) collective-permute-start(bf16[1,32,512]{2,1,0:T(8,128)(2,1)S(1)} %get-tuple-element.74), channel_id=1, source_target_pairs={{0,8},{8,16},{16,24},{24,32},{32,40},{40,48},{48,56},{56,64},{64,7... | collective-permute-start | bytes 98312 | tf_op jit(solution)/shard_map/ppermute | solution.py:51
  110.1 10.9 %collective-permute-start.8 = (bf16[1024,512]{1,0:T(8,128)(2,1)S(1)}, bf16[1024,512]{1,0:T(8,128)(2,1)S(1)}, u32[]{:S(2)}, u32[]{:S(2)}) collective-permute-start(bf16[1024,512]{1,0:T(8,128)(2,1)S(1)} %get-tuple-element.54), channel_id=1, source_target_pairs={{0,8},{1,9},{2,10},{3,11},{4,12},{5,13},{6,14},{7,15},{8,0},{9,1},... | collective-permute-start | bytes 3145736 | tf_op jit(solution)/shard_map/ppermute | solution.py:717
  110.5 5.9 %collective-permute-start.7 = (bf16[18,1,512]{2,1,0:T(2,128)(2,1)S(1)}, bf16[18,1,512]{2,1,0:T(2,128)(2,1)S(1)}, u32[]{:S(2)}, u32[]{:S(2)}) collective-permute-start(bf16[18,1,512]{2,1,0:T(2,128)(2,1)S(1)} %pad_maximum_fusion.6), channel_id=1, source_target_pairs={{0,1},{1,2},{2,3},{3,4},{4,5},{5,6},{6,7},{8,9},{9,10},{10,11},{11... | collective-permute-start | bytes 55304 | tf_op jit(solution)/shard_map/ppermute | solution.py:51
  113.5 7.4 %collective-permute-start.6 = (bf16[18,1,512]{2,1,0:T(2,128)(2,1)S(1)}, bf16[18,1,512]{2,1,0:T(2,128)(2,1)S(1)}, u32[]{:S(2)}, u32[]{:S(2)}) collective-permute-start(bf16[18,1,512]{2,1,0:T(2,128)(2,1)S(1)} %pad_maximum_fusion.5), channel_id=1, source_target_pairs={{1,0},{2,1},{3,2},{4,3},{5,4},{6,5},{7,6},{9,8},{10,9},{11,10},{12... | collective-permute-start | bytes 55304 | tf_op jit(solution)/shard_map/ppermute | solution.py:51
  122.8 10.0 %copy-start.2 = (bf16[512,512]{1,0:T(8,128)(2,1)S(1)}, bf16[512,512]{1,0:T(8,128)(2,1)}, u32[]{:S(2)}) copy-start(bf16[512,512]{1,0:T(8,128)(2,1)} %copy-done.1) | copy-start | bytes 1572868
  122.8 37.5 %all-to-all-start.2 = ((bf16[64,32,512]{2,1,0:T(8,128)(2,1)}), bf16[64,32,512]{2,1,0:T(8,128)(2,1)}, u32[]{:S(2)}, u32[]{:S(2)}) async-start(bf16[64,32,512]{2,1,0:T(8,128)(2,1)} %pad_maximum_fusion), calls=%async_computation.2 | async-start | bytes 4194304 | tf_op jit(solution)/shard_map/all_to_all | solution.py:45
  149.0 3.1 %collective-permute-start.10 = (bf16[1024,640]{1,0:T(8,128)(2,1)S(1)}, bf16[1024,640]{1,0:T(8,128)(2,1)S(1)}, u32[]{:S(2)}, u32[]{:S(2)}) collective-permute-start(bf16[1024,640]{1,0:T(8,128)(2,1)S(1)} %get-tuple-element.65), channel_id=1, source_target_pairs={{0,8},{1,9},{2,10},{3,11},{4,12},{5,13},{6,14},{7,15},{8,0},{9,1},... | collective-permute-start | bytes 3932168 | tf_op jit(solution)/shard_map/ppermute | solution.py:717
  160.3 25.0 %all-to-all-start.3 = ((bf16[64,16,640]{2,1,0:T(8,128)(2,1)}), bf16[64,16,640]{2,1,0:T(8,128)(2,1)S(1)}, u32[]{:S(2)}, u32[]{:S(2)}) async-start(bf16[64,16,640]{2,1,0:T(8,128)(2,1)} %bitcast.23), calls=%async_computation.3 | async-start | bytes 2621440 | tf_op jit(solution)/shard_map/all_to_all | solution.py:45

commit v5 on v4

--- a/solution.py
+++ b/solution.py
@@ -51,21 +51,28 @@
     return lax.ppermute(x, axis, pairs)
 
 
-def halo(x, width, ahead):
+def halo(x, width, ahead, beside):
     rows, cols, chans = x.shape
     above = shift(x[rows - width :], "row", 1)
     below = shift(x[:width], "row", -1)
     above, below, _ = lax.optimization_barrier((above, below, ahead))
-    to_right = jnp.concatenate(
-        [above[:, cols - width :], x[:, cols - width :], below[:, cols - width :]], 0
-    )
-    to_left = jnp.concatenate([above[:, :width], x[:, :width], below[:, :width]], 0)
-    left = shift(to_right, "col", 1)
-    right = shift(to_left, "col", -1)
-    gap = jnp.zeros((rows + 2 * width, 8 - 2 * width, chans), x.dtype)
-    sides = jnp.concatenate([right, gap, left], 1)
-    flat = [v.reshape(-1, chans) for v in (above, below, sides)]
-    return jnp.concatenate(flat, 0)
+    flat = lambda v: v.reshape(-1, chans)
+
+    def column(at, other):
+        parts = [above[:, at], x[:, at], below[:, at]]
+        return jnp.concatenate([flat(p) for p in parts] + [beside[:, other]], 0)
+
+    left = shift(column(slice(cols - width, cols), cols - 1), "col", 1)
+    right = shift(column(slice(0, width), 0), "col", -1)
+    n = (rows + 2 * width) * width
+
+    def sides(right, left, width):
+        right, left = [v.reshape(-1, width, chans) for v in (right, left)]
+        gap = jnp.zeros((right.shape[0], 8 - 2 * width, chans), x.dtype)
+        return flat(jnp.concatenate([right, gap, left], 1))
+
+    strips = [flat(above), flat(below), sides(right[:n], left[:n], width)]
+    return jnp.concatenate(strips, 0), sides(right[n:], left[n:], 1)
 
 
 def place(wide, centre, strips, width, rows, cols):
@@ -132,7 +139,7 @@
     return pltpu.roll(x, by % x.shape[0], 0)
 
 
-def expand_kernel(x_ref, we_ref, *refs):
+def expand_kernel(apply, x_ref, we_ref, *refs):
     act_out, normed = refs[-2:]
 
     @pl.when(pl.program_id(0) == 0)
@@ -141,18 +148,18 @@
 
     for tile in range(0, x_ref.shape[0], 128):
         at = slice(tile, tile + 128)
-        act_out[at, :] = gelu(dot(normed[at, :], we_ref[...])).astype(BF)
-
-
-def expand_block(x, w_expand, part, parts, held=None):
+        act_out[at, :] = apply(dot(normed[at, :], we_ref[...])).astype(BF)
+
+
+def expand_block(x, w_expand, apply, part, parts, held=None):
     tokens, width = x.shape
     hid = w_expand.shape[1]
     lanes = 512
     steps = hid // lanes // parts
     held = [] if held is None else [held]
     return pl.pallas_call(
-        expand_kernel,
-        name="expand",
+        functools.partial(expand_kernel, apply),
+        name=apply.__name__ + "_expand",
         grid=(steps,),
         in_specs=[
             pl.BlockSpec((tokens, width), lambda j: (0, 0)),
@@ -160,7 +167,7 @@
             *[pl.BlockSpec(memory_space=pl.ANY) for _ in held],
         ],
         out_specs=pl.BlockSpec((tokens, lanes), lambda j: (0, j + part * steps)),
-        out_shape=jax.ShapeDtypeStruct((tokens, hid), BF),
+        out_shape=pltpu.HBM((tokens, hid), BF),
         scratch_shapes=[pltpu.VMEM((tokens, width), BF)],
         input_output_aliases={2: 0} if held else {},
         compiler_params=pltpu.CompilerParams(vmem_limit_bytes=8 * MIB),
@@ -277,84 +284,103 @@
         cost_estimate=pl.CostEstimate(
             flops=2 * 700 * 512 * 2048, bytes_accessed=10 * 2**20, transcendentals=2**20
         ),
-    )(*in_hbm(x), strips, *in_hbm(go), act, *in_hbm(w_expand, w_depthwise, w_project))
+    )(*in_hbm(x), strips, *in_hbm(go, act, w_expand, w_depthwise, w_project))
+
+
+SLOPES = 512
 
 
 def slopes_kernel(
-    x_ref, strips_ref, we_ref, wd_ref, act_out, slope_c_out, slope_e_out, normed, normed_s, act
+    strips_ref, centre_ref, we_ref, wd_ref, wp_ref,
+    act_out, slope_out, resid_out,
+    normed, edge, beside, acc,
 ):
     rows, cols = 16, 32
 
     @pl.when(pl.program_id(0) == 0)
     def _():
-        normed[...] = normalize(x_ref[...].astype(F32))[0].astype(BF)
-        normed_s[...] = normalize(strips_ref[...].astype(F32))[0].astype(BF)
-
-    for tile in range(0, x_ref.shape[0], 128):
-        at = slice(tile, tile + 128)
-        pre = dot(normed[at, :], we_ref[...])
-        slope_e_out[at, :] = gelu_slope(pre).astype(BF)
-        act[2 + tile // cols : 2 + (tile + 128) // cols, 0:cols, :] = (
-            gelu(pre).astype(BF).astype(F32).reshape(128 // cols, cols, CHUNK)
-        )
-    strips = gelu(dot(normed_s[...], we_ref[...])).astype(BF).astype(F32)
-    place(act, None, strips, 2, rows, cols)
-    act_out[...] = act[1 : rows + 3].reshape(act_out.shape).astype(BF)
-    for lo in range(0, CHUNK, 128):
+        acc[...] = jnp.zeros(acc.shape, F32)
+        normed[...] = normalize(strips_ref[...].astype(F32))[0].astype(BF)
+
+    edge[...] = gelu(dot(normed[...], we_ref[...]))
+    for lo in range(0, SLOPES, 128):
         lanes = slice(lo, lo + 128)
         taps = [wd_ref[k : k + 1, lanes].astype(F32) for k in range(9)]
-        lines = [act[0, :, lanes], act[1, :, lanes]]
+
+        def line(r):
+            if r < 2:
+                centre = edge[r * cols : (r + 1) * cols, lanes]
+            elif r < rows + 2:
+                centre = centre_ref[(r - 2) * cols : (r - 1) * cols, lanes].astype(F32)
+            else:
+                centre = edge[(r - rows) * cols : (r - rows + 1) * cols, lanes]
+            side = edge[4 * cols + 8 * r : 4 * cols + 8 * (r + 1), lanes]
+            return jnp.concatenate([centre, side], 0)
+
+        lines = [line(0), line(1)]
         held = None
         for r in range(rows + 2):
-            lines = lines[-2:] + [act[r + 2, :, lanes]]
+            lines = lines[-2:] + [line(r + 2)]
             sums = [sum(lines[i] * taps[3 * i + j] for i in range(3)) for j in range(3)]
-            slope = gelu_slope(sums[1] + roll(sums[0], 1) + roll(sums[2], -1))
+            conv = sums[1] + roll(sums[0], 1) + roll(sums[2], -1)
+            slope = gelu_slope(conv)
+            if 1 <= r <= rows:
+                beside[8 * (r - 1) : 8 * r, lanes] = gelu(conv[cols:])
             if r % 2:
-                pair = jnp.concatenate([held, slope], 0).astype(BF)
-                slope_c_out[(r - 1) * WIDE : (r + 1) * WIDE, lanes] = pair
+                at = slice((r - 1) * WIDE, (r + 1) * WIDE)
+                act_out[at, lanes] = jnp.concatenate(lines[:2], 0).astype(BF)
+                slope_out[at, lanes] = jnp.concatenate([held, slope], 0).astype(BF)
             held = slope
-
-
-def slopes_block(x, strips, w_expand, w_depthwise):
-    tokens, width = x.shape
-    hid = w_expand.shape[1]
-    rows, cols = 16, 32
+    acc[...] += dot(beside[...].astype(BF), wp_ref[...])
+
+    @pl.when(pl.program_id(0) == pl.num_programs(0) - 1)
+    def _():
+        at = 2 * (2 * cols) + 2 * 8
+        resid_out[...] = (strips_ref[at : at + 8 * rows, :].astype(F32) + acc[...]).astype(BF)
+
+
+def slopes_block(strips, centre, w_expand, w_depthwise, w_project):
+    tokens, hid = centre.shape
+    width = strips.shape[1]
+    rows = 16
     wide = (rows + 2) * WIDE
-    whole = lambda a: pl.BlockSpec(a.shape, lambda j: (0,) * a.ndim)
     return pl.pallas_call(
         slopes_kernel,
         name="gelu_slopes",
-        grid=(hid // CHUNK,),
+        grid=(hid // SLOPES,),
         in_specs=[
-            whole(x), whole(strips),
-            pl.BlockSpec((width, CHUNK), lambda j: (0, j)),
-            pl.BlockSpec((9, CHUNK), lambda j: (0, j)),
+            pl.BlockSpec(strips.shape, lambda j: (0, 0)),
+            pl.BlockSpec((tokens, SLOPES), lambda j: (0, j)),
+            pl.BlockSpec((width, SLOPES), lambda j: (0, j)),
+            pl.BlockSpec((9, SLOPES), lambda j: (0, j)),
+            pl.BlockSpec((SLOPES, width), lambda j: (j, 0)),
         ],
         out_specs=[
-            pl.BlockSpec((wide, CHUNK), lambda j: (0, j)),
-            pl.BlockSpec((wide, CHUNK), lambda j: (0, j)),
-            pl.BlockSpec((tokens, CHUNK), lambda j: (0, j)),
+            pl.BlockSpec((wide, SLOPES), lambda j: (0, j)),
+            pl.BlockSpec((wide, SLOPES), lambda j: (0, j)),
+            pl.BlockSpec((8 * rows, width), lambda j: (0, 0)),
         ],
         out_shape=[
             pltpu.HBM((wide, hid), BF),
             pltpu.HBM((wide, hid), BF),
-            pltpu.HBM((tokens, hid), BF),
+            pltpu.HBM((8 * rows, width), BF),
         ],
         scratch_shapes=[
-            pltpu.VMEM((tokens, width), BF),
             pltpu.VMEM(strips.shape, BF),
-            pltpu.VMEM((rows + 4, WIDE, CHUNK), F32),
-        ],
-        compiler_params=pltpu.CompilerParams(vmem_limit_bytes=16 * MIB),
+            pltpu.VMEM((strips.shape[0], SLOPES), F32),
+            pltpu.VMEM((8 * rows, SLOPES), F32),
+            pltpu.VMEM((8 * rows, width), F32),
+        ],
+        compiler_params=pltpu.CompilerParams(vmem_limit_bytes=18 * MIB),
         cost_estimate=pl.CostEstimate(
             flops=2 * 10**10, bytes_accessed=12 * 2**20, transcendentals=3 * 2**20
         ),
-    )(*in_hbm(x), strips, *in_hbm(w_expand, w_depthwise))
+    )(strips, *in_hbm(centre, w_expand, w_depthwise, w_project))
 
 
 def attention_kernel(
-    in_ref, wq_hbm, wo_hbm, send_hbm, gq_hbm, att_hbm,
-    wq, wo, qkv, gatt, att, gq, send, gqb, attended, sems,
+    col_ref, in_ref, wq_hbm, wo_hbm, send_hbm, gq_hbm, att_hbm,
+    wq, wo, qkv, gatt, att, gq, send, gqb, attended, edge, sems,
 ):
     tokens, width = attended.shape
     groups = 8
@@ -419,30 +445,40 @@
     gqb[...] = jnp.concatenate([gq[i] for i in range(3 * quads)], 1).astype(BF)
     store_gq = pltpu.make_async_copy(gqb, gq_hbm, sems.at[3])
     store_gq.start()
-    stores = []
-    for half in range(2):
-        at = pl.ds(half * tokens // 2, tokens // 2)
-        rows = slice(half * tokens // 2, (half + 1) * tokens // 2)
-        send[rows, 0:width] = dot(attended[rows, :], wo[...]).astype(BF)
-        send[rows, width:] = dot_nt(gqb[rows, :], wq[...]).astype(BF)
-        store = pltpu.make_async_copy(send.at[at], send_hbm.at[at], sems.at[4 + half])
-        store.start()
-        stores.append(store)
-    for store in [store_att, store_gq, *stores]:
+    grad = dot_nt(gqb[...], wq[...])
+    send[:, width : 2 * width] = grad.astype(BF)
+    put(gatt, 0, grad)
+    place = lax.broadcasted_iota(jnp.int32, (members, 128), 0) % 8
+    last = col_ref[0] % 4 == 3
+    for i in range(quads):
+        first_col = gatt[i, pl.ds(0, members, stride=groups), :]
+        last_col = gatt[i, pl.ds(groups - 1, members, stride=groups), :]
+        to_left = jnp.where(place == 7, 0.0, roll(first_col, -1))
+        to_right = jnp.where(place == 0, 0.0, roll(last_col, 1))
+        found = jnp.where(last, to_right, to_left)
+        edge[pl.ds(2 * i, members, stride=groups), :] = found
+        edge[pl.ds(2 * i + 1, members, stride=groups), :] = pltpu.roll(found, 64, 1)
+    send[:, 2 * width :] = edge[...].astype(BF)
+    send[:, 0:width] = dot(attended[...], wo[...]).astype(BF)
+    store_send = pltpu.make_async_copy(send, send_hbm, sems.at[4])
+    store_send.start()
+    for store in [store_att, store_gq, store_send]:
         store.wait()
 
 
-def attention_block(arrived, w_qkv, w_out):
+def attention_block(col, arrived, w_qkv, w_out):
     tokens = arrived.shape[0]
     width = w_out.shape[0]
     anywhere = pl.BlockSpec(memory_space=pl.ANY)
     return pl.pallas_call(
         attention_kernel,
         name="grid_attention",
-        in_specs=[pl.BlockSpec(memory_space=pltpu.VMEM), anywhere, anywhere],
+        in_specs=[
+            pl.BlockSpec(memory_space=pltpu.SMEM), pl.BlockSpec(memory_space=pltpu.VMEM), anywhere, anywhere
+        ],
         out_specs=[anywhere] * 3,
         out_shape=[
-            pltpu.HBM((tokens, 2 * width), BF),
+            pltpu.HBM((tokens, 2 * width + 128), BF),
             pltpu.HBM((tokens, 3 * width), BF),
             pltpu.HBM((tokens, width), BF),
         ],
@@ -453,33 +489,62 @@
             pltpu.VMEM((width // 128, tokens, 128), F32),
             pltpu.VMEM((width // 128, tokens, 128), F32),
             pltpu.VMEM((3 * width // 128, tokens, 128), F32),
-            pltpu.VMEM((tokens, 2 * width), BF),
+            pltpu.VMEM((tokens, 2 * width + 128), BF),
             pltpu.VMEM((tokens, 3 * width), BF),
             pltpu.VMEM((tokens, width), BF),
-            pltpu.SemaphoreType.DMA((6,)),
+            pltpu.VMEM((tokens, 128), F32),
+            pltpu.SemaphoreType.DMA((5,)),
         ],
         compiler_params=pltpu.CompilerParams(vmem_limit_bytes=24 * MIB),
         cost_estimate=pl.CostEstimate(
             flops=2 * 512 * 512 * 512 * 8, bytes_accessed=7 * 2**20, transcendentals=2**20
         ),
-    )(arrived, *in_hbm(w_qkv, w_out))
-
-
-def residual_kernel(home_ref, resid_ref, go_ref, out_ref, gr_ref):
-    width = resid_ref.shape[1]
+    )(col, arrived, *in_hbm(w_qkv, w_out))
+
+
+def residual_kernel(
+    home_ref, resid_ref, go_ref, resid_s_ref, go_s_ref, out_ref, gr_ref, side_out, first_out, last_out,
+    packed, side,
+):
+    tokens, width = resid_ref.shape
+    rows, cols = 16, 32
     resid = resid_ref[...].astype(F32)
     out_ref[...] = (resid + home_ref[:, 0:width].astype(F32)).astype(BF)
-    back = normalize_back(resid, home_ref[:, width:].astype(F32))
-    gr_ref[...] = (go_ref[...].astype(F32) + back).astype(BF)
-
-
-def residual_block(home, resid, go):
+    back = normalize_back(resid, home_ref[:, width : 2 * width].astype(F32))
+    gr = (go_ref[...].astype(F32) + back).astype(BF)
+    gr_ref[...] = gr
+    packed[...] = home_ref[:, 2 * width :].astype(F32)
+    side[...] = jnp.zeros(side.shape, F32)
+    low = lax.broadcasted_iota(jnp.int32, (rows, 128), 1) < 64
+    for i in range(width // 128):
+        for at, start in ((0, 0), (7, cols - 8)):
+            even = packed[pl.ds(start + 2 * i, rows, stride=cols), :]
+            odd = packed[pl.ds(start + 2 * i + 1, rows, stride=cols), :]
+            side[i, pl.ds(at, rows, stride=8), :] = jnp.where(low, even, pltpu.roll(odd, 64, 1))
+    grad = jnp.concatenate([side[i] for i in range(width // 128)], 1)
+    back = normalize_back(resid_s_ref[...].astype(F32), grad)
+    gr_s = (go_s_ref[...].astype(F32) + back).astype(BF).astype(F32)
+    side_out[...] = gr_s.astype(BF)
+    none = jnp.zeros((8, width), F32)
+    own = gr.astype(F32)
+    first_out[...] = jnp.concatenate([own[0:cols], gr_s[0:8], none], 0).astype(BF)
+    last_out[...] = jnp.concatenate([own[tokens - cols :], gr_s[8 * rows - 8 :], none], 0).astype(BF)
+
+
+def residual_block(home, resid, go, resid_s, go_s):
+    tokens, width = resid.shape
+    beside = resid_s.shape[0]
+    shapes = [(tokens, width), (tokens, width), (beside, width), (48, width), (48, width)]
     return pl.pallas_call(
         residual_kernel,
         name="residual",
-        out_shape=[jax.ShapeDtypeStruct(resid.shape, BF)] * 2,
-        compiler_params=pltpu.CompilerParams(vmem_limit_bytes=8 * MIB),
-    )(home, *in_hbm(resid, go))
+        out_shape=[jax.ShapeDtypeStruct(shape, BF) for shape in shapes],
+        scratch_shapes=[
+            pltpu.VMEM((tokens, 128), F32),
+            pltpu.VMEM((width // 128, beside, 128), F32),
+        ],
+        compiler_params=pltpu.CompilerParams(vmem_limit_bytes=12 * MIB),
+    )(home, *in_hbm(resid, go, resid_s), go_s)
 
 
 def split_by_core(core, full, mine_out, other_out):
@@ -493,7 +558,8 @@
 
 
 def backward_kernel(
-    core_ref, x_ref, gr_ref, strips_ref, act_ref, slope_c_ref, slope_e_ref, wd_ref, wp_ref,
+    core_ref, x_ref, gr_ref, above_ref, below_ref, side_ref, act_ref, slope_c_ref, slope_e_ref,
+    wd_ref, wp_ref,
     gpre, mine_out, other_out,
     wide, grad_wide, normed, gmid, act, full, taps_t,
 ):
@@ -503,7 +569,10 @@
 
     @pl.when(step == 0)
     def _():
-        place(wide, gr_ref[...].astype(F32), strips_ref[...].astype(F32), 1, rows, cols)
+        wide[0] = above_ref[0:WIDE, :].astype(F32)
+        wide[rows + 1] = below_ref[0:WIDE, :].astype(F32)
+        wide[1 : 1 + rows, 0:cols, :] = gr_ref[...].astype(F32).reshape(rows, cols, width)
+        wide[1 : 1 + rows, cols:, :] = side_ref[...].astype(F32).reshape(rows, 8, width)
         grad_wide[...] = wide[...].reshape(grad_wide.shape).astype(BF)
         normed[...] = normalize(x_ref[...].astype(F32))[0].astype(BF)
         taps_t[...] = jnp.zeros(taps_t.shape, F32)
@@ -537,7 +606,7 @@
     split_by_core(core_ref[0], full, mine_out, other_out)
 
 
-def backward_block(core, x, gr, strips, act, slope_c, slope_e, w_depthwise, w_project):
+def backward_block(core, x, gr, near, act, slope_c, slope_e, w_depthwise, w_project):
     tokens, width = x.shape
     hid = w_project.shape[0]
     rows, cols = 16, 32
@@ -549,7 +618,7 @@
             num_scalar_prefetch=1,
             grid=(hid // CHUNK,),
             in_specs=[
-                whole(x), whole(gr), whole(strips),
+                whole(x), whole(gr), *[whole(a) for a in near],
                 pl.BlockSpec(((rows + 2) * WIDE, CHUNK), lambda j, c: (0, j)),
                 pl.BlockSpec(((rows + 2) * WIDE, CHUNK), lambda j, c: (0, j)),
                 pl.BlockSpec((tokens, CHUNK), lambda j, c: (0, j)),
@@ -580,7 +649,7 @@
         cost_estimate=pl.CostEstimate(
             flops=16 * 512 * 512 * 2048, bytes_accessed=20 * 2**20, transcendentals=2**20
         ),
-    )(core, *in_hbm(x), gr, strips, *in_hbm(act, slope_c, slope_e, w_depthwise, w_project))
+    )(core, *in_hbm(x), gr, *near, *in_hbm(act, slope_c, slope_e, w_depthwise, w_project))
 
 
 def input_kernel(gpre_ref, we_ref, x_ref, gr_ref, gx_out):
@@ -722,27 +791,30 @@
     _, rows, cols, width = block_input.shape
     tokens = rows * cols
     core = (lax.axis_index("row") % 2).astype(jnp.int32).reshape(1)
+    col = lax.axis_index("col").astype(jnp.int32).reshape(1)
     image = block_input[0]
     x = image.reshape(tokens, width)
     go = grad_out[0].reshape(tokens, width)
-    act0 = expand_block(x, w_expand, 0, 2)
-    centre = expand_block(x, w_expand, 1, 2, act0)
-    strips = halo(image, 2, act0)
+    act0 = expand_block(x, w_expand, gelu, 0, 2)
+    centre = expand_block(x, w_expand, gelu, 1, 2, act0)
+    strips, go_side = halo(image, 2, act0, grad_out[0])
     mid, resid, send = forward_block(x, strips, go, centre, w_expand, w_depthwise, w_project)
     arrived = across_chips(send.reshape(64, 8, 2 * width)).reshape(tokens, 2 * width)
-    slopes = slopes_block(x, strips, w_expand, w_depthwise)
-    arrived, (act, slope_c, slope_e) = lax.optimization_barrier((arrived, slopes))
-    back, gqkv, attended = attention_block(arrived, w_qkv, w_out)
-    home = across_chips(back.reshape(64, 8, 2 * width)).reshape(tokens, 2 * width)
+    slopes = slopes_block(strips, centre, w_expand, w_depthwise, w_project)
+    arrived, (act, slope_c, resid_side) = lax.optimization_barrier((arrived, slopes))
+    back, gqkv, attended = attention_block(col, arrived, w_qkv, w_out)
+    home = across_chips(back.reshape(64, 8, -1)).reshape(tokens, -1)
+    slope_e = expand_block(x, w_expand, gelu_slope, 0, 1)
+    home, slope_e = lax.optimization_barrier((home, slope_e))
     attention_pair = add_pair(*attention_grads(core, arrived, gqkv, attended))
-    out, gr = residual_block(home, resid, go)
-    mine, other = project_grads(core, mid, gr)
-    strips = halo(gr.reshape(rows, cols, width), 1, mine)
-    first = jnp.concatenate([add_pair(mine, other), attention_pair], 1)
-    strips, first = lax.optimization_barrier((strips, first))
+    out, gr, side, first_row, last_row = residual_block(home, resid, go, resid_side, go_side)
+    above, below = shift(last_row, "row", 1), shift(first_row, "row", -1)
+    project_pair = add_pair(*project_grads(core, mid, gr))
+    first = jnp.concatenate([project_pair, attention_pair], 1)
+    above, below, first = lax.optimization_barrier((above, below, first))
     first = across_chips(first)
     gpre, mine, other = backward_block(
-        core, x, gr, strips, act, slope_c, slope_e, w_depthwise, w_project
+        core, x, gr, (above, below, side), act, slope_c, slope_e, w_depthwise, w_project
     )
     gx = input_grads(gpre, w_expand, x, gr)
     second = add_pair(mine, other)

time: 187 us -> 184 us (0.984)
  waiting for transfers between devices: 42.4 us -> 31.8 us
  Pallas kernels: 76.8 us -> 82.2 us
    ppermute x8 -> x6, waiting for transfers between devices: 8.04 us -> 0.19 us  [shift(): return lax.ppermute(x, axis, pairs)]
    pallas_call x3 -> x4, Pallas kernels: 20.5 us -> 25.1 us  [the longest x3 12.8 us: expand_block(): pl.pallas_call(functools.partial(expand_kernel, apply), name=apply.__name...]
    ppermute x8 -> x6, starting transfers between devices: 19.3 us -> 15.4 us  [shift(): return lax.ppermute(x, axis, pairs)]
    ppermute x3, starting transfers between devices: 0.41 us -> 4.14 us  [add_pair(): got = lax.ppermute(other, AX, other_core())]
    all_to_all x4, waiting for transfers between devices: 31.3 us -> 29 us  [across_chips(): lax.all_to_all(x, AX, 0, 0, tiled=True, axis_index_groups=device_groups(C...]
  transfers between devices with their start and end apart: 15 -> 13, of which waited for: 7 -> 6; matrix products, arithmetic and copies ran while one was open for 4% -> 6% of each run, Pallas kernels for 29% -> 32%
where the time goes in v5:
time: 184 us; the launch traced here: 182 us
  Pallas kernels  82.2 us (45%)
  starting transfers between devices  54.1 us (29%)
  waiting for transfers between devices  31.8 us (17%)
  other arithmetic  7.04 us (4%)
  local copies, waits for them, and re-layouts  5.47 us (3%)
    all_to_all x4, starting transfers between devices, across_chips(): lax.all_to_all(x, AX, 0, 0, tiled=True, axis_index_groups=device_groups(C...  34.6 us
    all_to_all x4, waiting for transfers between devices, across_chips(): lax.all_to_all(x, AX, 0, 0, tiled=True, axis_index_groups=device_groups(C...  29 us
    pallas_call x1, Pallas kernels, backward_block(): pl.pallas_call(backward_kernel, name='mbconv_backward', grid_spec=pltpu.P...  16.2 us
    ppermute x6, starting transfers between devices, shift(): return lax.ppermute(x, axis, pairs)  15.4 us
    pallas_call x3, Pallas kernels, expand_block(): pl.pallas_call(functools.partial(expand_kernel, apply), name=apply.__name...  12.8 us
    pallas_call x1, Pallas kernels, slopes_block(): pl.pallas_call(slopes_kernel, name='gelu_slopes', grid=(hid // SLOPES,),...  12.3 us
    pallas_call x1, Pallas kernels, attention_block(): pl.pallas_call(attention_kernel, name='grid_attention', in_specs=[pl.Bloc...  11.6 us
    pallas_call x1, Pallas kernels, forward_block(): pl.pallas_call(forward_kernel, name='mbconv_forward', grid=(hid // FORWAR...  10.9 us
  transfers between devices with their start and end apart: 13, of which 6 were waited for; matrix products, arithmetic and copies ran while one was open for 6% of the time, Pallas kernels for 32%

profile of v5, /device:TPU:0, one launch (start us, length us, event | category | flops | bytes accessed | tf_op | source)
XLA Modules:
  0.0 181.6 jit_solution(7564001609372693894)
XLA Ops:
  2.8 3.0 %collective-permute-start = (bf16[2,32,512]{2,1,0:T(8,128)(2,1)S(1)}, bf16[2,32,512]{2,1,0:T(8,128)(2,1)S(1)}, u32[]{:S(2)}, u32[]{:S(2)}) collective-permute-start(bf16[2,32,512]{2,1,0:T(8,128)(2,1)S(1)} %get-tuple-element.84), channel_id=1, source_target_pairs={{0,8},{8,16},{16,24},{24,32},{32,40},{40,48},{48,56},{56,64},{64,7... | collective-permute-start | bytes 196616 | tf_op jit(solution)/shard_map/ppermute | solution.py:51
  8.2 3.4 %gelu_expand.2.refs_0_ = bf16[512,2048]{1,0:T(8,128)(2,1)} custom-call(bf16[512,512]{1,0:T(8,128)(2,1)} %bitcast.52, bf16[512,2048]{1,0:T(8,128)(2,1)} %we_ref.11), custom_call_target="tpu_custom_call" | custom-call | flops 4294967296 | bytes 3145728 | tf_op jit(solution)/shard_map/gelu_expand/pallas_call | solution.py:160
  13.3 6.1 %collective-permute-start.3 = (bf16[56,512]{1,0:T(8,128)(2,1)S(1)}, bf16[56,512]{1,0:T(8,128)(2,1)S(1)}, u32[]{:S(2)}, u32[]{:S(2)}) collective-permute-start(bf16[56,512]{1,0:T(8,128)(2,1)S(1)} %pad_maximum_fusion.3), channel_id=1, source_target_pairs={{0,1},{1,2},{2,3},{3,4},{4,5},{5,6},{6,7},{8,9},{9,10},{10,11},{11... | collective-permute-start | bytes 172040 | tf_op jit(solution)/shard_map/ppermute | solution.py:51
  19.4 3.4 %gelu_expand.3.act_ref.centre_ref = bf16[512,2048]{1,0:T(8,128)(2,1)} custom-call(bf16[512,512]{1,0:T(8,128)(2,1)} %bitcast.53, bf16[512,2048]{1,0:T(8,128)(2,1)} %we_ref.11, bf16[512,2048]{1,0:T(8,128)(2,1)} %gelu_expand.2.refs_0_), custom_call_target="tpu_custom_call", output_to_operand_aliasing={{}: (2, {})} | custom-call | flops 4294967296 | bytes 3145728 | tf_op jit(solution)/shard_map/gelu_expand/pallas_call | solution.py:160
  23.1 10.9 %mbconv_forward.1 = (bf16[512,2048]{1,0:T(8,128)(2,1)}, bf16[512,512]{1,0:T(8,128)(2,1)}, bf16[512,1024]{1,0:T(8,128)(2,1)}) custom-call(bf16[512,512]{1,0:T(8,128)(2,1)} %bitcast.54, bf16[288,512]{1,0:T(8,128)(2,1)S(1)} %pad_maximum_fusion.1.strips_ref, bf16[512,512]{1,0:T(8,128)(2,1)} %bitcast.45, bf16[512,2048]{1,0:T(8,128)(2,1)} %gelu_expand.3.act_ref.centre_ref, ...), custom_call_target="tpu_custom_call" | custom-call | flops 1468006400 | bytes 10485760 | tf_op jit(solution)/shard_map/mbconv_forward/pallas_call | solution.py:254
  34.0 12.4 %all-to-all-start = ((bf16[64,8,1024]{2,1,0:T(8,128)(2,1)}), bf16[64,8,1024]{2,1,0:T(8,128)(2,1)S(1)}, u32[]{:S(2)}, u32[]{:S(2)}) async-start(bf16[64,8,1024]{2,1,0:T(8,128)(2,1)} %bitcast.50), calls=%async_computation | async-start | bytes 2097152 | tf_op jit(solution)/shard_map/all_to_all | solution.py:45
  46.5 12.3 %gelu_slopes.1 = (bf16[720,2048]{1,0:T(8,128)(2,1)}, bf16[720,2048]{1,0:T(8,128)(2,1)}, bf16[128,512]{1,0:T(8,128)(2,1)}) custom-call(bf16[288,512]{1,0:T(8,128)(2,1)S(1)} %pad_maximum_fusion.1.strips_ref, bf16[512,2048]{1,0:T(8,128)(2,1)} %gelu_expand.3.act_ref.centre_ref, bf16[512,2048]{1,0:T(8,128)(2,1)} %we_ref.11, bf16[9,2048]{1,0:T(8,128)(2,1)} %wd_ref.5, ...), custom_call_target="tpu_custom_call" | custom-call | flops 20000000000 | bytes 12582912 | tf_op jit(solution)/shard_map/gelu_slopes/pallas_call | solution.py:347
  58.7 5.6 %all-to-all-done = bf16[64,8,1024]{2,1,0:T(8,128)(2,1)S(1)} async-done(((bf16[64,8,1024]{2,1,0:T(8,128)(2,1)}), bf16[64,8,1024]{2,1,0:T(8,128)(2,1)S(1)}, u32[]{:S(2)}, u32[]{:S(2)}) %all-to-all-start) | async-done | bytes 1048608 | tf_op jit(solution)/shard_map/all_to_all | solution.py:45
  64.4 11.6 %grid_attention.1 = (bf16[512,1152]{1,0:T(8,128)(2,1)}, bf16[512,1536]{1,0:T(8,128)(2,1)}, bf16[512,512]{1,0:T(8,128)(2,1)}) custom-call(s32[1]{0:T(128)} %bitcast.col_ref, bf16[512,1024]{1,0:T(8,128)(2,1)S(1)} %bitcast.43, bf16[512,1536]{1,0:T(8,128)(2,1)} %wq_hbm.1, bf16[512,512]{1,0:T(8,128)(2,1)} %wo_hbm.1), custom_call_target="tpu_custom_call" | custom-call | flops 2147483648 | bytes 7340032 | tf_op jit(solution)/shard_map/grid_attention/pallas_call | solution.py:473
  76.0 5.8 %all-to-all-start.1 = ((bf16[64,8,1152]{2,1,0:T(8,128)(2,1)}), bf16[64,8,1152]{2,1,0:T(8,128)(2,1)S(1)}, u32[]{:S(2)}, u32[]{:S(2)}) async-start(bf16[64,8,1152]{2,1,0:T(8,128)(2,1)} %bitcast.49), calls=%async_computation.1 | async-start | bytes 2359296 | tf_op jit(solution)/shard_map/all_to_all | solution.py:45
  81.8 5.9 %gelu_slope_expand.1.slope_e_ref = bf16[512,2048]{1,0:T(8,128)(2,1)} custom-call(bf16[512,512]{1,0:T(8,128)(2,1)} %bitcast.55, bf16[512,2048]{1,0:T(8,128)(2,1)} %we_ref.11), custom_call_target="tpu_custom_call" | custom-call | flops 4294967296 | bytes 3145728 | tf_op jit(solution)/shard_map/gelu_slope_expand/pallas_call | solution.py:160
  87.8 4.8 %attention_grads.1 = (f32[1024,512]{1,0:T(8,128)S(1)}, bf16[1024,512]{1,0:T(8,128)(2,1)}) custom-call(s32[1]{0:T(128)} %bitcast.20.core_ref, bf16[512,1024]{1,0:T(8,128)(2,1)} %bitcast.44, bf16[512,1536]{1,0:T(8,128)(2,1)} %get-tuple-element.61.gqkv_ref, bf16[512,512]{1,0:T(8,128)(2,1)} %get-tuple-element.62.att_ref), custom_call_target="tpu_custom_call" | custom-call | flops 1073741824 | bytes 8388608 | tf_op jit(solution)/shard_map/attention_grads/pallas_call | solution.py:762
  93.5 8.7 %all-to-all-done.1 = bf16[64,8,1152]{2,1,0:T(8,128)(2,1)S(1)} async-done(((bf16[64,8,1152]{2,1,0:T(8,128)(2,1)}), bf16[64,8,1152]{2,1,0:T(8,128)(2,1)S(1)}, u32[]{:S(2)}, u32[]{:S(2)}) %all-to-all-start.1) | async-done | bytes 1179680 | tf_op jit(solution)/shard_map/all_to_all | solution.py:45
  102.2 2.2 %residual.1 = (bf16[512,512]{1,0:T(8,128)(2,1)}, bf16[512,512]{1,0:T(8,128)(2,1)S(1)}, bf16[128,512]{1,0:T(8,128)(2,1)S(1)}, bf16[48,512]{1,0:T(8,128)(2,1)S(1)}, bf16[48,512]{1,0:T(8,128)(2,1)S(1)}) custom-call(bf16[512,1152]{1,0:T(8,128)(2,1)S(1)} %bitcast.42, bf16[512,512]{1,0:T(8,128)(2,1)} %get-tuple-element.52.resid_ref, bf16[512,512]{1,0:T(8,128)(2,1)} %bitcast.46, ...), custom_call_target="tpu_custom_call" | custom-call | tf_op jit(solution)/shard_map/residual/pallas_call | solution.py:538
  104.4 3.9 %grad_project.1 = (f32[1024,512]{1,0:T(8,128)S(1)}, bf16[1024,512]{1,0:T(8,128)(2,1)S(1)}) custom-call(s32[1]{0:T(128)} %bitcast.20.core_ref, bf16[512,2048]{1,0:T(8,128)(2,1)} %get-tuple-element.58.mid_ref, bf16[512,512]{1,0:T(8,128)(2,1)S(1)} %get-tuple-element.55.gr_ref), custom_call_target="tpu_custom_call" | custom-call | flops 1073741824 | bytes 7340032 | tf_op jit(solution)/shard_map/grad_project/pallas_call | solution.py:713
  110.0 2.4 %collective-permute-start.4 = (bf16[48,512]{1,0:T(8,128)(2,1)S(1)}, bf16[48,512]{1,0:T(8,128)(2,1)S(1)}, u32[]{:S(2)}, u32[]{:S(2)}) collective-permute-start(bf16[48,512]{1,0:T(8,128)(2,1)S(1)} %get-tuple-element.56), channel_id=1, source_target_pairs={{0,8},{8,16},{16,24},{24,32},{32,40},{40,48},{48,56},{56,64},{64,7... | collective-permute-start | bytes 147464 | tf_op jit(solution)/shard_map/ppermute | solution.py:51
  115.8 9.0 %all-to-all-start.2 = ((bf16[64,32,512]{2,1,0:T(8,128)(2,1)}), bf16[64,32,512]{2,1,0:T(8,128)(2,1)}, u32[]{:S(2)}, u32[]{:S(2)}) async-start(bf16[64,32,512]{2,1,0:T(8,128)(2,1)} %pad_maximum_fusion), calls=%async_computation.2 | async-start | bytes 4194304 | tf_op jit(solution)/shard_map/all_to_all | solution.py:45
  124.8 16.2 %mbconv_backward.1 = (bf16[512,2048]{1,0:T(8,128)(2,1)}, f32[1024,640]{1,0:T(8,128)S(1)}, bf16[1024,640]{1,0:T(8,128)(2,1)S(1)}) custom-call(s32[1]{0:T(128)} %bitcast.20.core_ref, bf16[512,512]{1,0:T(8,128)(2,1)} %bitcast.56, bf16[512,512]{1,0:T(8,128)(2,1)S(1)} %copy-done.2, bf16[48,512]{1,0:T(8,128)(2,1)S(1)} %collective-permute-done.4.above_ref, ...), custom_call_target="tpu_custom_call" | custom-call | flops 8589934592 | bytes 20971520 | tf_op jit(solution)/shard_map/mbconv_backward/pallas_call | solution.py:614
  141.0 3.2 %collective-permute-start.8 = (bf16[1024,640]{1,0:T(8,128)(2,1)S(1)}, bf16[1024,640]{1,0:T(8,128)(2,1)S(1)}, u32[]{:S(2)}, u32[]{:S(2)}) collective-permute-start(bf16[1024,640]{1,0:T(8,128)(2,1)S(1)} %get-tuple-element.73), channel_id=1, source_target_pairs={{0,8},{1,9},{2,10},{3,11},{4,12},{5,13},{6,14},{7,15},{8,0},{9,1},... | collective-permute-start | bytes 3932168 | tf_op jit(solution)/shard_map/ppermute | solution.py:786
  144.3 2.7 %collective-permute-done.8 = bf16[1024,640]{1,0:T(8,128)(2,1)S(1)} collective-permute-done((bf16[1024,640]{1,0:T(8,128)(2,1)S(1)}, bf16[1024,640]{1,0:T(8,128)(2,1)S(1)}, u32[]{:S(2)}, u32[]{:S(2)}) %collective-permute-start.8) | collective-permute-done | bytes 1310752 | tf_op jit(solution)/shard_map/ppermute | solution.py:786
  148.4 3.5 %all-to-all-done.2 = bf16[64,32,512]{2,1,0:T(8,128)(2,1)} async-done(((bf16[64,32,512]{2,1,0:T(8,128)(2,1)}), bf16[64,32,512]{2,1,0:T(8,128)(2,1)}, u32[]{:S(2)}, u32[]{:S(2)}) %all-to-all-start.2) | async-done | bytes 2097184 | tf_op jit(solution)/shard_map/all_to_all | solution.py:45
  151.9 7.3 %all-to-all-start.3 = ((bf16[64,16,640]{2,1,0:T(8,128)(2,1)}), bf16[64,16,640]{2,1,0:T(8,128)(2,1)S(1)}, u32[]{:S(2)}, u32[]{:S(2)}) async-start(bf16[64,16,640]{2,1,0:T(8,128)(2,1)} %bitcast.24), calls=%async_computation.3 | async-start | bytes 2621440 | tf_op jit(solution)/shard_map/all_to_all | solution.py:45
  159.3 6.6 %grad_input.1 = bf16[512,512]{1,0:T(8,128)(2,1)} custom-call(bf16[512,2048]{1,0:T(8,128)(2,1)} %get-tuple-element.71.gpre_ref, bf16[512,2048]{1,0:T(8,128)(2,1)} %we_ref.11, bf16[512,512]{1,0:T(8,128)(2,1)} %bitcast.57, bf16[512,512]{1,0:T(8,128)(2,1)} %copy-done.1), custom_call_target="tpu_custom_call" | custom-call | flops 2147483648 | bytes 6291456 | tf_op jit(solution)/shard_map/grad_input/pallas_call | solution.py:664
  169.7 11.1 %all-to-all-done.3.parts_ref = bf16[64,16,640]{2,1,0:T(8,128)(2,1)S(1)} async-done(((bf16[64,16,640]{2,1,0:T(8,128)(2,1)}), bf16[64,16,640]{2,1,0:T(8,128)(2,1)S(1)}, u32[]{:S(2)}, u32[]{:S(2)}) %all-to-all-start.3) | async-done | bytes 1310752 | tf_op jit(solution)/shard_map/all_to_all | solution.py:45
  (56 shorter events, 18.3 us)
Async XLA Ops:
  1.5 10.4 %collective-permute-start.1 = (bf16[2,32,512]{2,1,0:T(8,128)(2,1)S(1)}, bf16[2,32,512]{2,1,0:T(8,128)(2,1)S(1)}, u32[]{:S(2)}, u32[]{:S(2)}) collective-permute-start(bf16[2,32,512]{2,1,0:T(8,128)(2,1)S(1)} %get-tuple-element.83), channel_id=1, source_target_pairs={{8,0},{16,8},{24,16},{32,24},{40,32},{48,40},{56,48},{64,56},{72,6... | collective-permute-start | bytes 196616 | tf_op jit(solution)/shard_map/ppermute | solution.py:51
  2.8 9.1 %collective-permute-start = (bf16[2,32,512]{2,1,0:T(8,128)(2,1)S(1)}, bf16[2,32,512]{2,1,0:T(8,128)(2,1)S(1)}, u32[]{:S(2)}, u32[]{:S(2)}) collective-permute-start(bf16[2,32,512]{2,1,0:T(8,128)(2,1)S(1)} %get-tuple-element.84), channel_id=1, source_target_pairs={{0,8},{8,16},{16,24},{24,32},{32,40},{40,48},{48,56},{56,64},{64,7... | collective-permute-start | bytes 196616 | tf_op jit(solution)/shard_map/ppermute | solution.py:51
  12.0 10.8 %collective-permute-start.2 = (bf16[56,512]{1,0:T(8,128)(2,1)S(1)}, bf16[56,512]{1,0:T(8,128)(2,1)S(1)}, u32[]{:S(2)}, u32[]{:S(2)}) collective-permute-start(bf16[56,512]{1,0:T(8,128)(2,1)S(1)} %pad_maximum_fusion.2), channel_id=1, source_target_pairs={{1,0},{2,1},{3,2},{4,3},{5,4},{6,5},{7,6},{9,8},{10,9},{11,10},{12... | collective-permute-start | bytes 172040 | tf_op jit(solution)/shard_map/ppermute | solution.py:51
  13.3 9.5 %collective-permute-start.3 = (bf16[56,512]{1,0:T(8,128)(2,1)S(1)}, bf16[56,512]{1,0:T(8,128)(2,1)S(1)}, u32[]{:S(2)}, u32[]{:S(2)}) collective-permute-start(bf16[56,512]{1,0:T(8,128)(2,1)S(1)} %pad_maximum_fusion.3), channel_id=1, source_target_pairs={{0,1},{1,2},{2,3},{3,4},{4,5},{5,6},{6,7},{8,9},{9,10},{10,11},{11... | collective-permute-start | bytes 172040 | tf_op jit(solution)/shard_map/ppermute | solution.py:51
  34.0 30.4 %all-to-all-start = ((bf16[64,8,1024]{2,1,0:T(8,128)(2,1)}), bf16[64,8,1024]{2,1,0:T(8,128)(2,1)S(1)}, u32[]{:S(2)}, u32[]{:S(2)}) async-start(bf16[64,8,1024]{2,1,0:T(8,128)(2,1)} %bitcast.50), calls=%async_computation | async-start | bytes 2097152 | tf_op jit(solution)/shard_map/all_to_all | solution.py:45
  64.4 11.6 %copy-start = (bf16[64,8,1024]{2,1,0:T(8,128)(2,1)}, bf16[64,8,1024]{2,1,0:T(8,128)(2,1)S(1)}, u32[]{:S(2)}) copy-start(bf16[64,8,1024]{2,1,0:T(8,128)(2,1)S(1)} %all-to-all-done) | copy-start | bytes 3145732
  76.0 26.2 %all-to-all-start.1 = ((bf16[64,8,1152]{2,1,0:T(8,128)(2,1)}), bf16[64,8,1152]{2,1,0:T(8,128)(2,1)S(1)}, u32[]{:S(2)}, u32[]{:S(2)}) async-start(bf16[64,8,1152]{2,1,0:T(8,128)(2,1)} %bitcast.49), calls=%async_computation.1 | async-start | bytes 2359296 | tf_op jit(solution)/shard_map/all_to_all | solution.py:45
  92.5 15.9 %collective-permute-start.7 = (bf16[1024,512]{1,0:T(8,128)(2,1)}, bf16[1024,512]{1,0:T(8,128)(2,1)}, u32[]{:S(2)}, u32[]{:S(2)}) collective-permute-start(bf16[1024,512]{1,0:T(8,128)(2,1)} %get-tuple-element.64), channel_id=1, source_target_pairs={{0,8},{1,9},{2,10},{3,11},{4,12},{5,13},{6,14},{7,15},{8,0},{9,1},... | collective-permute-start | bytes 3145736 | tf_op jit(solution)/shard_map/ppermute | solution.py:786
  104.4 4.0 %copy-start.1 = (bf16[512,512]{1,0:T(8,128)(2,1)}, bf16[512,512]{1,0:T(8,128)(2,1)S(1)}, u32[]{:S(2)}) copy-start(bf16[512,512]{1,0:T(8,128)(2,1)S(1)} %get-tuple-element.55.gr_ref) | copy-start | bytes 1572868
  108.4 5.4 %collective-permute-start.6 = (bf16[1024,512]{1,0:T(8,128)(2,1)S(1)}, bf16[1024,512]{1,0:T(8,128)(2,1)S(1)}, u32[]{:S(2)}, u32[]{:S(2)}) collective-permute-start(bf16[1024,512]{1,0:T(8,128)(2,1)S(1)} %get-tuple-element.60), channel_id=1, source_target_pairs={{0,8},{1,9},{2,10},{3,11},{4,12},{5,13},{6,14},{7,15},{8,0},{9,1},... | collective-permute-start | bytes 3145736 | tf_op jit(solution)/shard_map/ppermute | solution.py:786
  110.0 5.5 %collective-permute-start.4 = (bf16[48,512]{1,0:T(8,128)(2,1)S(1)}, bf16[48,512]{1,0:T(8,128)(2,1)S(1)}, u32[]{:S(2)}, u32[]{:S(2)}) collective-permute-start(bf16[48,512]{1,0:T(8,128)(2,1)S(1)} %get-tuple-element.56), channel_id=1, source_target_pairs={{0,8},{8,16},{16,24},{24,32},{32,40},{40,48},{48,56},{56,64},{64,7... | collective-permute-start | bytes 147464 | tf_op jit(solution)/shard_map/ppermute | solution.py:51
  112.4 3.3 %collective-permute-start.5 = (bf16[48,512]{1,0:T(8,128)(2,1)S(1)}, bf16[48,512]{1,0:T(8,128)(2,1)S(1)}, u32[]{:S(2)}, u32[]{:S(2)}) collective-permute-start(bf16[48,512]{1,0:T(8,128)(2,1)S(1)} %get-tuple-element.57), channel_id=1, source_target_pairs={{8,0},{16,8},{24,16},{32,24},{40,32},{48,40},{56,48},{64,56},{72,6... | collective-permute-start | bytes 147464 | tf_op jit(solution)/shard_map/ppermute | solution.py:51
  115.6 9.2 %copy-start.2 = (bf16[512,512]{1,0:T(8,128)(2,1)S(1)}, bf16[512,512]{1,0:T(8,128)(2,1)}, u32[]{:S(2)}) copy-start(bf16[512,512]{1,0:T(8,128)(2,1)} %copy-done.1) | copy-start | bytes 1572868
  115.8 36.2 %all-to-all-start.2 = ((bf16[64,32,512]{2,1,0:T(8,128)(2,1)}), bf16[64,32,512]{2,1,0:T(8,128)(2,1)}, u32[]{:S(2)}, u32[]{:S(2)}) async-start(bf16[64,32,512]{2,1,0:T(8,128)(2,1)} %pad_maximum_fusion), calls=%async_computation.2 | async-start | bytes 4194304 | tf_op jit(solution)/shard_map/all_to_all | solution.py:45
  141.0 5.9 %collective-permute-start.8 = (bf16[1024,640]{1,0:T(8,128)(2,1)S(1)}, bf16[1024,640]{1,0:T(8,128)(2,1)S(1)}, u32[]{:S(2)}, u32[]{:S(2)}) collective-permute-start(bf16[1024,640]{1,0:T(8,128)(2,1)S(1)} %get-tuple-element.73), channel_id=1, source_target_pairs={{0,8},{1,9},{2,10},{3,11},{4,12},{5,13},{6,14},{7,15},{8,0},{9,1},... | collective-permute-start | bytes 3932168 | tf_op jit(solution)/shard_map/ppermute | solution.py:786
  151.9 28.9 %all-to-all-start.3 = ((bf16[64,16,640]{2,1,0:T(8,128)(2,1)}), bf16[64,16,640]{2,1,0:T(8,128)(2,1)S(1)}, u32[]{:S(2)}, u32[]{:S(2)}) async-start(bf16[64,16,640]{2,1,0:T(8,128)(2,1)} %bitcast.24), calls=%async_computation.3 | async-start | bytes 2621440 | tf_op jit(solution)/shard_map/all_to_all | solution.py:45

commit v6 on v5

--- a/solution.py
+++ b/solution.py
@@ -58,21 +58,21 @@
     above, below, _ = lax.optimization_barrier((above, below, ahead))
     flat = lambda v: v.reshape(-1, chans)
 
-    def column(at, other):
-        parts = [above[:, at], x[:, at], below[:, at]]
-        return jnp.concatenate([flat(p) for p in parts] + [beside[:, other]], 0)
-
-    left = shift(column(slice(cols - width, cols), cols - 1), "col", 1)
-    right = shift(column(slice(0, width), 0), "col", -1)
+    def column(at):
+        parts = [above[:, at], x[:, at], below[:, at], beside[:, at]]
+        return jnp.concatenate([flat(p) for p in parts], 0)
+
+    left = shift(column(slice(cols - width, cols)), "col", 1)
+    right = shift(column(slice(0, width)), "col", -1)
     n = (rows + 2 * width) * width
 
-    def sides(right, left, width):
+    def sides(right, left):
         right, left = [v.reshape(-1, width, chans) for v in (right, left)]
         gap = jnp.zeros((right.shape[0], 8 - 2 * width, chans), x.dtype)
         return flat(jnp.concatenate([right, gap, left], 1))
 
-    strips = [flat(above), flat(below), sides(right[:n], left[:n], width)]
-    return jnp.concatenate(strips, 0), sides(right[n:], left[n:], 1)
+    strips = [flat(above), flat(below), sides(right[:n], left[:n])]
+    return jnp.concatenate(strips, 0), sides(right[n:], left[n:])
 
 
 def place(wide, centre, strips, width, rows, cols):
@@ -557,6 +557,13 @@
         other_out[at, :] = full[pl.ds(other, half), :].astype(BF)
 
 
+def pack(rows, width):
+    blocks = rows.reshape(8, 2, 8, -1)
+    low, high = [blocks[:, i].reshape(64, -1) for i in range(2)]
+    more = low[:, width:] + pltpu.roll(high[:, width:], 64, 1)
+    return jnp.concatenate([low[:, :width], high[:, :width], more], 1)
+
+
 def backward_kernel(
     core_ref, x_ref, gr_ref, above_ref, below_ref, side_ref, act_ref, slope_c_ref, slope_e_ref,
     wd_ref, wp_ref,
@@ -603,7 +610,10 @@
             taps_t[k : k + 1, lanes] = jnp.sum(sums[k], 0, keepdims=True)
     full[:, 0:width] = dot_tn(gpre[...], normed[...])
     full[:, width:] = taps_t[...].T
-    split_by_core(core_ref[0], full, mine_out, other_out)
+    own = pl.multiple_of(core_ref[0] * (CHUNK // 2), CHUNK // 2)
+    other = pl.multiple_of(CHUNK // 2 - own, CHUNK // 2)
+    mine_out[...] = pack(full[pl.ds(own, CHUNK // 2), :], width)
+    other_out[...] = pack(full[pl.ds(other, CHUNK // 2), :], width).astype(BF)
 
 
 def backward_block(core, x, gr, near, act, slope_c, slope_e, w_depthwise, w_project):
@@ -627,8 +637,8 @@
             ],
             out_specs=[
                 pl.BlockSpec((tokens, CHUNK), lambda j, c: (0, j)),
-                pl.BlockSpec((CHUNK // 2, width + 128), lambda j, c: (j, 0)),
-                pl.BlockSpec((CHUNK // 2, width + 128), lambda j, c: (j, 0)),
+                pl.BlockSpec((CHUNK // 4, 2 * width + 128), lambda j, c: (j, 0)),
+                pl.BlockSpec((CHUNK // 4, 2 * width + 128), lambda j, c: (j, 0)),
             ],
             scratch_shapes=[
                 pltpu.VMEM((rows + 2, WIDE, width), F32),
@@ -642,8 +652,8 @@
         ),
         out_shape=[
             pltpu.HBM((tokens, hid), BF),
-            jax.ShapeDtypeStruct((hid // 2, width + 128), F32),
-            jax.ShapeDtypeStruct((hid // 2, width + 128), BF),
+            jax.ShapeDtypeStruct((hid // 4, 2 * width + 128), F32),
+            jax.ShapeDtypeStruct((hid // 4, 2 * width + 128), BF),
         ],
         compiler_params=pltpu.CompilerParams(vmem_limit_bytes=18 * MIB),
         cost_estimate=pl.CostEstimate(
@@ -683,18 +693,20 @@
 def finish_kernel(parts_ref, expand_out, depth_out):
     total = jnp.sum(parts_ref[...].astype(F32), 0)
     own, width = expand_out.shape
-    expand_out[...] = total[:, 0:width]
-    square = jnp.concatenate([total[:, width:], jnp.zeros((128 - own, 128), F32)], 0)
-    depth_out[...] = square.T[0:9, 0:own]
+    expand_out[0 : own // 2, :] = total[:, 0:width]
+    expand_out[own // 2 :, :] = total[:, width : 2 * width]
+    more = total[:, 2 * width :]
+    rows = [more, pltpu.roll(more, 64, 1), jnp.zeros((128 - own, 128), F32)]
+    depth_out[...] = jnp.concatenate(rows, 0).T[0:9, 0:own]
 
 
 def finish(parts):
-    _, own, lanes = parts.shape
+    own, width = 2 * parts.shape[1], (parts.shape[2] - 128) // 2
     return pl.pallas_call(
         finish_kernel,
         name="last_sum",
         out_shape=[
-            pltpu.HBM((own, lanes - 128), F32),
+            pltpu.HBM((own, width), F32),
             pltpu.HBM((9, own), F32),
         ],
         compiler_params=pltpu.CompilerParams(vmem_limit_bytes=10 * MIB),
@@ -784,7 +796,7 @@
 
 def add_pair(mine, other):
     got = lax.ppermute(other, AX, other_core())
-    return (mine + got.astype(F32)).astype(BF).reshape(64, 16, -1)
+    return (mine + got.astype(F32)).astype(BF).reshape(64, mine.shape[0] // 64, -1)
 
 
 def body(block_input, w_expand, w_depthwise, w_project, w_qkv, w_out, grad_out):

time: 184 us -> 182 us (0.989)
  transfers between devices with their start and end apart: 13 -> 13, of which waited for: 6 -> 6; matrix products, arithmetic and copies ran while one was open for 6% -> 6% of each run, Pallas kernels for 32% -> 33%
where the time goes in v6:
time: 182 us; the launch traced here: 180 us
  Pallas kernels  82.9 us (46%)
  starting transfers between devices  53.9 us (30%)
  waiting for transfers between devices  30.4 us (17%)
  other arithmetic  6.92 us (4%)
  local copies, waits for them, and re-layouts  5.1 us (3%)
    all_to_all x4, starting transfers between devices, across_chips(): lax.all_to_all(x, AX, 0, 0, tiled=True, axis_index_groups=device_groups(C...  34.5 us
    all_to_all x4, waiting for transfers between devices, across_chips(): lax.all_to_all(x, AX, 0, 0, tiled=True, axis_index_groups=device_groups(C...  27.7 us
    pallas_call x1, Pallas kernels, backward_block(): pl.pallas_call(backward_kernel, name='mbconv_backward', grid_spec=pltpu.P...  16.9 us
    ppermute x6, starting transfers between devices, shift(): return lax.ppermute(x, axis, pairs)  15.4 us
    pallas_call x3, Pallas kernels, expand_block(): pl.pallas_call(functools.partial(expand_kernel, apply), name=apply.__name...  12.8 us
    pallas_call x1, Pallas kernels, slopes_block(): pl.pallas_call(slopes_kernel, name='gelu_slopes', grid=(hid // SLOPES,),...  12.3 us
    pallas_call x1, Pallas kernels, attention_block(): pl.pallas_call(attention_kernel, name='grid_attention', in_specs=[pl.Bloc...  11.6 us
    pallas_call x1, Pallas kernels, forward_block(): pl.pallas_call(forward_kernel, name='mbconv_forward', grid=(hid // FORWAR...  11 us
  transfers between devices with their start and end apart: 13, of which 6 were waited for; matrix products, arithmetic and copies ran while one was open for 6% of the time, Pallas kernels for 33%

profile of v6, /device:TPU:0, one launch (start us, length us, event | category | flops | bytes accessed | tf_op | source)
XLA Modules:
  0.0 180.1 jit_solution(16574777282183411277)
XLA Ops:
  2.8 3.0 %collective-permute-start = (bf16[2,32,512]{2,1,0:T(8,128)(2,1)S(1)}, bf16[2,32,512]{2,1,0:T(8,128)(2,1)S(1)}, u32[]{:S(2)}, u32[]{:S(2)}) collective-permute-start(bf16[2,32,512]{2,1,0:T(8,128)(2,1)S(1)} %get-tuple-element.84), channel_id=1, source_target_pairs={{0,8},{8,16},{16,24},{24,32},{32,40},{40,48},{48,56},{56,64},{64,7... | collective-permute-start | bytes 196616 | tf_op jit(solution)/shard_map/ppermute | solution.py:51
  6.9 3.4 %gelu_expand.2.refs_0_ = bf16[512,2048]{1,0:T(8,128)(2,1)} custom-call(bf16[512,512]{1,0:T(8,128)(2,1)} %bitcast.44, bf16[512,2048]{1,0:T(8,128)(2,1)} %we_ref.11), custom_call_target="tpu_custom_call" | custom-call | flops 4294967296 | bytes 3145728 | tf_op jit(solution)/shard_map/gelu_expand/pallas_call | solution.py:160
  13.0 6.1 %collective-permute-start.3 = (bf16[72,512]{1,0:T(8,128)(2,1)S(1)}, bf16[72,512]{1,0:T(8,128)(2,1)S(1)}, u32[]{:S(2)}, u32[]{:S(2)}) collective-permute-start(bf16[72,512]{1,0:T(8,128)(2,1)S(1)} %pad_maximum_fusion.3), channel_id=1, source_target_pairs={{0,1},{1,2},{2,3},{3,4},{4,5},{5,6},{6,7},{8,9},{9,10},{10,11},{11... | collective-permute-start | bytes 221192 | tf_op jit(solution)/shard_map/ppermute | solution.py:51
  19.0 3.4 %gelu_expand.3.act_ref.centre_ref = bf16[512,2048]{1,0:T(8,128)(2,1)} custom-call(bf16[512,512]{1,0:T(8,128)(2,1)} %bitcast.45, bf16[512,2048]{1,0:T(8,128)(2,1)} %we_ref.11, bf16[512,2048]{1,0:T(8,128)(2,1)} %gelu_expand.2.refs_0_), custom_call_target="tpu_custom_call", output_to_operand_aliasing={{}: (2, {})} | custom-call | flops 4294967296 | bytes 3145728 | tf_op jit(solution)/shard_map/gelu_expand/pallas_call | solution.py:160
  22.7 11.0 %mbconv_forward.1 = (bf16[512,2048]{1,0:T(8,128)(2,1)}, bf16[512,512]{1,0:T(8,128)(2,1)}, bf16[512,1024]{1,0:T(8,128)(2,1)}) custom-call(bf16[512,512]{1,0:T(8,128)(2,1)} %bitcast.46, bf16[288,512]{1,0:T(8,128)(2,1)S(1)} %pad_maximum_fusion.1.strips_ref, bf16[512,512]{1,0:T(8,128)(2,1)} %bitcast.39, bf16[512,2048]{1,0:T(8,128)(2,1)} %gelu_expand.3.act_ref.centre_ref, ...), custom_call_target="tpu_custom_call" | custom-call | flops 1468006400 | bytes 10485760 | tf_op jit(solution)/shard_map/mbconv_forward/pallas_call | solution.py:254
  33.7 12.5 %all-to-all-start = ((bf16[64,8,1024]{2,1,0:T(8,128)(2,1)}), bf16[64,8,1024]{2,1,0:T(8,128)(2,1)S(1)}, u32[]{:S(2)}, u32[]{:S(2)}) async-start(bf16[64,8,1024]{2,1,0:T(8,128)(2,1)} %bitcast.42), calls=%async_computation | async-start | bytes 2097152 | tf_op jit(solution)/shard_map/all_to_all | solution.py:45
  46.2 12.3 %gelu_slopes.1 = (bf16[720,2048]{1,0:T(8,128)(2,1)}, bf16[720,2048]{1,0:T(8,128)(2,1)}, bf16[128,512]{1,0:T(8,128)(2,1)}) custom-call(bf16[288,512]{1,0:T(8,128)(2,1)S(1)} %pad_maximum_fusion.1.strips_ref, bf16[512,2048]{1,0:T(8,128)(2,1)} %gelu_expand.3.act_ref.centre_ref, bf16[512,2048]{1,0:T(8,128)(2,1)} %we_ref.11, bf16[9,2048]{1,0:T(8,128)(2,1)} %wd_ref.5, ...), custom_call_target="tpu_custom_call" | custom-call | flops 20000000000 | bytes 12582912 | tf_op jit(solution)/shard_map/gelu_slopes/pallas_call | solution.py:347
  58.5 5.8 %all-to-all-done = bf16[64,8,1024]{2,1,0:T(8,128)(2,1)S(1)} async-done(((bf16[64,8,1024]{2,1,0:T(8,128)(2,1)}), bf16[64,8,1024]{2,1,0:T(8,128)(2,1)S(1)}, u32[]{:S(2)}, u32[]{:S(2)}) %all-to-all-start) | async-done | bytes 1048608 | tf_op jit(solution)/shard_map/all_to_all | solution.py:45
  64.3 11.6 %grid_attention.1 = (bf16[512,1152]{1,0:T(8,128)(2,1)}, bf16[512,1536]{1,0:T(8,128)(2,1)}, bf16[512,512]{1,0:T(8,128)(2,1)}) custom-call(s32[1]{0:T(128)} %bitcast.col_ref, bf16[512,1024]{1,0:T(8,128)(2,1)S(1)} %bitcast.34, bf16[512,1536]{1,0:T(8,128)(2,1)} %wq_hbm.1, bf16[512,512]{1,0:T(8,128)(2,1)} %wo_hbm.1), custom_call_target="tpu_custom_call" | custom-call | flops 2147483648 | bytes 7340032 | tf_op jit(solution)/shard_map/grid_attention/pallas_call | solution.py:473
  75.9 5.7 %all-to-all-start.1 = ((bf16[64,8,1152]{2,1,0:T(8,128)(2,1)}), bf16[64,8,1152]{2,1,0:T(8,128)(2,1)S(1)}, u32[]{:S(2)}, u32[]{:S(2)}) async-start(bf16[64,8,1152]{2,1,0:T(8,128)(2,1)} %bitcast.41), calls=%async_computation.1 | async-start | bytes 2359296 | tf_op jit(solution)/shard_map/all_to_all | solution.py:45
  81.6 4.8 %attention_grads.1 = (f32[1024,512]{1,0:T(8,128)S(1)}, bf16[1024,512]{1,0:T(8,128)(2,1)}) custom-call(s32[1]{0:T(128)} %bitcast.16.core_ref, bf16[512,1024]{1,0:T(8,128)(2,1)} %bitcast.35, bf16[512,1536]{1,0:T(8,128)(2,1)} %get-tuple-element.61.gqkv_ref, bf16[512,512]{1,0:T(8,128)(2,1)} %get-tuple-element.62.att_ref), custom_call_target="tpu_custom_call" | custom-call | flops 1073741824 | bytes 8388608 | tf_op jit(solution)/shard_map/attention_grads/pallas_call | solution.py:774
  87.2 5.9 %gelu_slope_expand.1.slope_e_ref = bf16[512,2048]{1,0:T(8,128)(2,1)} custom-call(bf16[512,512]{1,0:T(8,128)(2,1)} %bitcast.47, bf16[512,2048]{1,0:T(8,128)(2,1)} %we_ref.11), custom_call_target="tpu_custom_call" | custom-call | flops 4294967296 | bytes 3145728 | tf_op jit(solution)/shard_map/gelu_slope_expand/pallas_call | solution.py:160
  93.2 8.7 %all-to-all-done.1 = bf16[64,8,1152]{2,1,0:T(8,128)(2,1)S(1)} async-done(((bf16[64,8,1152]{2,1,0:T(8,128)(2,1)}), bf16[64,8,1152]{2,1,0:T(8,128)(2,1)S(1)}, u32[]{:S(2)}, u32[]{:S(2)}) %all-to-all-start.1) | async-done | bytes 1179680 | tf_op jit(solution)/shard_map/all_to_all | solution.py:45
  101.9 2.2 %residual.1 = (bf16[512,512]{1,0:T(8,128)(2,1)}, bf16[512,512]{1,0:T(8,128)(2,1)S(1)}, bf16[128,512]{1,0:T(8,128)(2,1)S(1)}, bf16[48,512]{1,0:T(8,128)(2,1)S(1)}, bf16[48,512]{1,0:T(8,128)(2,1)S(1)}) custom-call(bf16[512,1152]{1,0:T(8,128)(2,1)S(1)} %bitcast.33, bf16[512,512]{1,0:T(8,128)(2,1)} %get-tuple-element.52.resid_ref, bf16[512,512]{1,0:T(8,128)(2,1)} %bitcast.40, ...), custom_call_target="tpu_custom_call" | custom-call | tf_op jit(solution)/shard_map/residual/pallas_call | solution.py:538
  104.2 3.9 %grad_project.1 = (f32[1024,512]{1,0:T(8,128)S(1)}, bf16[1024,512]{1,0:T(8,128)(2,1)S(1)}) custom-call(s32[1]{0:T(128)} %bitcast.16.core_ref, bf16[512,2048]{1,0:T(8,128)(2,1)} %get-tuple-element.58.mid_ref, bf16[512,512]{1,0:T(8,128)(2,1)S(1)} %get-tuple-element.55.gr_ref), custom_call_target="tpu_custom_call" | custom-call | flops 1073741824 | bytes 7340032 | tf_op jit(solution)/shard_map/grad_project/pallas_call | solution.py:725
  109.8 2.4 %collective-permute-start.4 = (bf16[48,512]{1,0:T(8,128)(2,1)S(1)}, bf16[48,512]{1,0:T(8,128)(2,1)S(1)}, u32[]{:S(2)}, u32[]{:S(2)}) collective-permute-start(bf16[48,512]{1,0:T(8,128)(2,1)S(1)} %get-tuple-element.56), channel_id=1, source_target_pairs={{0,8},{8,16},{16,24},{24,32},{32,40},{40,48},{48,56},{56,64},{64,7... | collective-permute-start | bytes 147464 | tf_op jit(solution)/shard_map/ppermute | solution.py:51
  115.5 9.0 %all-to-all-start.2 = ((bf16[64,32,512]{2,1,0:T(8,128)(2,1)}), bf16[64,32,512]{2,1,0:T(8,128)(2,1)}, u32[]{:S(2)}, u32[]{:S(2)}) async-start(bf16[64,32,512]{2,1,0:T(8,128)(2,1)} %pad_maximum_fusion), calls=%async_computation.2 | async-start | bytes 4194304 | tf_op jit(solution)/shard_map/all_to_all | solution.py:45
  124.5 16.9 %mbconv_backward.1 = (bf16[512,2048]{1,0:T(8,128)(2,1)}, f32[512,1152]{1,0:T(8,128)S(1)}, bf16[512,1152]{1,0:T(8,128)(2,1)S(1)}) custom-call(s32[1]{0:T(128)} %bitcast.16.core_ref, bf16[512,512]{1,0:T(8,128)(2,1)} %bitcast.48, bf16[512,512]{1,0:T(8,128)(2,1)S(1)} %copy-done.2, bf16[48,512]{1,0:T(8,128)(2,1)S(1)} %collective-permute-done.4.above_ref, ...), custom_call_target="tpu_custom_call" | custom-call | flops 8589934592 | bytes 20971520 | tf_op jit(solution)/shard_map/mbconv_backward/pallas_call | solution.py:624
  141.4 3.1 %collective-permute-start.8 = (bf16[512,1152]{1,0:T(8,128)(2,1)S(1)}, bf16[512,1152]{1,0:T(8,128)(2,1)S(1)}, u32[]{:S(2)}, u32[]{:S(2)}) collective-permute-start(bf16[512,1152]{1,0:T(8,128)(2,1)S(1)} %get-tuple-element.73), channel_id=1, source_target_pairs={{0,8},{1,9},{2,10},{3,11},{4,12},{5,13},{6,14},{7,15},{8,0},{9,1},... | collective-permute-start | bytes 3538952 | tf_op jit(solution)/shard_map/ppermute | solution.py:798
  144.6 2.5 %collective-permute-done.8 = bf16[512,1152]{1,0:T(8,128)(2,1)S(1)} collective-permute-done((bf16[512,1152]{1,0:T(8,128)(2,1)S(1)}, bf16[512,1152]{1,0:T(8,128)(2,1)S(1)}, u32[]{:S(2)}, u32[]{:S(2)}) %collective-permute-start.8) | collective-permute-done | bytes 1179680 | tf_op jit(solution)/shard_map/ppermute | solution.py:798
  148.3 3.3 %all-to-all-done.2 = bf16[64,32,512]{2,1,0:T(8,128)(2,1)} async-done(((bf16[64,32,512]{2,1,0:T(8,128)(2,1)}), bf16[64,32,512]{2,1,0:T(8,128)(2,1)}, u32[]{:S(2)}, u32[]{:S(2)}) %all-to-all-start.2) | async-done | bytes 2097184 | tf_op jit(solution)/shard_map/all_to_all | solution.py:45
  151.6 7.3 %all-to-all-start.3 = ((bf16[64,8,1152]{2,1,0:T(8,128)(2,1)}), bf16[64,8,1152]{2,1,0:T(8,128)(2,1)S(1)}, u32[]{:S(2)}, u32[]{:S(2)}) async-start(bf16[64,8,1152]{2,1,0:T(8,128)(2,1)} %fusion), calls=%async_computation.3 | async-start | bytes 2359296 | tf_op jit(solution)/shard_map/all_to_all | solution.py:45
  159.0 6.6 %grad_input.1 = bf16[512,512]{1,0:T(8,128)(2,1)} custom-call(bf16[512,2048]{1,0:T(8,128)(2,1)} %get-tuple-element.71.gpre_ref, bf16[512,2048]{1,0:T(8,128)(2,1)} %we_ref.11, bf16[512,512]{1,0:T(8,128)(2,1)} %bitcast.49, bf16[512,512]{1,0:T(8,128)(2,1)} %copy-done.1), custom_call_target="tpu_custom_call" | custom-call | flops 2147483648 | bytes 6291456 | tf_op jit(solution)/shard_map/grad_input/pallas_call | solution.py:674
  169.4 9.9 %all-to-all-done.3.parts_ref = bf16[64,8,1152]{2,1,0:T(8,128)(2,1)S(1)} async-done(((bf16[64,8,1152]{2,1,0:T(8,128)(2,1)}), bf16[64,8,1152]{2,1,0:T(8,128)(2,1)S(1)}, u32[]{:S(2)}, u32[]{:S(2)}) %all-to-all-start.3) | async-done | bytes 1179680 | tf_op jit(solution)/shard_map/all_to_all | solution.py:45
  (59 shorter events, 17.9 us)
Async XLA Ops:
  1.5 10.0 %collective-permute-start.1 = (bf16[2,32,512]{2,1,0:T(8,128)(2,1)S(1)}, bf16[2,32,512]{2,1,0:T(8,128)(2,1)S(1)}, u32[]{:S(2)}, u32[]{:S(2)}) collective-permute-start(bf16[2,32,512]{2,1,0:T(8,128)(2,1)S(1)} %get-tuple-element.83), channel_id=1, source_target_pairs={{8,0},{16,8},{24,16},{32,24},{40,32},{48,40},{56,48},{64,56},{72,6... | collective-permute-start | bytes 196616 | tf_op jit(solution)/shard_map/ppermute | solution.py:51
  2.8 8.7 %collective-permute-start = (bf16[2,32,512]{2,1,0:T(8,128)(2,1)S(1)}, bf16[2,32,512]{2,1,0:T(8,128)(2,1)S(1)}, u32[]{:S(2)}, u32[]{:S(2)}) collective-permute-start(bf16[2,32,512]{2,1,0:T(8,128)(2,1)S(1)} %get-tuple-element.84), channel_id=1, source_target_pairs={{0,8},{8,16},{16,24},{24,32},{32,40},{40,48},{48,56},{56,64},{64,7... | collective-permute-start | bytes 196616 | tf_op jit(solution)/shard_map/ppermute | solution.py:51
  11.5 11.0 %copy-start.3 = (bf16[8]{0:T(256)(128)(2,1)}, bf16[8]{0:T(256)(128)(2,1)S(1)}, u32[]{:S(2)}) copy-start(bf16[8]{0:T(256)(128)(2,1)S(1)} %pad.9.clone) | copy-start | bytes 52
  11.7 10.8 %collective-permute-start.2 = (bf16[72,512]{1,0:T(8,128)(2,1)S(1)}, bf16[72,512]{1,0:T(8,128)(2,1)S(1)}, u32[]{:S(2)}, u32[]{:S(2)}) collective-permute-start(bf16[72,512]{1,0:T(8,128)(2,1)S(1)} %pad_maximum_fusion.2), channel_id=1, source_target_pairs={{1,0},{2,1},{3,2},{4,3},{5,4},{6,5},{7,6},{9,8},{10,9},{11,10},{12... | collective-permute-start | bytes 221192 | tf_op jit(solution)/shard_map/ppermute | solution.py:51
  13.0 9.5 %collective-permute-start.3 = (bf16[72,512]{1,0:T(8,128)(2,1)S(1)}, bf16[72,512]{1,0:T(8,128)(2,1)S(1)}, u32[]{:S(2)}, u32[]{:S(2)}) collective-permute-start(bf16[72,512]{1,0:T(8,128)(2,1)S(1)} %pad_maximum_fusion.3), channel_id=1, source_target_pairs={{0,1},{1,2},{2,3},{3,4},{4,5},{5,6},{6,7},{8,9},{9,10},{10,11},{11... | collective-permute-start | bytes 221192 | tf_op jit(solution)/shard_map/ppermute | solution.py:51
  33.7 30.6 %all-to-all-start = ((bf16[64,8,1024]{2,1,0:T(8,128)(2,1)}), bf16[64,8,1024]{2,1,0:T(8,128)(2,1)S(1)}, u32[]{:S(2)}, u32[]{:S(2)}) async-start(bf16[64,8,1024]{2,1,0:T(8,128)(2,1)} %bitcast.42), calls=%async_computation | async-start | bytes 2097152 | tf_op jit(solution)/shard_map/all_to_all | solution.py:45
  64.3 11.6 %copy-start = (bf16[64,8,1024]{2,1,0:T(8,128)(2,1)}, bf16[64,8,1024]{2,1,0:T(8,128)(2,1)S(1)}, u32[]{:S(2)}) copy-start(bf16[64,8,1024]{2,1,0:T(8,128)(2,1)S(1)} %all-to-all-done) | copy-start | bytes 3145732
  75.9 26.0 %all-to-all-start.1 = ((bf16[64,8,1152]{2,1,0:T(8,128)(2,1)}), bf16[64,8,1152]{2,1,0:T(8,128)(2,1)S(1)}, u32[]{:S(2)}, u32[]{:S(2)}) async-start(bf16[64,8,1152]{2,1,0:T(8,128)(2,1)} %bitcast.41), calls=%async_computation.1 | async-start | bytes 2359296 | tf_op jit(solution)/shard_map/all_to_all | solution.py:45
  86.4 6.8 %copy-start.4 = (bf16[8]{0:T(256)(128)(2,1)S(1)}, bf16[8]{0:T(256)(128)(2,1)}, u32[]{:S(2)}) copy-start(bf16[8]{0:T(256)(128)(2,1)} %copy-done.3) | copy-start | bytes 52
  86.4 21.8 %collective-permute-start.7 = (bf16[1024,512]{1,0:T(8,128)(2,1)}, bf16[1024,512]{1,0:T(8,128)(2,1)}, u32[]{:S(2)}, u32[]{:S(2)}) collective-permute-start(bf16[1024,512]{1,0:T(8,128)(2,1)} %get-tuple-element.64), channel_id=1, source_target_pairs={{0,8},{1,9},{2,10},{3,11},{4,12},{5,13},{6,14},{7,15},{8,0},{9,1},... | collective-permute-start | bytes 3145736 | tf_op jit(solution)/shard_map/ppermute | solution.py:798
  104.1 4.0 %copy-start.1 = (bf16[512,512]{1,0:T(8,128)(2,1)}, bf16[512,512]{1,0:T(8,128)(2,1)S(1)}, u32[]{:S(2)}) copy-start(bf16[512,512]{1,0:T(8,128)(2,1)S(1)} %get-tuple-element.55.gr_ref) | copy-start | bytes 1572868
  108.1 5.4 %collective-permute-start.6 = (bf16[1024,512]{1,0:T(8,128)(2,1)S(1)}, bf16[1024,512]{1,0:T(8,128)(2,1)S(1)}, u32[]{:S(2)}, u32[]{:S(2)}) collective-permute-start(bf16[1024,512]{1,0:T(8,128)(2,1)S(1)} %get-tuple-element.60), channel_id=1, source_target_pairs={{0,8},{1,9},{2,10},{3,11},{4,12},{5,13},{6,14},{7,15},{8,0},{9,1},... | collective-permute-start | bytes 3145736 | tf_op jit(solution)/shard_map/ppermute | solution.py:798
  109.8 5.6 %collective-permute-start.4 = (bf16[48,512]{1,0:T(8,128)(2,1)S(1)}, bf16[48,512]{1,0:T(8,128)(2,1)S(1)}, u32[]{:S(2)}, u32[]{:S(2)}) collective-permute-start(bf16[48,512]{1,0:T(8,128)(2,1)S(1)} %get-tuple-element.56), channel_id=1, source_target_pairs={{0,8},{8,16},{16,24},{24,32},{32,40},{40,48},{48,56},{56,64},{64,7... | collective-permute-start | bytes 147464 | tf_op jit(solution)/shard_map/ppermute | solution.py:51
  112.2 3.3 %collective-permute-start.5 = (bf16[48,512]{1,0:T(8,128)(2,1)S(1)}, bf16[48,512]{1,0:T(8,128)(2,1)S(1)}, u32[]{:S(2)}, u32[]{:S(2)}) collective-permute-start(bf16[48,512]{1,0:T(8,128)(2,1)S(1)} %get-tuple-element.57), channel_id=1, source_target_pairs={{8,0},{16,8},{24,16},{32,24},{40,32},{48,40},{56,48},{64,56},{72,6... | collective-permute-start | bytes 147464 | tf_op jit(solution)/shard_map/ppermute | solution.py:51
  115.3 9.2 %copy-start.2 = (bf16[512,512]{1,0:T(8,128)(2,1)S(1)}, bf16[512,512]{1,0:T(8,128)(2,1)}, u32[]{:S(2)}) copy-start(bf16[512,512]{1,0:T(8,128)(2,1)} %copy-done.1) | copy-start | bytes 1572868
  115.5 36.1 %all-to-all-start.2 = ((bf16[64,32,512]{2,1,0:T(8,128)(2,1)}), bf16[64,32,512]{2,1,0:T(8,128)(2,1)}, u32[]{:S(2)}, u32[]{:S(2)}) async-start(bf16[64,32,512]{2,1,0:T(8,128)(2,1)} %pad_maximum_fusion), calls=%async_computation.2 | async-start | bytes 4194304 | tf_op jit(solution)/shard_map/all_to_all | solution.py:45
  141.4 5.6 %collective-permute-start.8 = (bf16[512,1152]{1,0:T(8,128)(2,1)S(1)}, bf16[512,1152]{1,0:T(8,128)(2,1)S(1)}, u32[]{:S(2)}, u32[]{:S(2)}) collective-permute-start(bf16[512,1152]{1,0:T(8,128)(2,1)S(1)} %get-tuple-element.73), channel_id=1, source_target_pairs={{0,8},{1,9},{2,10},{3,11},{4,12},{5,13},{6,14},{7,15},{8,0},{9,1},... | collective-permute-start | bytes 3538952 | tf_op jit(solution)/shard_map/ppermute | solution.py:798
  151.6 27.6 %all-to-all-start.3 = ((bf16[64,8,1152]{2,1,0:T(8,128)(2,1)}), bf16[64,8,1152]{2,1,0:T(8,128)(2,1)S(1)}, u32[]{:S(2)}, u32[]{:S(2)}) async-start(bf16[64,8,1152]{2,1,0:T(8,128)(2,1)} %fusion), calls=%async_computation.3 | async-start | bytes 2359296 | tf_op jit(solution)/shard_map/all_to_all | solution.py:45

commit v7 on v6

--- a/solution.py
+++ b/solution.py
@@ -503,6 +503,34 @@
 
 
 def residual_kernel(
+    core_ref, home_ref, resid_ref, go_ref, resid_s_ref, go_s_ref, mid_hbm,
+    out_ref, gr_ref, side_out, first_out, last_out, mine_out, other_out,
+    packed, side, mid, full, sems,
+):
+    steps, _, lanes = mid.shape
+    loads = [
+        pltpu.make_async_copy(mid_hbm.at[:, pl.ds(lanes * i, lanes)], mid.at[i], sems.at[i])
+        for i in range(steps)
+    ]
+    for load in loads:
+        load.start()
+    residual_step(
+        home_ref, resid_ref, go_ref, resid_s_ref, go_s_ref,
+        out_ref, gr_ref, side_out, first_out, last_out, packed, side,
+    )
+    half = 128
+    for i in range(steps):
+        loads[i].wait()
+        full[...] = dot_tn(mid[i], gr_ref[...])
+        for j in range(lanes // (2 * half)):
+            at = i * lanes // 2 + j * half
+            own = pl.multiple_of((2 * j + core_ref[0]) * half, half)
+            other = pl.multiple_of((2 * j + 1 - core_ref[0]) * half, half)
+            mine_out[at : at + half, :] = full[pl.ds(own, half), :]
+            other_out[at : at + half, :] = full[pl.ds(other, half), :].astype(BF)
+
+
+def residual_step(
     home_ref, resid_ref, go_ref, resid_s_ref, go_s_ref, out_ref, gr_ref, side_out, first_out, last_out,
     packed, side,
 ):
@@ -531,30 +559,37 @@
     last_out[...] = jnp.concatenate([own[tokens - cols :], gr_s[8 * rows - 8 :], none], 0).astype(BF)
 
 
-def residual_block(home, resid, go, resid_s, go_s):
+def residual_block(core, home, resid, go, resid_s, go_s, mid):
     tokens, width = resid.shape
+    hid = mid.shape[1]
+    lanes = 512
     beside = resid_s.shape[0]
     shapes = [(tokens, width), (tokens, width), (beside, width), (48, width), (48, width)]
+    vmem = pl.BlockSpec(memory_space=pltpu.VMEM)
     return pl.pallas_call(
         residual_kernel,
-        name="residual",
-        out_shape=[jax.ShapeDtypeStruct(shape, BF) for shape in shapes],
+        name="residual_project",
+        in_specs=[
+            pl.BlockSpec(memory_space=pltpu.SMEM), *[vmem] * 5, pl.BlockSpec(memory_space=pl.ANY)
+        ],
+        out_specs=[vmem] * 7,
+        out_shape=[
+            *[jax.ShapeDtypeStruct(shape, BF) for shape in shapes],
+            jax.ShapeDtypeStruct((hid // 2, width), F32),
+            jax.ShapeDtypeStruct((hid // 2, width), BF),
+        ],
         scratch_shapes=[
             pltpu.VMEM((tokens, 128), F32),
             pltpu.VMEM((width // 128, beside, 128), F32),
-        ],
-        compiler_params=pltpu.CompilerParams(vmem_limit_bytes=12 * MIB),
-    )(home, *in_hbm(resid, go, resid_s), go_s)
-
-
-def split_by_core(core, full, mine_out, other_out):
-    half = 128
-    for j in range(full.shape[0] // (2 * half)):
-        at = slice(j * half, (j + 1) * half)
-        own = pl.multiple_of((2 * j + core) * half, half)
-        other = pl.multiple_of((2 * j + 1 - core) * half, half)
-        mine_out[at, :] = full[pl.ds(own, half), :]
-        other_out[at, :] = full[pl.ds(other, half), :].astype(BF)
+            pltpu.VMEM((hid // lanes, tokens, lanes), BF),
+            pltpu.VMEM((lanes, width), F32),
+            pltpu.SemaphoreType.DMA((hid // lanes,)),
+        ],
+        compiler_params=pltpu.CompilerParams(vmem_limit_bytes=20 * MIB),
+        cost_estimate=pl.CostEstimate(
+            flops=2 * 512 * 512 * 2048, bytes_accessed=7 * 2**20, transcendentals=0
+        ),
+    )(core, home, *in_hbm(resid, go, resid_s), go_s, *in_hbm(mid))
 
 
 def pack(rows, width):
@@ -564,17 +599,19 @@
     return jnp.concatenate([low[:, :width], high[:, :width], more], 1)
 
 
+BACK = 512
+
+
 def backward_kernel(
     core_ref, x_ref, gr_ref, above_ref, below_ref, side_ref, act_ref, slope_c_ref, slope_e_ref,
     wd_ref, wp_ref,
     gpre, mine_out, other_out,
-    wide, grad_wide, normed, gmid, act, full, taps_t,
+    wide, grad_wide, normed, gmid, full, taps_t,
 ):
-    step = pl.program_id(0)
     rows, cols = 16, 32
     width = x_ref.shape[1]
 
-    @pl.when(step == 0)
+    @pl.when(pl.program_id(0) == 0)
     def _():
         wide[0] = above_ref[0:WIDE, :].astype(F32)
         wide[rows + 1] = below_ref[0:WIDE, :].astype(F32)
@@ -584,36 +621,43 @@
         normed[...] = normalize(x_ref[...].astype(F32))[0].astype(BF)
         taps_t[...] = jnp.zeros(taps_t.shape, F32)
 
-    gm = dot_nt(grad_wide[...], wp_ref[...]) * slope_c_ref[...].astype(F32)
-    gmid[...] = gm.reshape(gmid.shape)
-    act[...] = act_ref[...].astype(F32).reshape(act.shape)
-    inside = lax.broadcasted_iota(jnp.int32, (WIDE, 128), 0) < cols
-    for lo in range(0, CHUNK, 128):
+    def seen(whole):
+        return roll(whole, 1)[0:cols], whole[0:cols], roll(whole, -1)[0:cols]
+
+    for lo in range(0, BACK, 128):
         lanes = slice(lo, lo + 128)
+        if lo % 256 == 0:
+            both = slice(lo, lo + 256)
+            gm = dot_nt(grad_wide[...], wp_ref[both, :]) * slope_c_ref[:, both].astype(F32)
+            gmid[:, :, both] = gm.reshape(rows + 2, WIDE, 256)
         taps = [wd_ref[k : k + 1, lanes].astype(F32) for k in range(9)]
+        lines = [seen(gmid[0, :, lanes]), seen(gmid[1, :, lanes])]
+        for r in range(rows):
+            lines = lines[-2:] + [seen(gmid[r + 2, :, lanes])]
+            grad_act = sum(lines[2 - k // 3][2 - k % 3] * taps[k] for k in range(9))
+            at = slice(r * cols, (r + 1) * cols)
+            gpre[at, lanes] = (grad_act * slope_e_ref[at, lanes].astype(F32)).astype(BF)
         sums = [None] * 9
-        grads = [gmid[0, :, lanes], gmid[1, :, lanes]]
-        acts = [act[0, :, lanes], act[1, :, lanes]]
-        for r in range(rows):
-            grads = grads[-2:] + [gmid[r + 2, :, lanes]]
-            acts = acts[-2:] + [act[r + 2, :, lanes]]
-            parts = [sum(grads[2 - i] * taps[3 * i + j] for i in range(3)) for j in range(3)]
-            grad_act = parts[1] + roll(parts[0], -1) + roll(parts[2], 1)
-            at = slice(r * cols, (r + 1) * cols)
-            gpre[at, lanes] = (grad_act[0:cols] * slope_e_ref[at, lanes].astype(F32)).astype(BF)
-            own = jnp.where(inside, grads[1], 0.0)
-            moved = [roll(own, -1), own, roll(own, 1)]
-            for k in range(9):
-                prod = jnp.sum((acts[k // 3] * moved[k % 3]).reshape(WIDE // 8, 8, 128), 0)
-                sums[k] = prod if r == 0 else sums[k] + prod
+        lines = []
+        for r in range(-2, rows):
+            if r % 2 == 0:
+                pair = act_ref[(r + 2) * WIDE : (r + 4) * WIDE, lanes].astype(F32)
+            lines = lines[-2:] + [seen(pair[r % 2 * WIDE : (r % 2 + 1) * WIDE])]
+            if r >= 0:
+                own = gmid[r + 1, 0:cols, lanes]
+                for k in range(9):
+                    prod = jnp.sum((lines[k // 3][k % 3] * own).reshape(cols // 8, 8, 128), 0)
+                    sums[k] = prod if r == 0 else sums[k] + prod
         for k in range(9):
             taps_t[k : k + 1, lanes] = jnp.sum(sums[k], 0, keepdims=True)
-    full[:, 0:width] = dot_tn(gpre[...], normed[...])
-    full[:, width:] = taps_t[...].T
-    own = pl.multiple_of(core_ref[0] * (CHUNK // 2), CHUNK // 2)
-    other = pl.multiple_of(CHUNK // 2 - own, CHUNK // 2)
-    mine_out[...] = pack(full[pl.ds(own, CHUNK // 2), :], width)
-    other_out[...] = pack(full[pl.ds(other, CHUNK // 2), :], width).astype(BF)
+        if lo % 256:
+            both = slice(lo - 128, lo + 128)
+            full[both, 0:width] = dot_tn(gpre[:, both], normed[...])
+            full[both, width:] = taps_t[:, both].T
+            for out, core in ((mine_out, core_ref[0]), (other_out, 1 - core_ref[0])):
+                at = pl.multiple_of(core * 128 + (lo - 128), 128)
+                rows_out = pack(full[pl.ds(at, 128), :], width)
+                out[(lo - 128) // 4 : (lo + 128) // 4, :] = rows_out.astype(out.dtype)
 
 
 def backward_block(core, x, gr, near, act, slope_c, slope_e, w_depthwise, w_project):
@@ -626,28 +670,27 @@
         name="mbconv_backward",
         grid_spec=pltpu.PrefetchScalarGridSpec(
             num_scalar_prefetch=1,
-            grid=(hid // CHUNK,),
+            grid=(hid // BACK,),
             in_specs=[
                 whole(x), whole(gr), *[whole(a) for a in near],
-                pl.BlockSpec(((rows + 2) * WIDE, CHUNK), lambda j, c: (0, j)),
-                pl.BlockSpec(((rows + 2) * WIDE, CHUNK), lambda j, c: (0, j)),
-                pl.BlockSpec((tokens, CHUNK), lambda j, c: (0, j)),
-                pl.BlockSpec((9, CHUNK), lambda j, c: (0, j)),
-                pl.BlockSpec((CHUNK, width), lambda j, c: (j, 0)),
+                pl.BlockSpec(((rows + 2) * WIDE, BACK), lambda j, c: (0, j)),
+                pl.BlockSpec(((rows + 2) * WIDE, BACK), lambda j, c: (0, j)),
+                pl.BlockSpec((tokens, BACK), lambda j, c: (0, j)),
+                pl.BlockSpec((9, BACK), lambda j, c: (0, j)),
+                pl.BlockSpec((BACK, width), lambda j, c: (j, 0)),
             ],
             out_specs=[
-                pl.BlockSpec((tokens, CHUNK), lambda j, c: (0, j)),
-                pl.BlockSpec((CHUNK // 4, 2 * width + 128), lambda j, c: (j, 0)),
-                pl.BlockSpec((CHUNK // 4, 2 * width + 128), lambda j, c: (j, 0)),
+                pl.BlockSpec((tokens, BACK), lambda j, c: (0, j)),
+                pl.BlockSpec((BACK // 4, 2 * width + 128), lambda j, c: (j, 0)),
+                pl.BlockSpec((BACK // 4, 2 * width + 128), lambda j, c: (j, 0)),
             ],
             scratch_shapes=[
                 pltpu.VMEM((rows + 2, WIDE, width), F32),
                 pltpu.VMEM(((rows + 2) * WIDE, width), BF),
                 pltpu.VMEM((tokens, width), BF),
-                pltpu.VMEM((rows + 2, WIDE, CHUNK), F32),
-                pltpu.VMEM((rows + 2, WIDE, CHUNK), F32),
-                pltpu.VMEM((CHUNK, width + 128), F32),
-                pltpu.VMEM((128, CHUNK), F32),
+                pltpu.VMEM((rows + 2, WIDE, BACK), F32),
+                pltpu.VMEM((BACK, width + 128), F32),
+                pltpu.VMEM((128, BACK), F32),
             ],
         ),
         out_shape=[
@@ -655,7 +698,7 @@
             jax.ShapeDtypeStruct((hid // 4, 2 * width + 128), F32),
             jax.ShapeDtypeStruct((hid // 4, 2 * width + 128), BF),
         ],
-        compiler_params=pltpu.CompilerParams(vmem_limit_bytes=18 * MIB),
+        compiler_params=pltpu.CompilerParams(vmem_limit_bytes=24 * MIB),
         cost_estimate=pl.CostEstimate(
             flops=16 * 512 * 512 * 2048, bytes_accessed=20 * 2**20, transcendentals=2**20
         ),
@@ -711,39 +754,6 @@
         ],
         compiler_params=pltpu.CompilerParams(vmem_limit_bytes=10 * MIB),
     )(parts)
-
-
-def project_kernel(core_ref, mid_ref, gr_ref, mine_out, other_out, full):
-    full[...] = dot_tn(mid_ref[...], gr_ref[...])
-    split_by_core(core_ref[0], full, mine_out, other_out)
-
-
-def project_grads(core, mid, gr):
-    tokens, hid = mid.shape
-    width = gr.shape[1]
-    lanes = 512
-    return pl.pallas_call(
-        project_kernel,
-        name="grad_project",
-        grid_spec=pltpu.PrefetchScalarGridSpec(
-            num_scalar_prefetch=1,
-            grid=(hid // lanes,),
-            in_specs=[
-                pl.BlockSpec((tokens, lanes), lambda j, c: (0, j)),
-                pl.BlockSpec((tokens, width), lambda j, c: (0, 0)),
-            ],
-            out_specs=[pl.BlockSpec((lanes // 2, width), lambda j, c: (j, 0))] * 2,
-            scratch_shapes=[pltpu.VMEM((lanes, width), F32)],
-        ),
-        out_shape=[
-            jax.ShapeDtypeStruct((hid // 2, width), F32),
-            jax.ShapeDtypeStruct((hid // 2, width), BF),
-        ],
-        compiler_params=pltpu.CompilerParams(vmem_limit_bytes=8 * MIB),
-        cost_estimate=pl.CostEstimate(
-            flops=2 * 512 * 512 * 2048, bytes_accessed=7 * 2**20, transcendentals=0
-        ),
-    )(core, *in_hbm(mid), gr)
 
 
 def attention_grads_kernel(
@@ -817,11 +827,13 @@
     back, gqkv, attended = attention_block(col, arrived, w_qkv, w_out)
     home = across_chips(back.reshape(64, 8, -1)).reshape(tokens, -1)
     slope_e = expand_block(x, w_expand, gelu_slope, 0, 1)
+    attention_pair = add_pair(*attention_grads(core, arrived, gqkv, attended))
     home, slope_e = lax.optimization_barrier((home, slope_e))
-    attention_pair = add_pair(*attention_grads(core, arrived, gqkv, attended))
-    out, gr, side, first_row, last_row = residual_block(home, resid, go, resid_side, go_side)
+    out, gr, side, first_row, last_row, mine, other = residual_block(
+        core, home, resid, go, resid_side, go_side, mid
+    )
     above, below = shift(last_row, "row", 1), shift(first_row, "row", -1)
-    project_pair = add_pair(*project_grads(core, mid, gr))
+    project_pair = add_pair(mine, other)
     first = jnp.concatenate([project_pair, attention_pair], 1)
     above, below, first = lax.optimization_barrier((above, below, first))
     first = across_chips(first)

time: 182 us -> 182 us (level)
  Pallas kernels: 82.9 us -> 79.5 us
  waiting for transfers between devices: 30.4 us -> 33.3 us
    all_to_all x4, waiting for transfers between devices: 27.7 us -> 30.6 us  [across_chips(): lax.all_to_all(x, AX, 0, 0, tiled=True, axis_index_groups=device_groups(C...]
    pallas_call x1, Pallas kernels: 16.9 us -> 14.1 us  [backward_block(): pl.pallas_call(backward_kernel, name='mbconv_backward', grid_spec=pltpu.P...]
    pallas_call x2 -> x1, Pallas kernels: 6.14 us -> 5.48 us  [residual_block(): pl.pallas_call(residual_kernel, name='residual_project', in_specs=[pl.Blo...]
  transfers between devices with their start and end apart: 13 -> 13, of which waited for: 6 -> 6; matrix products, arithmetic and copies ran while one was open for 6% -> 6% of each run, Pallas kernels for 33% -> 31%
where the time goes in v7:
time: 182 us; the launch traced here: 180 us
  Pallas kernels  79.5 us (44%)
  starting transfers between devices  53.7 us (30%)
  waiting for transfers between devices  33.3 us (18%)
  other arithmetic  7.16 us (4%)
  local copies, waits for them, and re-layouts  5.1 us (3%)
    all_to_all x4, starting transfers between devices, across_chips(): lax.all_to_all(x, AX, 0, 0, tiled=True, axis_index_groups=device_groups(C...  34.5 us
    all_to_all x4, waiting for transfers between devices, across_chips(): lax.all_to_all(x, AX, 0, 0, tiled=True, axis_index_groups=device_groups(C...  30.6 us
    ppermute x6, starting transfers between devices, shift(): return lax.ppermute(x, axis, pairs)  15.3 us
    pallas_call x1, Pallas kernels, backward_block(): pl.pallas_call(backward_kernel, name='mbconv_backward', grid_spec=pltpu.P...  14.1 us
    pallas_call x3, Pallas kernels, expand_block(): pl.pallas_call(functools.partial(expand_kernel, apply), name=apply.__name...  12.8 us
    pallas_call x1, Pallas kernels, slopes_block(): pl.pallas_call(slopes_kernel, name='gelu_slopes', grid=(hid // SLOPES,),...  12.3 us
    pallas_call x1, Pallas kernels, attention_block(): pl.pallas_call(attention_kernel, name='grid_attention', in_specs=[pl.Bloc...  11.6 us
    pallas_call x1, Pallas kernels, forward_block(): pl.pallas_call(forward_kernel, name='mbconv_forward', grid=(hid // FORWAR...  11 us
  transfers between devices with their start and end apart: 13, of which 6 were waited for; matrix products, arithmetic and copies ran while one was open for 6% of the time, Pallas kernels for 31%

profile of v7, /device:TPU:0, one launch (start us, length us, event | category | flops | bytes accessed | tf_op | source)
XLA Modules:
  0.0 179.7 jit_solution(17351191736382421483)
XLA Ops:
  2.8 3.0 %collective-permute-start = (bf16[2,32,512]{2,1,0:T(8,128)(2,1)S(1)}, bf16[2,32,512]{2,1,0:T(8,128)(2,1)S(1)}, u32[]{:S(2)}, u32[]{:S(2)}) collective-permute-start(bf16[2,32,512]{2,1,0:T(8,128)(2,1)S(1)} %get-tuple-element.84), channel_id=1, source_target_pairs={{0,8},{8,16},{16,24},{24,32},{32,40},{40,48},{48,56},{56,64},{64,7... | collective-permute-start | bytes 196616 | tf_op jit(solution)/shard_map/ppermute | solution.py:51
  6.9 3.4 %gelu_expand.2.refs_0_ = bf16[512,2048]{1,0:T(8,128)(2,1)} custom-call(bf16[512,512]{1,0:T(8,128)(2,1)} %bitcast.44, bf16[512,2048]{1,0:T(8,128)(2,1)} %we_ref.11), custom_call_target="tpu_custom_call" | custom-call | flops 4294967296 | bytes 3145728 | tf_op jit(solution)/shard_map/gelu_expand/pallas_call | solution.py:160
  13.0 6.1 %collective-permute-start.3 = (bf16[72,512]{1,0:T(8,128)(2,1)S(1)}, bf16[72,512]{1,0:T(8,128)(2,1)S(1)}, u32[]{:S(2)}, u32[]{:S(2)}) collective-permute-start(bf16[72,512]{1,0:T(8,128)(2,1)S(1)} %pad_maximum_fusion.3), channel_id=1, source_target_pairs={{0,1},{1,2},{2,3},{3,4},{4,5},{5,6},{6,7},{8,9},{9,10},{10,11},{11... | collective-permute-start | bytes 221192 | tf_op jit(solution)/shard_map/ppermute | solution.py:51
  19.1 3.4 %gelu_expand.3.act_ref.centre_ref = bf16[512,2048]{1,0:T(8,128)(2,1)} custom-call(bf16[512,512]{1,0:T(8,128)(2,1)} %bitcast.45, bf16[512,2048]{1,0:T(8,128)(2,1)} %we_ref.11, bf16[512,2048]{1,0:T(8,128)(2,1)} %gelu_expand.2.refs_0_), custom_call_target="tpu_custom_call", output_to_operand_aliasing={{}: (2, {})} | custom-call | flops 4294967296 | bytes 3145728 | tf_op jit(solution)/shard_map/gelu_expand/pallas_call | solution.py:160
  22.7 11.0 %mbconv_forward.1 = (bf16[512,2048]{1,0:T(8,128)(2,1)}, bf16[512,512]{1,0:T(8,128)(2,1)}, bf16[512,1024]{1,0:T(8,128)(2,1)}) custom-call(bf16[512,512]{1,0:T(8,128)(2,1)} %bitcast.46, bf16[288,512]{1,0:T(8,128)(2,1)S(1)} %pad_maximum_fusion.1.strips_ref, bf16[512,512]{1,0:T(8,128)(2,1)} %bitcast.39, bf16[512,2048]{1,0:T(8,128)(2,1)} %gelu_expand.3.act_ref.centre_ref, ...), custom_call_target="tpu_custom_call" | custom-call | flops 1468006400 | bytes 10485760 | tf_op jit(solution)/shard_map/mbconv_forward/pallas_call | solution.py:254
  33.7 12.5 %all-to-all-start = ((bf16[64,8,1024]{2,1,0:T(8,128)(2,1)}), bf16[64,8,1024]{2,1,0:T(8,128)(2,1)S(1)}, u32[]{:S(2)}, u32[]{:S(2)}) async-start(bf16[64,8,1024]{2,1,0:T(8,128)(2,1)} %bitcast.42), calls=%async_computation | async-start | bytes 2097152 | tf_op jit(solution)/shard_map/all_to_all | solution.py:45
  46.2 12.3 %gelu_slopes.1 = (bf16[720,2048]{1,0:T(8,128)(2,1)}, bf16[720,2048]{1,0:T(8,128)(2,1)}, bf16[128,512]{1,0:T(8,128)(2,1)}) custom-call(bf16[288,512]{1,0:T(8,128)(2,1)S(1)} %pad_maximum_fusion.1.strips_ref, bf16[512,2048]{1,0:T(8,128)(2,1)} %gelu_expand.3.act_ref.centre_ref, bf16[512,2048]{1,0:T(8,128)(2,1)} %we_ref.11, bf16[9,2048]{1,0:T(8,128)(2,1)} %wd_ref.5, ...), custom_call_target="tpu_custom_call" | custom-call | flops 20000000000 | bytes 12582912 | tf_op jit(solution)/shard_map/gelu_slopes/pallas_call | solution.py:347
  58.5 5.8 %all-to-all-done = bf16[64,8,1024]{2,1,0:T(8,128)(2,1)S(1)} async-done(((bf16[64,8,1024]{2,1,0:T(8,128)(2,1)}), bf16[64,8,1024]{2,1,0:T(8,128)(2,1)S(1)}, u32[]{:S(2)}, u32[]{:S(2)}) %all-to-all-start) | async-done | bytes 1048608 | tf_op jit(solution)/shard_map/all_to_all | solution.py:45
  64.3 11.6 %grid_attention.1 = (bf16[512,1152]{1,0:T(8,128)(2,1)}, bf16[512,1536]{1,0:T(8,128)(2,1)}, bf16[512,512]{1,0:T(8,128)(2,1)}) custom-call(s32[1]{0:T(128)} %bitcast.1.col_ref, bf16[512,1024]{1,0:T(8,128)(2,1)S(1)} %bitcast.34, bf16[512,1536]{1,0:T(8,128)(2,1)} %wq_hbm.1, bf16[512,512]{1,0:T(8,128)(2,1)} %wo_hbm.1), custom_call_target="tpu_custom_call" | custom-call | flops 2147483648 | bytes 7340032 | tf_op jit(solution)/shard_map/grid_attention/pallas_call | solution.py:473
  75.9 5.7 %all-to-all-start.1 = ((bf16[64,8,1152]{2,1,0:T(8,128)(2,1)}), bf16[64,8,1152]{2,1,0:T(8,128)(2,1)S(1)}, u32[]{:S(2)}, u32[]{:S(2)}) async-start(bf16[64,8,1152]{2,1,0:T(8,128)(2,1)} %bitcast.41), calls=%async_computation.1 | async-start | bytes 2359296 | tf_op jit(solution)/shard_map/all_to_all | solution.py:45
  81.6 4.8 %attention_grads.1 = (f32[1024,512]{1,0:T(8,128)S(1)}, bf16[1024,512]{1,0:T(8,128)(2,1)}) custom-call(s32[1]{0:T(128)} %bitcast.core_ref, bf16[512,1024]{1,0:T(8,128)(2,1)} %bitcast.35, bf16[512,1536]{1,0:T(8,128)(2,1)} %get-tuple-element.61.gqkv_ref, bf16[512,512]{1,0:T(8,128)(2,1)} %get-tuple-element.62.att_ref), custom_call_target="tpu_custom_call" | custom-call | flops 1073741824 | bytes 8388608 | tf_op jit(solution)/shard_map/attention_grads/pallas_call | solution.py:784
  87.2 5.9 %gelu_slope_expand.1.slope_e_ref = bf16[512,2048]{1,0:T(8,128)(2,1)} custom-call(bf16[512,512]{1,0:T(8,128)(2,1)} %bitcast.47, bf16[512,2048]{1,0:T(8,128)(2,1)} %we_ref.11), custom_call_target="tpu_custom_call" | custom-call | flops 4294967296 | bytes 3145728 | tf_op jit(solution)/shard_map/gelu_slope_expand/pallas_call | solution.py:160
  93.2 8.7 %all-to-all-done.1 = bf16[64,8,1152]{2,1,0:T(8,128)(2,1)S(1)} async-done(((bf16[64,8,1152]{2,1,0:T(8,128)(2,1)}), bf16[64,8,1152]{2,1,0:T(8,128)(2,1)S(1)}, u32[]{:S(2)}, u32[]{:S(2)}) %all-to-all-start.1) | async-done | bytes 1179680 | tf_op jit(solution)/shard_map/all_to_all | solution.py:45
  101.9 5.5 %residual_project.1 = (bf16[512,512]{1,0:T(8,128)(2,1)}, bf16[512,512]{1,0:T(8,128)(2,1)S(1)}, bf16[128,512]{1,0:T(8,128)(2,1)S(1)}, bf16[48,512]{1,0:T(8,128)(2...) custom-call(s32[1]{0:T(128)} %bitcast.core_ref, ...), custom_call_target="tpu_custom_call" | custom-call | flops 1073741824 | bytes 7340032 | tf_op jit(solution)/shard_map/residual_project/pallas_call | solution.py:569
  109.2 2.3 %collective-permute-start.4 = (bf16[48,512]{1,0:T(8,128)(2,1)S(1)}, bf16[48,512]{1,0:T(8,128)(2,1)S(1)}, u32[]{:S(2)}, u32[]{:S(2)}) collective-permute-start(bf16[48,512]{1,0:T(8,128)(2,1)S(1)} %get-tuple-element.57), channel_id=1, source_target_pairs={{0,8},{8,16},{16,24},{24,32},{32,40},{40,48},{48,56},{56,64},{64,7... | collective-permute-start | bytes 147464 | tf_op jit(solution)/shard_map/ppermute | solution.py:51
  114.9 9.0 %all-to-all-start.2 = ((bf16[64,32,512]{2,1,0:T(8,128)(2,1)}), bf16[64,32,512]{2,1,0:T(8,128)(2,1)}, u32[]{:S(2)}, u32[]{:S(2)}) async-start(bf16[64,32,512]{2,1,0:T(8,128)(2,1)} %pad_maximum_fusion), calls=%async_computation.2 | async-start | bytes 4194304 | tf_op jit(solution)/shard_map/all_to_all | solution.py:45
  124.0 14.1 %mbconv_backward.1 = (bf16[512,2048]{1,0:T(8,128)(2,1)}, f32[512,1152]{1,0:T(8,128)S(1)}, bf16[512,1152]{1,0:T(8,128)(2,1)S(1)}) custom-call(s32[1]{0:T(128)} %bitcast.core_ref, bf16[512,512]{1,0:T(8,128)(2,1)} %bitcast.48, bf16[512,512]{1,0:T(8,128)(2,1)S(1)} %copy-done.2, bf16[48,512]{1,0:T(8,128)(2,1)S(1)} %collective-permute-done.4.above_ref, ...), custom_call_target="tpu_custom_call" | custom-call | flops 8589934592 | bytes 20971520 | tf_op jit(solution)/shard_map/mbconv_backward/pallas_call | solution.py:668
  138.1 3.1 %collective-permute-start.8 = (bf16[512,1152]{1,0:T(8,128)(2,1)S(1)}, bf16[512,1152]{1,0:T(8,128)(2,1)S(1)}, u32[]{:S(2)}, u32[]{:S(2)}) collective-permute-start(bf16[512,1152]{1,0:T(8,128)(2,1)S(1)} %get-tuple-element.73), channel_id=1, source_target_pairs={{0,8},{1,9},{2,10},{3,11},{4,12},{5,13},{6,14},{7,15},{8,0},{9,1},... | collective-permute-start | bytes 3538952 | tf_op jit(solution)/shard_map/ppermute | solution.py:808
  141.2 2.5 %collective-permute-done.8 = bf16[512,1152]{1,0:T(8,128)(2,1)S(1)} collective-permute-done((bf16[512,1152]{1,0:T(8,128)(2,1)S(1)}, bf16[512,1152]{1,0:T(8,128)(2,1)S(1)}, u32[]{:S(2)}, u32[]{:S(2)}) %collective-permute-start.8) | collective-permute-done | bytes 1179680 | tf_op jit(solution)/shard_map/ppermute | solution.py:808
  145.0 6.2 %all-to-all-done.2 = bf16[64,32,512]{2,1,0:T(8,128)(2,1)} async-done(((bf16[64,32,512]{2,1,0:T(8,128)(2,1)}), bf16[64,32,512]{2,1,0:T(8,128)(2,1)}, u32[]{:S(2)}, u32[]{:S(2)}) %all-to-all-start.2) | async-done | bytes 2097184 | tf_op jit(solution)/shard_map/all_to_all | solution.py:45
  151.2 7.2 %all-to-all-start.3 = ((bf16[64,8,1152]{2,1,0:T(8,128)(2,1)}), bf16[64,8,1152]{2,1,0:T(8,128)(2,1)S(1)}, u32[]{:S(2)}, u32[]{:S(2)}) async-start(bf16[64,8,1152]{2,1,0:T(8,128)(2,1)} %fusion), calls=%async_computation.3 | async-start | bytes 2359296 | tf_op jit(solution)/shard_map/all_to_all | solution.py:45
  158.5 6.6 %grad_input.1 = bf16[512,512]{1,0:T(8,128)(2,1)} custom-call(bf16[512,2048]{1,0:T(8,128)(2,1)} %get-tuple-element.71.gpre_ref, bf16[512,2048]{1,0:T(8,128)(2,1)} %we_ref.11, bf16[512,512]{1,0:T(8,128)(2,1)} %bitcast.49, bf16[512,512]{1,0:T(8,128)(2,1)} %copy-done.1), custom_call_target="tpu_custom_call" | custom-call | flops 2147483648 | bytes 6291456 | tf_op jit(solution)/shard_map/grad_input/pallas_call | solution.py:717
  165.1 1.9 %convert_reduce_fusion = f32[32,512]{1,0:T(8,128)S(1)} fusion(bf16[64,32,512]{2,1,0:T(8,128)(2,1)} %all-to-all-done.2), kind=kLoop, calls=%fused_computation | loop fusion | flops 2080768 | bytes 2162688 | tf_op jit(solution)/shard_map/reduce_sum | solution.py:847
  168.9 9.9 %all-to-all-done.3.parts_ref = bf16[64,8,1152]{2,1,0:T(8,128)(2,1)S(1)} async-done(((bf16[64,8,1152]{2,1,0:T(8,128)(2,1)}), bf16[64,8,1152]{2,1,0:T(8,128)(2,1)S(1)}, u32[]{:S(2)}, u32[]{:S(2)}) %all-to-all-start.3) | async-done | bytes 1179680 | tf_op jit(solution)/shard_map/all_to_all | solution.py:45
  (58 shorter events, 16.2 us)
Async XLA Ops:
  1.5 10.0 %collective-permute-start.1 = (bf16[2,32,512]{2,1,0:T(8,128)(2,1)S(1)}, bf16[2,32,512]{2,1,0:T(8,128)(2,1)S(1)}, u32[]{:S(2)}, u32[]{:S(2)}) collective-permute-start(bf16[2,32,512]{2,1,0:T(8,128)(2,1)S(1)} %get-tuple-element.83), channel_id=1, source_target_pairs={{8,0},{16,8},{24,16},{32,24},{40,32},{48,40},{56,48},{64,56},{72,6... | collective-permute-start | bytes 196616 | tf_op jit(solution)/shard_map/ppermute | solution.py:51
  2.8 8.7 %collective-permute-start = (bf16[2,32,512]{2,1,0:T(8,128)(2,1)S(1)}, bf16[2,32,512]{2,1,0:T(8,128)(2,1)S(1)}, u32[]{:S(2)}, u32[]{:S(2)}) collective-permute-start(bf16[2,32,512]{2,1,0:T(8,128)(2,1)S(1)} %get-tuple-element.84), channel_id=1, source_target_pairs={{0,8},{8,16},{16,24},{24,32},{32,40},{40,48},{48,56},{56,64},{64,7... | collective-permute-start | bytes 196616 | tf_op jit(solution)/shard_map/ppermute | solution.py:51
  11.5 11.0 %copy-start.3 = (bf16[8]{0:T(256)(128)(2,1)}, bf16[8]{0:T(256)(128)(2,1)S(1)}, u32[]{:S(2)}) copy-start(bf16[8]{0:T(256)(128)(2,1)S(1)} %pad.9.clone) | copy-start | bytes 52
  11.7 10.8 %collective-permute-start.2 = (bf16[72,512]{1,0:T(8,128)(2,1)S(1)}, bf16[72,512]{1,0:T(8,128)(2,1)S(1)}, u32[]{:S(2)}, u32[]{:S(2)}) collective-permute-start(bf16[72,512]{1,0:T(8,128)(2,1)S(1)} %pad_maximum_fusion.2), channel_id=1, source_target_pairs={{1,0},{2,1},{3,2},{4,3},{5,4},{6,5},{7,6},{9,8},{10,9},{11,10},{12... | collective-permute-start | bytes 221192 | tf_op jit(solution)/shard_map/ppermute | solution.py:51
  13.0 9.5 %collective-permute-start.3 = (bf16[72,512]{1,0:T(8,128)(2,1)S(1)}, bf16[72,512]{1,0:T(8,128)(2,1)S(1)}, u32[]{:S(2)}, u32[]{:S(2)}) collective-permute-start(bf16[72,512]{1,0:T(8,128)(2,1)S(1)} %pad_maximum_fusion.3), channel_id=1, source_target_pairs={{0,1},{1,2},{2,3},{3,4},{4,5},{5,6},{6,7},{8,9},{9,10},{10,11},{11... | collective-permute-start | bytes 221192 | tf_op jit(solution)/shard_map/ppermute | solution.py:51
  33.7 30.6 %all-to-all-start = ((bf16[64,8,1024]{2,1,0:T(8,128)(2,1)}), bf16[64,8,1024]{2,1,0:T(8,128)(2,1)S(1)}, u32[]{:S(2)}, u32[]{:S(2)}) async-start(bf16[64,8,1024]{2,1,0:T(8,128)(2,1)} %bitcast.42), calls=%async_computation | async-start | bytes 2097152 | tf_op jit(solution)/shard_map/all_to_all | solution.py:45
  64.3 11.6 %copy-start = (bf16[64,8,1024]{2,1,0:T(8,128)(2,1)}, bf16[64,8,1024]{2,1,0:T(8,128)(2,1)S(1)}, u32[]{:S(2)}) copy-start(bf16[64,8,1024]{2,1,0:T(8,128)(2,1)S(1)} %all-to-all-done) | copy-start | bytes 3145732
  75.9 26.0 %all-to-all-start.1 = ((bf16[64,8,1152]{2,1,0:T(8,128)(2,1)}), bf16[64,8,1152]{2,1,0:T(8,128)(2,1)S(1)}, u32[]{:S(2)}, u32[]{:S(2)}) async-start(bf16[64,8,1152]{2,1,0:T(8,128)(2,1)} %bitcast.41), calls=%async_computation.1 | async-start | bytes 2359296 | tf_op jit(solution)/shard_map/all_to_all | solution.py:45
  86.4 6.8 %copy-start.4 = (bf16[8]{0:T(256)(128)(2,1)S(1)}, bf16[8]{0:T(256)(128)(2,1)}, u32[]{:S(2)}) copy-start(bf16[8]{0:T(256)(128)(2,1)} %copy-done.3) | copy-start | bytes 52
  86.4 21.1 %collective-permute-start.7 = (bf16[1024,512]{1,0:T(8,128)(2,1)}, bf16[1024,512]{1,0:T(8,128)(2,1)}, u32[]{:S(2)}, u32[]{:S(2)}) collective-permute-start(bf16[1024,512]{1,0:T(8,128)(2,1)} %get-tuple-element.64), channel_id=1, source_target_pairs={{0,8},{1,9},{2,10},{3,11},{4,12},{5,13},{6,14},{7,15},{8,0},{9,1},... | collective-permute-start | bytes 3145736 | tf_op jit(solution)/shard_map/ppermute | solution.py:808
  107.4 1.8 copy-start.1
  107.4 5.4 %collective-permute-start.6 = (bf16[1024,512]{1,0:T(8,128)(2,1)S(1)}, bf16[1024,512]{1,0:T(8,128)(2,1)S(1)}, u32[]{:S(2)}, u32[]{:S(2)}) collective-permute-start(bf16[1024,512]{1,0:T(8,128)(2,1)S(1)} %get-tuple-element.60), channel_id=1, source_target_pairs={{0,8},{1,9},{2,10},{3,11},{4,12},{5,13},{6,14},{7,15},{8,0},{9,1},... | collective-permute-start | bytes 3145736 | tf_op jit(solution)/shard_map/ppermute | solution.py:808
  109.2 5.6 %collective-permute-start.4 = (bf16[48,512]{1,0:T(8,128)(2,1)S(1)}, bf16[48,512]{1,0:T(8,128)(2,1)S(1)}, u32[]{:S(2)}, u32[]{:S(2)}) collective-permute-start(bf16[48,512]{1,0:T(8,128)(2,1)S(1)} %get-tuple-element.57), channel_id=1, source_target_pairs={{0,8},{8,16},{16,24},{24,32},{32,40},{40,48},{48,56},{56,64},{64,7... | collective-permute-start | bytes 147464 | tf_op jit(solution)/shard_map/ppermute | solution.py:51
  111.5 3.4 %collective-permute-start.5 = (bf16[48,512]{1,0:T(8,128)(2,1)S(1)}, bf16[48,512]{1,0:T(8,128)(2,1)S(1)}, u32[]{:S(2)}, u32[]{:S(2)}) collective-permute-start(bf16[48,512]{1,0:T(8,128)(2,1)S(1)} %get-tuple-element.58), channel_id=1, source_target_pairs={{8,0},{16,8},{24,16},{32,24},{40,32},{48,40},{56,48},{64,56},{72,6... | collective-permute-start | bytes 147464 | tf_op jit(solution)/shard_map/ppermute | solution.py:51
  114.8 9.2 %copy-start.2 = (bf16[512,512]{1,0:T(8,128)(2,1)S(1)}, bf16[512,512]{1,0:T(8,128)(2,1)}, u32[]{:S(2)}) copy-start(bf16[512,512]{1,0:T(8,128)(2,1)} %copy-done.1) | copy-start | bytes 1572868
  114.9 36.3 %all-to-all-start.2 = ((bf16[64,32,512]{2,1,0:T(8,128)(2,1)}), bf16[64,32,512]{2,1,0:T(8,128)(2,1)}, u32[]{:S(2)}, u32[]{:S(2)}) async-start(bf16[64,32,512]{2,1,0:T(8,128)(2,1)} %pad_maximum_fusion), calls=%async_computation.2 | async-start | bytes 4194304 | tf_op jit(solution)/shard_map/all_to_all | solution.py:45
  138.1 5.5 %collective-permute-start.8 = (bf16[512,1152]{1,0:T(8,128)(2,1)S(1)}, bf16[512,1152]{1,0:T(8,128)(2,1)S(1)}, u32[]{:S(2)}, u32[]{:S(2)}) collective-permute-start(bf16[512,1152]{1,0:T(8,128)(2,1)S(1)} %get-tuple-element.73), channel_id=1, source_target_pairs={{0,8},{1,9},{2,10},{3,11},{4,12},{5,13},{6,14},{7,15},{8,0},{9,1},... | collective-permute-start | bytes 3538952 | tf_op jit(solution)/shard_map/ppermute | solution.py:808
  151.2 27.5 %all-to-all-start.3 = ((bf16[64,8,1152]{2,1,0:T(8,128)(2,1)}), bf16[64,8,1152]{2,1,0:T(8,128)(2,1)S(1)}, u32[]{:S(2)}, u32[]{:S(2)}) async-start(bf16[64,8,1152]{2,1,0:T(8,128)(2,1)} %fusion), calls=%async_computation.3 | async-start | bytes 2359296 | tf_op jit(solution)/shard_map/all_to_all | solution.py:45

commit v8 on v7

--- a/solution.py
+++ b/solution.py
@@ -438,7 +438,7 @@
             gq[2 * quads + i, at, :] = dot(pb[i], do[i])
         return 0
 
-    lax.fori_loop(0, groups, one_group, 0)
+    lax.fori_loop(0, groups, one_group, 0, unroll=True)
     attended[...] = jnp.concatenate([att[i] for i in range(quads)], 1).astype(BF)
     store_att = pltpu.make_async_copy(attended, att_hbm, sems.at[2])
     store_att.start()

time: 182 us -> 180 us (0.989)
  Pallas kernels: 79.5 us -> 77.4 us
    pallas_call x1, Pallas kernels: 11.6 us -> 9.47 us  [attention_block(): pl.pallas_call(attention_kernel, name='grid_attention', in_specs=[pl.Bloc...]
  transfers between devices with their start and end apart: 13 -> 13, of which waited for: 6 -> 6; matrix products, arithmetic and copies ran while one was open for 6% -> 6% of each run, Pallas kernels for 31% -> 32%
where the time goes in v8:
time: 180 us; the launch traced here: 178 us
  Pallas kernels  77.4 us (43%)
  starting transfers between devices  53.9 us (30%)
  waiting for transfers between devices  33.1 us (18%)
  other arithmetic  7.16 us (4%)
  local copies, waits for them, and re-layouts  5.1 us (3%)
    all_to_all x4, starting transfers between devices, across_chips(): lax.all_to_all(x, AX, 0, 0, tiled=True, axis_index_groups=device_groups(C...  34.7 us
    all_to_all x4, waiting for transfers between devices, across_chips(): lax.all_to_all(x, AX, 0, 0, tiled=True, axis_index_groups=device_groups(C...  30.4 us
    ppermute x6, starting transfers between devices, shift(): return lax.ppermute(x, axis, pairs)  15.3 us
    pallas_call x1, Pallas kernels, backward_block(): pl.pallas_call(backward_kernel, name='mbconv_backward', grid_spec=pltpu.P...  14.1 us
    pallas_call x3, Pallas kernels, expand_block(): pl.pallas_call(functools.partial(expand_kernel, apply), name=apply.__name...  12.8 us
    pallas_call x1, Pallas kernels, slopes_block(): pl.pallas_call(slopes_kernel, name='gelu_slopes', grid=(hid // SLOPES,),...  12.3 us
    pallas_call x1, Pallas kernels, forward_block(): pl.pallas_call(forward_kernel, name='mbconv_forward', grid=(hid // FORWAR...  11 us
    pallas_call x1, Pallas kernels, attention_block(): pl.pallas_call(attention_kernel, name='grid_attention', in_specs=[pl.Bloc...  9.47 us
  transfers between devices with their start and end apart: 13, of which 6 were waited for; matrix products, arithmetic and copies ran while one was open for 6% of the time, Pallas kernels for 32%

profile of v8, /device:TPU:0, one launch (start us, length us, event | category | flops | bytes accessed | tf_op | source)
XLA Modules:
  0.0 177.6 jit_solution(16068070486117667359)
XLA Ops:
  2.8 3.0 %collective-permute-start = (bf16[2,32,512]{2,1,0:T(8,128)(2,1)S(1)}, bf16[2,32,512]{2,1,0:T(8,128)(2,1)S(1)}, u32[]{:S(2)}, u32[]{:S(2)}) collective-permute-start(bf16[2,32,512]{2,1,0:T(8,128)(2,1)S(1)} %get-tuple-element.84), channel_id=1, source_target_pairs={{0,8},{8,16},{16,24},{24,32},{32,40},{40,48},{48,56},{56,64},{64,7... | collective-permute-start | bytes 196616 | tf_op jit(solution)/shard_map/ppermute | solution.py:51
  6.9 3.4 %gelu_expand.2.refs_0_ = bf16[512,2048]{1,0:T(8,128)(2,1)} custom-call(bf16[512,512]{1,0:T(8,128)(2,1)} %bitcast.44, bf16[512,2048]{1,0:T(8,128)(2,1)} %we_ref.11), custom_call_target="tpu_custom_call" | custom-call | flops 4294967296 | bytes 3145728 | tf_op jit(solution)/shard_map/gelu_expand/pallas_call | solution.py:160
  13.0 6.1 %collective-permute-start.3 = (bf16[72,512]{1,0:T(8,128)(2,1)S(1)}, bf16[72,512]{1,0:T(8,128)(2,1)S(1)}, u32[]{:S(2)}, u32[]{:S(2)}) collective-permute-start(bf16[72,512]{1,0:T(8,128)(2,1)S(1)} %pad_maximum_fusion.3), channel_id=1, source_target_pairs={{0,1},{1,2},{2,3},{3,4},{4,5},{5,6},{6,7},{8,9},{9,10},{10,11},{11... | collective-permute-start | bytes 221192 | tf_op jit(solution)/shard_map/ppermute | solution.py:51
  19.1 3.4 %gelu_expand.3.act_ref.centre_ref = bf16[512,2048]{1,0:T(8,128)(2,1)} custom-call(bf16[512,512]{1,0:T(8,128)(2,1)} %bitcast.45, bf16[512,2048]{1,0:T(8,128)(2,1)} %we_ref.11, bf16[512,2048]{1,0:T(8,128)(2,1)} %gelu_expand.2.refs_0_), custom_call_target="tpu_custom_call", output_to_operand_aliasing={{}: (2, {})} | custom-call | flops 4294967296 | bytes 3145728 | tf_op jit(solution)/shard_map/gelu_expand/pallas_call | solution.py:160
  22.7 11.0 %mbconv_forward.1 = (bf16[512,2048]{1,0:T(8,128)(2,1)}, bf16[512,512]{1,0:T(8,128)(2,1)}, bf16[512,1024]{1,0:T(8,128)(2,1)}) custom-call(bf16[512,512]{1,0:T(8,128)(2,1)} %bitcast.46, bf16[288,512]{1,0:T(8,128)(2,1)S(1)} %pad_maximum_fusion.1.strips_ref, bf16[512,512]{1,0:T(8,128)(2,1)} %bitcast.39, bf16[512,2048]{1,0:T(8,128)(2,1)} %gelu_expand.3.act_ref.centre_ref, ...), custom_call_target="tpu_custom_call" | custom-call | flops 1468006400 | bytes 10485760 | tf_op jit(solution)/shard_map/mbconv_forward/pallas_call | solution.py:254
  33.7 12.7 %all-to-all-start = ((bf16[64,8,1024]{2,1,0:T(8,128)(2,1)}), bf16[64,8,1024]{2,1,0:T(8,128)(2,1)S(1)}, u32[]{:S(2)}, u32[]{:S(2)}) async-start(bf16[64,8,1024]{2,1,0:T(8,128)(2,1)} %bitcast.42), calls=%async_computation | async-start | bytes 2097152 | tf_op jit(solution)/shard_map/all_to_all | solution.py:45
  46.4 12.3 %gelu_slopes.1 = (bf16[720,2048]{1,0:T(8,128)(2,1)}, bf16[720,2048]{1,0:T(8,128)(2,1)}, bf16[128,512]{1,0:T(8,128)(2,1)}) custom-call(bf16[288,512]{1,0:T(8,128)(2,1)S(1)} %pad_maximum_fusion.1.strips_ref, bf16[512,2048]{1,0:T(8,128)(2,1)} %gelu_expand.3.act_ref.centre_ref, bf16[512,2048]{1,0:T(8,128)(2,1)} %we_ref.11, bf16[9,2048]{1,0:T(8,128)(2,1)} %wd_ref.5, ...), custom_call_target="tpu_custom_call" | custom-call | flops 20000000000 | bytes 12582912 | tf_op jit(solution)/shard_map/gelu_slopes/pallas_call | solution.py:347
  58.7 5.6 %all-to-all-done = bf16[64,8,1024]{2,1,0:T(8,128)(2,1)S(1)} async-done(((bf16[64,8,1024]{2,1,0:T(8,128)(2,1)}), bf16[64,8,1024]{2,1,0:T(8,128)(2,1)S(1)}, u32[]{:S(2)}, u32[]{:S(2)}) %all-to-all-start) | async-done | bytes 1048608 | tf_op jit(solution)/shard_map/all_to_all | solution.py:45
  64.3 9.5 %grid_attention.1 = (bf16[512,1152]{1,0:T(8,128)(2,1)}, bf16[512,1536]{1,0:T(8,128)(2,1)}, bf16[512,512]{1,0:T(8,128)(2,1)}) custom-call(s32[1]{0:T(128)} %bitcast.1.col_ref, bf16[512,1024]{1,0:T(8,128)(2,1)S(1)} %bitcast.34, bf16[512,1536]{1,0:T(8,128)(2,1)} %wq_hbm.1, bf16[512,512]{1,0:T(8,128)(2,1)} %wo_hbm.1), custom_call_target="tpu_custom_call" | custom-call | flops 2147483648 | bytes 7340032 | tf_op jit(solution)/shard_map/grid_attention/pallas_call | solution.py:473
  73.8 5.7 %all-to-all-start.1 = ((bf16[64,8,1152]{2,1,0:T(8,128)(2,1)}), bf16[64,8,1152]{2,1,0:T(8,128)(2,1)S(1)}, u32[]{:S(2)}, u32[]{:S(2)}) async-start(bf16[64,8,1152]{2,1,0:T(8,128)(2,1)} %bitcast.41), calls=%async_computation.1 | async-start | bytes 2359296 | tf_op jit(solution)/shard_map/all_to_all | solution.py:45
  79.5 4.8 %attention_grads.1 = (f32[1024,512]{1,0:T(8,128)S(1)}, bf16[1024,512]{1,0:T(8,128)(2,1)}) custom-call(s32[1]{0:T(128)} %bitcast.core_ref, bf16[512,1024]{1,0:T(8,128)(2,1)} %bitcast.35, bf16[512,1536]{1,0:T(8,128)(2,1)} %get-tuple-element.61.gqkv_ref, bf16[512,512]{1,0:T(8,128)(2,1)} %get-tuple-element.62.att_ref), custom_call_target="tpu_custom_call" | custom-call | flops 1073741824 | bytes 8388608 | tf_op jit(solution)/shard_map/attention_grads/pallas_call | solution.py:784
  85.1 5.9 %gelu_slope_expand.1.slope_e_ref = bf16[512,2048]{1,0:T(8,128)(2,1)} custom-call(bf16[512,512]{1,0:T(8,128)(2,1)} %bitcast.47, bf16[512,2048]{1,0:T(8,128)(2,1)} %we_ref.11), custom_call_target="tpu_custom_call" | custom-call | flops 4294967296 | bytes 3145728 | tf_op jit(solution)/shard_map/gelu_slope_expand/pallas_call | solution.py:160
  91.1 8.7 %all-to-all-done.1 = bf16[64,8,1152]{2,1,0:T(8,128)(2,1)S(1)} async-done(((bf16[64,8,1152]{2,1,0:T(8,128)(2,1)}), bf16[64,8,1152]{2,1,0:T(8,128)(2,1)S(1)}, u32[]{:S(2)}, u32[]{:S(2)}) %all-to-all-start.1) | async-done | bytes 1179680 | tf_op jit(solution)/shard_map/all_to_all | solution.py:45
  99.8 5.5 %residual_project.1 = (bf16[512,512]{1,0:T(8,128)(2,1)}, bf16[512,512]{1,0:T(8,128)(2,1)S(1)}, bf16[128,512]{1,0:T(8,128)(2,1)S(1)}, bf16[48,512]{1,0:T(8,128)(2...) custom-call(s32[1]{0:T(128)} %bitcast.core_ref, ...), custom_call_target="tpu_custom_call" | custom-call | flops 1073741824 | bytes 7340032 | tf_op jit(solution)/shard_map/residual_project/pallas_call | solution.py:569
  107.1 2.3 %collective-permute-start.4 = (bf16[48,512]{1,0:T(8,128)(2,1)S(1)}, bf16[48,512]{1,0:T(8,128)(2,1)S(1)}, u32[]{:S(2)}, u32[]{:S(2)}) collective-permute-start(bf16[48,512]{1,0:T(8,128)(2,1)S(1)} %get-tuple-element.57), channel_id=1, source_target_pairs={{0,8},{8,16},{16,24},{24,32},{32,40},{40,48},{48,56},{56,64},{64,7... | collective-permute-start | bytes 147464 | tf_op jit(solution)/shard_map/ppermute | solution.py:51
  112.8 9.0 %all-to-all-start.2 = ((bf16[64,32,512]{2,1,0:T(8,128)(2,1)}), bf16[64,32,512]{2,1,0:T(8,128)(2,1)}, u32[]{:S(2)}, u32[]{:S(2)}) async-start(bf16[64,32,512]{2,1,0:T(8,128)(2,1)} %pad_maximum_fusion), calls=%async_computation.2 | async-start | bytes 4194304 | tf_op jit(solution)/shard_map/all_to_all | solution.py:45
  121.9 14.1 %mbconv_backward.1 = (bf16[512,2048]{1,0:T(8,128)(2,1)}, f32[512,1152]{1,0:T(8,128)S(1)}, bf16[512,1152]{1,0:T(8,128)(2,1)S(1)}) custom-call(s32[1]{0:T(128)} %bitcast.core_ref, bf16[512,512]{1,0:T(8,128)(2,1)} %bitcast.48, bf16[512,512]{1,0:T(8,128)(2,1)S(1)} %copy-done.2, bf16[48,512]{1,0:T(8,128)(2,1)S(1)} %collective-permute-done.4.above_ref, ...), custom_call_target="tpu_custom_call" | custom-call | flops 8589934592 | bytes 20971520 | tf_op jit(solution)/shard_map/mbconv_backward/pallas_call | solution.py:668
  136.0 3.1 %collective-permute-start.8 = (bf16[512,1152]{1,0:T(8,128)(2,1)S(1)}, bf16[512,1152]{1,0:T(8,128)(2,1)S(1)}, u32[]{:S(2)}, u32[]{:S(2)}) collective-permute-start(bf16[512,1152]{1,0:T(8,128)(2,1)S(1)} %get-tuple-element.73), channel_id=1, source_target_pairs={{0,8},{1,9},{2,10},{3,11},{4,12},{5,13},{6,14},{7,15},{8,0},{9,1},... | collective-permute-start | bytes 3538952 | tf_op jit(solution)/shard_map/ppermute | solution.py:808
  139.1 2.5 %collective-permute-done.8 = bf16[512,1152]{1,0:T(8,128)(2,1)S(1)} collective-permute-done((bf16[512,1152]{1,0:T(8,128)(2,1)S(1)}, bf16[512,1152]{1,0:T(8,128)(2,1)S(1)}, u32[]{:S(2)}, u32[]{:S(2)}) %collective-permute-start.8) | collective-permute-done | bytes 1179680 | tf_op jit(solution)/shard_map/ppermute | solution.py:808
  142.9 6.2 %all-to-all-done.2 = bf16[64,32,512]{2,1,0:T(8,128)(2,1)} async-done(((bf16[64,32,512]{2,1,0:T(8,128)(2,1)}), bf16[64,32,512]{2,1,0:T(8,128)(2,1)}, u32[]{:S(2)}, u32[]{:S(2)}) %all-to-all-start.2) | async-done | bytes 2097184 | tf_op jit(solution)/shard_map/all_to_all | solution.py:45
  149.1 7.2 %all-to-all-start.3 = ((bf16[64,8,1152]{2,1,0:T(8,128)(2,1)}), bf16[64,8,1152]{2,1,0:T(8,128)(2,1)S(1)}, u32[]{:S(2)}, u32[]{:S(2)}) async-start(bf16[64,8,1152]{2,1,0:T(8,128)(2,1)} %fusion), calls=%async_computation.3 | async-start | bytes 2359296 | tf_op jit(solution)/shard_map/all_to_all | solution.py:45
  156.4 6.6 %grad_input.1 = bf16[512,512]{1,0:T(8,128)(2,1)} custom-call(bf16[512,2048]{1,0:T(8,128)(2,1)} %get-tuple-element.71.gpre_ref, bf16[512,2048]{1,0:T(8,128)(2,1)} %we_ref.11, bf16[512,512]{1,0:T(8,128)(2,1)} %bitcast.49, bf16[512,512]{1,0:T(8,128)(2,1)} %copy-done.1), custom_call_target="tpu_custom_call" | custom-call | flops 2147483648 | bytes 6291456 | tf_op jit(solution)/shard_map/grad_input/pallas_call | solution.py:717
  163.0 1.9 %convert_reduce_fusion = f32[32,512]{1,0:T(8,128)S(1)} fusion(bf16[64,32,512]{2,1,0:T(8,128)(2,1)} %all-to-all-done.2), kind=kLoop, calls=%fused_computation | loop fusion | flops 2080768 | bytes 2162688 | tf_op jit(solution)/shard_map/reduce_sum | solution.py:847
  166.8 9.9 %all-to-all-done.3.parts_ref = bf16[64,8,1152]{2,1,0:T(8,128)(2,1)S(1)} async-done(((bf16[64,8,1152]{2,1,0:T(8,128)(2,1)}), bf16[64,8,1152]{2,1,0:T(8,128)(2,1)S(1)}, u32[]{:S(2)}, u32[]{:S(2)}) %all-to-all-start.3) | async-done | bytes 1179680 | tf_op jit(solution)/shard_map/all_to_all | solution.py:45
  (58 shorter events, 16.2 us)
Async XLA Ops:
  1.5 10.0 %collective-permute-start.1 = (bf16[2,32,512]{2,1,0:T(8,128)(2,1)S(1)}, bf16[2,32,512]{2,1,0:T(8,128)(2,1)S(1)}, u32[]{:S(2)}, u32[]{:S(2)}) collective-permute-start(bf16[2,32,512]{2,1,0:T(8,128)(2,1)S(1)} %get-tuple-element.83), channel_id=1, source_target_pairs={{8,0},{16,8},{24,16},{32,24},{40,32},{48,40},{56,48},{64,56},{72,6... | collective-permute-start | bytes 196616 | tf_op jit(solution)/shard_map/ppermute | solution.py:51
  2.8 8.7 %collective-permute-start = (bf16[2,32,512]{2,1,0:T(8,128)(2,1)S(1)}, bf16[2,32,512]{2,1,0:T(8,128)(2,1)S(1)}, u32[]{:S(2)}, u32[]{:S(2)}) collective-permute-start(bf16[2,32,512]{2,1,0:T(8,128)(2,1)S(1)} %get-tuple-element.84), channel_id=1, source_target_pairs={{0,8},{8,16},{16,24},{24,32},{32,40},{40,48},{48,56},{56,64},{64,7... | collective-permute-start | bytes 196616 | tf_op jit(solution)/shard_map/ppermute | solution.py:51
  11.5 11.0 %copy-start.3 = (bf16[8]{0:T(256)(128)(2,1)}, bf16[8]{0:T(256)(128)(2,1)S(1)}, u32[]{:S(2)}) copy-start(bf16[8]{0:T(256)(128)(2,1)S(1)} %pad.9.clone) | copy-start | bytes 52
  11.7 10.8 %collective-permute-start.2 = (bf16[72,512]{1,0:T(8,128)(2,1)S(1)}, bf16[72,512]{1,0:T(8,128)(2,1)S(1)}, u32[]{:S(2)}, u32[]{:S(2)}) collective-permute-start(bf16[72,512]{1,0:T(8,128)(2,1)S(1)} %pad_maximum_fusion.2), channel_id=1, source_target_pairs={{1,0},{2,1},{3,2},{4,3},{5,4},{6,5},{7,6},{9,8},{10,9},{11,10},{12... | collective-permute-start | bytes 221192 | tf_op jit(solution)/shard_map/ppermute | solution.py:51
  13.0 9.5 %collective-permute-start.3 = (bf16[72,512]{1,0:T(8,128)(2,1)S(1)}, bf16[72,512]{1,0:T(8,128)(2,1)S(1)}, u32[]{:S(2)}, u32[]{:S(2)}) collective-permute-start(bf16[72,512]{1,0:T(8,128)(2,1)S(1)} %pad_maximum_fusion.3), channel_id=1, source_target_pairs={{0,1},{1,2},{2,3},{3,4},{4,5},{5,6},{6,7},{8,9},{9,10},{10,11},{11... | collective-permute-start | bytes 221192 | tf_op jit(solution)/shard_map/ppermute | solution.py:51
  33.7 30.6 %all-to-all-start = ((bf16[64,8,1024]{2,1,0:T(8,128)(2,1)}), bf16[64,8,1024]{2,1,0:T(8,128)(2,1)S(1)}, u32[]{:S(2)}, u32[]{:S(2)}) async-start(bf16[64,8,1024]{2,1,0:T(8,128)(2,1)} %bitcast.42), calls=%async_computation | async-start | bytes 2097152 | tf_op jit(solution)/shard_map/all_to_all | solution.py:45
  64.3 9.5 %copy-start = (bf16[64,8,1024]{2,1,0:T(8,128)(2,1)}, bf16[64,8,1024]{2,1,0:T(8,128)(2,1)S(1)}, u32[]{:S(2)}) copy-start(bf16[64,8,1024]{2,1,0:T(8,128)(2,1)S(1)} %all-to-all-done) | copy-start | bytes 3145732
  73.8 26.0 %all-to-all-start.1 = ((bf16[64,8,1152]{2,1,0:T(8,128)(2,1)}), bf16[64,8,1152]{2,1,0:T(8,128)(2,1)S(1)}, u32[]{:S(2)}, u32[]{:S(2)}) async-start(bf16[64,8,1152]{2,1,0:T(8,128)(2,1)} %bitcast.41), calls=%async_computation.1 | async-start | bytes 2359296 | tf_op jit(solution)/shard_map/all_to_all | solution.py:45
  84.3 6.7 %copy-start.4 = (bf16[8]{0:T(256)(128)(2,1)S(1)}, bf16[8]{0:T(256)(128)(2,1)}, u32[]{:S(2)}) copy-start(bf16[8]{0:T(256)(128)(2,1)} %copy-done.3) | copy-start | bytes 52
  84.3 21.2 %collective-permute-start.7 = (bf16[1024,512]{1,0:T(8,128)(2,1)}, bf16[1024,512]{1,0:T(8,128)(2,1)}, u32[]{:S(2)}, u32[]{:S(2)}) collective-permute-start(bf16[1024,512]{1,0:T(8,128)(2,1)} %get-tuple-element.64), channel_id=1, source_target_pairs={{0,8},{1,9},{2,10},{3,11},{4,12},{5,13},{6,14},{7,15},{8,0},{9,1},... | collective-permute-start | bytes 3145736 | tf_op jit(solution)/shard_map/ppermute | solution.py:808
  105.3 1.8 %copy-start.1 = (bf16[512,512]{1,0:T(8,128)(2,1)}, bf16[512,512]{1,0:T(8,128)(2,1)S(1)}, u32[]{:S(2)}) copy-start(bf16[512,512]{1,0:T(8,128)(2,1)S(1)} %get-tuple-element.56.gr_ref) | copy-start | bytes 1572868
  105.3 5.4 %collective-permute-start.6 = (bf16[1024,512]{1,0:T(8,128)(2,1)S(1)}, bf16[1024,512]{1,0:T(8,128)(2,1)S(1)}, u32[]{:S(2)}, u32[]{:S(2)}) collective-permute-start(bf16[1024,512]{1,0:T(8,128)(2,1)S(1)} %get-tuple-element.60), channel_id=1, source_target_pairs={{0,8},{1,9},{2,10},{3,11},{4,12},{5,13},{6,14},{7,15},{8,0},{9,1},... | collective-permute-start | bytes 3145736 | tf_op jit(solution)/shard_map/ppermute | solution.py:808
  107.1 5.6 %collective-permute-start.4 = (bf16[48,512]{1,0:T(8,128)(2,1)S(1)}, bf16[48,512]{1,0:T(8,128)(2,1)S(1)}, u32[]{:S(2)}, u32[]{:S(2)}) collective-permute-start(bf16[48,512]{1,0:T(8,128)(2,1)S(1)} %get-tuple-element.57), channel_id=1, source_target_pairs={{0,8},{8,16},{16,24},{24,32},{32,40},{40,48},{48,56},{56,64},{64,7... | collective-permute-start | bytes 147464 | tf_op jit(solution)/shard_map/ppermute | solution.py:51
  109.4 3.4 %collective-permute-start.5 = (bf16[48,512]{1,0:T(8,128)(2,1)S(1)}, bf16[48,512]{1,0:T(8,128)(2,1)S(1)}, u32[]{:S(2)}, u32[]{:S(2)}) collective-permute-start(bf16[48,512]{1,0:T(8,128)(2,1)S(1)} %get-tuple-element.58), channel_id=1, source_target_pairs={{8,0},{16,8},{24,16},{32,24},{40,32},{48,40},{56,48},{64,56},{72,6... | collective-permute-start | bytes 147464 | tf_op jit(solution)/shard_map/ppermute | solution.py:51
  112.7 9.2 %copy-start.2 = (bf16[512,512]{1,0:T(8,128)(2,1)S(1)}, bf16[512,512]{1,0:T(8,128)(2,1)}, u32[]{:S(2)}) copy-start(bf16[512,512]{1,0:T(8,128)(2,1)} %copy-done.1) | copy-start | bytes 1572868
  112.8 36.3 %all-to-all-start.2 = ((bf16[64,32,512]{2,1,0:T(8,128)(2,1)}), bf16[64,32,512]{2,1,0:T(8,128)(2,1)}, u32[]{:S(2)}, u32[]{:S(2)}) async-start(bf16[64,32,512]{2,1,0:T(8,128)(2,1)} %pad_maximum_fusion), calls=%async_computation.2 | async-start | bytes 4194304 | tf_op jit(solution)/shard_map/all_to_all | solution.py:45
  136.0 5.5 %collective-permute-start.8 = (bf16[512,1152]{1,0:T(8,128)(2,1)S(1)}, bf16[512,1152]{1,0:T(8,128)(2,1)S(1)}, u32[]{:S(2)}, u32[]{:S(2)}) collective-permute-start(bf16[512,1152]{1,0:T(8,128)(2,1)S(1)} %get-tuple-element.73), channel_id=1, source_target_pairs={{0,8},{1,9},{2,10},{3,11},{4,12},{5,13},{6,14},{7,15},{8,0},{9,1},... | collective-permute-start | bytes 3538952 | tf_op jit(solution)/shard_map/ppermute | solution.py:808
  149.1 27.5 %all-to-all-start.3 = ((bf16[64,8,1152]{2,1,0:T(8,128)(2,1)}), bf16[64,8,1152]{2,1,0:T(8,128)(2,1)S(1)}, u32[]{:S(2)}, u32[]{:S(2)}) async-start(bf16[64,8,1152]{2,1,0:T(8,128)(2,1)} %fusion), calls=%async_computation.3 | async-start | bytes 2359296 | tf_op jit(solution)/shard_map/all_to_all | solution.py:45
